TPU v7x, 1024 devices: a whole 4x8x16 slice. The times are simulated.
1024 devices in a mesh: sec: 2 (over x_lo), row: 16 (over y, x_hi), col: 32 (over z, core).
Axes of the slice: x: 4 (x_hi: 2, x_lo: 2; x = x_hi * 2 + x_lo), y: 8, z: 16, core: 2. Of those that a mesh axis runs over, the one named last changes fastest.
Arguments:
- atm_state: bfloat16 [768, 4096, 128], P(('sec', 'row'), 'col'), may hold values from -6 to 6
- vert_inverse: bfloat16 [128, 128], replicated, may hold values from -1 to 2
- pair_block: int32 [32768], P(('sec', 'row', 'col')), may hold values from 0 to 23
- pair_ocean: int32 [32768], P(('sec', 'row', 'col')), may hold values from 0 to 255, as said below
- pair_weight: bfloat16 [32768, 128, 128], P(('sec', 'row', 'col')), may hold values from -0.5 to 0.5
- ocean_state: bfloat16 [8192, 128, 128], P(('sec', 'row', 'col')), may hold values from -6 to 6
- flux_coupling: bfloat16 [128, 128], replicated, may hold values from -0.5 to 0.5
- ocean_mix: bfloat16 [128, 128], replicated, may hold values from -1 to 2
- land_mask: int32 [8192, 128], P(('sec', 'row', 'col')), may hold values 0 or 1
Outputs:
- atm_next: bfloat16 [768, 4096, 128], P(('sec', 'row'), 'col')
- ocean_next: bfloat16 [8192, 128, 128], P(('sec', 'row', 'col'))
- surface_on_atm: float32 [4, 768, 4096], P(None, ('sec', 'row'), 'col')
Inputs may be any that keep to these rules, and one draw needn't show every extreme that they name: `pair_ocean`: ocean block k of a row group belongs to the group's device k // 8 along col. Of the 32 pairs of one device at most 2 name blocks of one device, and in every row group one device receives exactly 2 pairs from every device of the group.
All inputs are finite; a program needn't handle non-finite values. No bound on the sum of `land_mask` on one device may be relied on, other than what follows from the above.
Results may differ from a plain program's by a relative error of at most 0.012.
Values may be sent and summed in bfloat16 or wider, within the bound.
No kernel may reach another device: no remote copies, remote signals or barrier semaphores. Data moves between devices by JAX's collectives and lax.ppermute only.
A program may use at most 32 MiB of HBM per device.

v0:
```python
import jax
import jax.numpy as jnp
from jax import lax
from jax.sharding import PartitionSpec as P

FIELDS = 4
SUB = 3


KAPPA = 0.24


def padded_2(array, sides, width):
    for axis, dim in sides:
        peers, length = (lax.axis_size(axis), array.shape[dim])
        up = [(i, (i + 1) % peers) for i in range(peers - 1)]
        down = [(j, i) for i, j in up]
        last = lax.slice_in_dim(array, length - width, length, axis=dim)
        first = lax.slice_in_dim(array, 0, width, axis=dim)
        before = lax.ppermute(last, axis, up)
        after = lax.ppermute(first, axis, down)
        array = jnp.concatenate([before, array, after], axis=dim)
    return array


def smooth_mix(padded, vert_inverse):
    values = padded.astype(jnp.float32)
    centre = values[1:-1, 1:-1]
    spread = (
        values[2:, 1:-1] + values[:-2, 1:-1] + values[1:-1, 2:] + values[1:-1, :-2] - 4.0 * centre
    )
    smooth = (centre + KAPPA * spread).astype(jnp.bfloat16)
    height, breadth, channels = smooth.shape
    mixed = jnp.dot(
        smooth.reshape(height * breadth, channels), vert_inverse, preferred_element_type=jnp.float32
    )
    return mixed.reshape(height, breadth, channels).astype(jnp.bfloat16)


def on_device(
    atm_state,
    vert_inverse,
    pair_block,
    pair_ocean,
    pair_weight,
    ocean_state,
    flux_coupling,
    ocean_mix,
    land_mask,
):
    height, breadth, channels = atm_state.shape
    current = atm_state
    for repeat in range(SUB):
        padded = padded_2(current, ((("sec", "row"), 0), ("col", 1)), 1)
        current = smooth_mix(padded, vert_inverse)
    blocks_dev = ocean_state.shape[0]
    ocean_adv = jnp.dot(
        ocean_state.reshape(blocks_dev * breadth, channels),
        ocean_mix,
        preferred_element_type=jnp.float32,
    ).astype(jnp.bfloat16)
    col_count = lax.axis_size("col")
    pair_count = pair_block.shape[0]
    capacity = 2 * pair_count // col_count
    owners = pair_ocean // blocks_dev
    positions = jnp.arange(pair_count)
    earlier = (owners[None, :] == owners[:, None]) & (positions[None, :] < positions[:, None])
    slot_index = owners * capacity + jnp.sum(earlier.astype(jnp.int32), axis=1)
    flux_rows = current[pair_block]
    contrib = jnp.einsum(
        "poa,pac->poc", pair_weight, flux_rows, preferred_element_type=jnp.float32
    ).astype(jnp.bfloat16)
    outgoing = (
        jnp.zeros((col_count * capacity, breadth, channels), jnp.bfloat16)
        .at[slot_index]
        .set(contrib)
    )
    outgoing = outgoing.reshape(col_count, capacity, breadth, channels)
    targets = (
        jnp.full((col_count * capacity,), -1, jnp.int32)
        .at[slot_index]
        .set(pair_ocean - owners * blocks_dev)
    )
    targets = targets.reshape(col_count, capacity)
    incoming, sources = (
        lax.all_to_all(outgoing, "col", split_axis=0, concat_axis=0, tiled=True),
        lax.all_to_all(targets, "col", split_axis=0, concat_axis=0, tiled=True),
    )
    local_ids = sources.reshape(col_count * capacity)
    selector = (local_ids[None, :] == jnp.arange(blocks_dev)[:, None]).astype(jnp.bfloat16)
    forcing = jnp.dot(
        selector,
        incoming.reshape(col_count * capacity, breadth * channels),
        preferred_element_type=jnp.float32,
    )
    forcing = forcing.reshape(blocks_dev * breadth, channels).astype(jnp.bfloat16)
    pushed = jnp.dot(forcing, flux_coupling, preferred_element_type=jnp.float32)
    updated = (
        (ocean_adv.astype(jnp.float32) + pushed)
        .astype(jnp.bfloat16)
        .reshape(blocks_dev, breadth, channels)
    )
    wet_cells = (land_mask == 1)[:, :, None]
    ocean_next = jnp.where(wet_cells, updated, ocean_state)
    surface = jnp.transpose(
        jnp.where(wet_cells, ocean_next, jnp.zeros_like(ocean_next))[:, :, :FIELDS], (0, 2, 1)
    )
    filled = (local_ids >= 0)[:, None, None]
    replies = jnp.where(
        filled, surface[jnp.maximum(local_ids, 0)], jnp.zeros((1, FIELDS, breadth), jnp.bfloat16)
    )
    replies = replies.reshape(col_count, capacity, FIELDS, breadth)
    answered = lax.all_to_all(replies, "col", split_axis=0, concat_axis=0, tiled=True)
    per_pair = answered.reshape(col_count * capacity, FIELDS, breadth)[slot_index]
    pair_terms = jnp.einsum(
        "pfo,poa->pfa", per_pair, pair_weight, preferred_element_type=jnp.float32
    )
    onehot_rows = (pair_block[:, None] == jnp.arange(height)[None, :]).astype(jnp.float32)
    surface_on_atm = jnp.einsum(
        "pb,pfa->fba", onehot_rows, pair_terms, precision=lax.Precision.HIGHEST
    )
    return (current, ocean_next, surface_on_atm)


def solution(mesh):
    return jax.shard_map(
        on_device,
        mesh=mesh,
        in_specs=(
            P(("sec", "row"), "col", None),
            P(),
            P(("sec", "row", "col")),
            P(("sec", "row", "col")),
            P(("sec", "row", "col"), None, None),
            P(("sec", "row", "col"), None, None),
            P(),
            P(),
            P(("sec", "row", "col"), None),
        ),
        out_specs=(
            P(("sec", "row"), "col", None),
            P(("sec", "row", "col"), None, None),
            P(None, ("sec", "row"), "col"),
        ),
        check_vma=False,
    )
```

profile of v0, /device:TPU:22, one launch (start us, length us, event | category | flops | bytes accessed | tf_op | source)
XLA Modules:
  0.0 239.2 jit_solution(9019528451694829480)
XLA Ops:
  1.5 4.3 %collective-permute-start = (bf16[1,128,128]{2,1,0:T(8,128)(2,1)S(1)}, bf16[1,128,128]{2,1,0:T(8,128)(2,1)S(1)}, u32[]{:S(2)}, u32[]{:S(2)}) collective-permute-start(bf16[1,128,128]{2,1,0:T(8,128)(2,1)S(1)} %get-tuple-element.18), channel_id=1, source_target_pairs={{0,32},{32,64},{64,96},{96,128},{128,160},{160,192},{192,224},{224... | collective-permute-start | bytes 98312 | tf_op jit(solution)/shard_map/ppermute | solution.py:20
  5.9 3.0 %collective-permute-start.1 = (bf16[1,128,128]{2,1,0:T(8,128)(2,1)S(1)}, bf16[1,128,128]{2,1,0:T(8,128)(2,1)S(1)}, u32[]{:S(2)}, u32[]{:S(2)}) collective-permute-start(bf16[1,128,128]{2,1,0:T(8,128)(2,1)S(1)} %get-tuple-element.17), channel_id=1, source_target_pairs={{32,0},{64,32},{96,64},{128,96},{160,128},{192,160},{224,192},{256... | collective-permute-start | bytes 98312 | tf_op jit(solution)/shard_map/ppermute | solution.py:21
  8.9 1.3 constant_dynamic-update-slice_fusion.1
  10.2 3.9 %collective-permute-done.1 = bf16[1,128,128]{2,1,0:T(8,128)(2,1)S(1)} collective-permute-done((bf16[1,128,128]{2,1,0:T(8,128)(2,1)S(1)}, bf16[1,128,128]{2,1,0:T(8,128)(2,1)S(1)}, u32[]{:S(2)}, u32[]{:S(2)}) %collective-permute-start.1) | collective-permute-done | bytes 32800 | tf_op jit(solution)/shard_map/ppermute | solution.py:21
  14.1 1.3 collective-permute-start.2
  15.4 1.3 collective-permute-start.3
  16.7 4.3 %collective-permute-done.3 = bf16[26,1,128]{2,1,0:T(2,128)(2,1)S(1)} collective-permute-done((bf16[26,1,128]{2,1,0:T(2,128)(2,1)S(1)}, bf16[26,1,128]{2,1,0:T(2,128)(2,1)S(1)}, u32[]{:S(2)}, u32[]{:S(2)}) %collective-permute-start.3) | collective-permute-done | bytes 6688 | tf_op jit(solution)/shard_map/ppermute | solution.py:21
  22.3 3.2 %collective-permute-start.4 = (bf16[1,128,128]{2,1,0:T(8,128)(2,1)S(1)}, bf16[1,128,128]{2,1,0:T(8,128)(2,1)S(1)}, u32[]{:S(2)}, u32[]{:S(2)}) collective-permute-start(bf16[1,128,128]{2,1,0:T(8,128)(2,1)S(1)} %get-tuple-element.15), channel_id=1, source_target_pairs={{0,32},{32,64},{64,96},{96,128},{128,160},{160,192},{192,224},{224... | collective-permute-start | bytes 98312 | tf_op jit(solution)/shard_map/ppermute | solution.py:20
  25.6 4.1 %collective-permute-start.5 = (bf16[1,128,128]{2,1,0:T(8,128)(2,1)S(1)}, bf16[1,128,128]{2,1,0:T(8,128)(2,1)S(1)}, u32[]{:S(2)}, u32[]{:S(2)}) collective-permute-start(bf16[1,128,128]{2,1,0:T(8,128)(2,1)S(1)} %get-tuple-element.16), channel_id=1, source_target_pairs={{32,0},{64,32},{96,64},{128,96},{160,128},{192,160},{224,192},{256... | collective-permute-start | bytes 98312 | tf_op jit(solution)/shard_map/ppermute | solution.py:21
  29.9 5.1 %collective-permute-done.5 = bf16[1,128,128]{2,1,0:T(8,128)(2,1)S(1)} collective-permute-done((bf16[1,128,128]{2,1,0:T(8,128)(2,1)S(1)}, bf16[1,128,128]{2,1,0:T(8,128)(2,1)S(1)}, u32[]{:S(2)}, u32[]{:S(2)}) %collective-permute-start.5) | collective-permute-done | bytes 32800 | tf_op jit(solution)/shard_map/ppermute | solution.py:21
  35.0 3.2 %collective-permute-start.6 = (bf16[26,1,128]{2,1,0:T(2,128)(2,1)S(1)}, bf16[26,1,128]{2,1,0:T(2,128)(2,1)S(1)}, u32[]{:S(2)}, u32[]{:S(2)}) collective-permute-start(bf16[26,1,128]{2,1,0:T(2,128)(2,1)S(1)} %get-tuple-element.9), channel_id=1, source_target_pairs={{0,1},{1,2},{2,3},{3,4},{4,5},{5,6},{6,7},{7,8},{8,9},{9,10},{10,1... | collective-permute-start | bytes 19976 | tf_op jit(solution)/shard_map/ppermute | solution.py:20
  38.3 1.3 collective-permute-start.7
  41.0 22.6 %all-to-all-start = ((s32[32,1,2]{2,1,0:T(1,128)}), s32[32,1,2]{2,1,0:T(1,128)S(1)}, u32[]{:S(2)}, u32[]{:S(2)}) async-start(s32[32,1,2]{2,1,0:T(1,128)} %bitcast.2), calls=%async_computation | async-start | bytes 32768 | tf_op jit(solution)/shard_map/all_to_all | solution.py:87
  63.9 0.9 convolution_convert_fusion.3
  64.9 5.4 %collective-permute-start.8 = (bf16[1,128,128]{2,1,0:T(8,128)(2,1)S(1)}, bf16[1,128,128]{2,1,0:T(8,128)(2,1)S(1)}, u32[]{:S(2)}, u32[]{:S(2)}) collective-permute-start(bf16[1,128,128]{2,1,0:T(8,128)(2,1)S(1)} %get-tuple-element.13), channel_id=1, source_target_pairs={{0,32},{32,64},{64,96},{96,128},{128,160},{160,192},{192,224},{224... | collective-permute-start | bytes 98312 | tf_op jit(solution)/shard_map/ppermute | solution.py:20
  70.3 1.9 collective-permute-start.9
  72.3 6.3 %collective-permute-done.9 = bf16[1,128,128]{2,1,0:T(8,128)(2,1)S(1)} collective-permute-done((bf16[1,128,128]{2,1,0:T(8,128)(2,1)S(1)}, bf16[1,128,128]{2,1,0:T(8,128)(2,1)S(1)}, u32[]{:S(2)}, u32[]{:S(2)}) %collective-permute-start.9) | collective-permute-done | bytes 32800 | tf_op jit(solution)/shard_map/ppermute | solution.py:21
  78.5 1.3 collective-permute-start.10
  79.8 1.3 collective-permute-start.11
  81.2 3.8 %collective-permute-done.11 = bf16[26,1,128]{2,1,0:T(2,128)(2,1)S(1)} collective-permute-done((bf16[26,1,128]{2,1,0:T(2,128)(2,1)S(1)}, bf16[26,1,128]{2,1,0:T(2,128)(2,1)S(1)}, u32[]{:S(2)}, u32[]{:S(2)}) %collective-permute-start.11) | collective-permute-done | bytes 6688 | tf_op jit(solution)/shard_map/ppermute | solution.py:21
  89.4 1.8 broadcast_in_dim.58
  91.2 4.6 %scatter_fusion = bf16[64,128,128]{2,1,0:T(8,128)(2,1)} fusion(bf16[64,128,128]{2,1,0:T(8,128)(2,1)} %broadcast_in_dim.58, s32[32]{0:T(128)S(1)} %compare_select_fusion.1, bf16[32,128,128]{2,1,0:T(8,128)(2,1)S(1)} %copy.29), kind=kCustom, calls=%fused_computation.4 | custom fusion | bytes 3145856 | tf_op jit(solution)/shard_map/scatter | solution.py:76
  95.8 14.4 %all-to-all-start.1 = ((bf16[32,2,128,128]{3,2,1,0:T(8,128)(2,1)}), bf16[32,2,128,128]{3,2,1,0:T(8,128)(2,1)S(1)}, u32[]{:S(2)}, u32[]{:S(2)}) async-start(bf16[32,2,128,128]{3,2,1,0:T(8,128)(2,1)} %bitcast.4), calls=%async_computation.1 | async-start | bytes 4194304 | tf_op jit(solution)/shard_map/all_to_all | solution.py:86
  110.2 1.0 fusion.16
  112.9 96.5 %all-to-all-done.1 = bf16[32,2,128,128]{3,2,1,0:T(8,128)(2,1)S(1)} async-done(((bf16[32,2,128,128]{3,2,1,0:T(8,128)(2,1)}), bf16[32,2,128,128]{3,2,1,0:T(8,128)(2,1)S(1)}, u32[]{:S(2)}, u32[]{:S(2)}) %all-to-all-start.1) | async-done | bytes 2097184 | tf_op jit(solution)/shard_map/all_to_all | solution.py:86
  209.4 1.9 convolution_convert_fusion
  211.3 1.1 convert_element_type.68
  212.4 1.2 fusion.15
  214.8 1.9 gather_fusion.1
  216.7 0.9 copy.32
  218.4 4.5 %all-to-all-start.2 = ((bf16[32,2,4,128]{3,2,1,0:T(4,128)(2,1)}), bf16[32,2,4,128]{3,2,1,0:T(4,128)(2,1)S(1)}, u32[]{:S(2)}, u32[]{:S(2)}) async-start(bf16[32,2,4,128]{3,2,1,0:T(4,128)(2,1)} %broadcast_select_fusion.1), calls=%async_computation.2 | async-start | bytes 131072 | tf_op jit(solution)/shard_map/all_to_all | solution.py:113
  223.0 14.4 %all-to-all-done.2 = bf16[32,2,4,128]{3,2,1,0:T(4,128)(2,1)S(1)} async-done(((bf16[32,2,4,128]{3,2,1,0:T(4,128)(2,1)}), bf16[32,2,4,128]{3,2,1,0:T(4,128)(2,1)S(1)}, u32[]{:S(2)}, u32[]{:S(2)}) %all-to-all-start.2) | async-done | bytes 65568 | tf_op jit(solution)/shard_map/all_to_all | solution.py:113
  (67 shorter events, 13.9 us)
Async XLA Ops:
  0.6 87.2 %copy-start = (bf16[32,128,128]{2,1,0:T(8,128)(2,1)S(1)}, bf16[32,128,128]{2,1,0:T(8,128)(2,1)}, u32[]{:S(2)}) copy-start(bf16[32,128,128]{2,1,0:T(8,128)(2,1)} %param.13) | copy-start | bytes 3145732
  0.6 16.1 %copy-start.9 = (s32[32]{0:T(128)S(1)}, s32[32]{0:T(128)}, u32[]{:S(2)}) copy-start(s32[32]{0:T(128)} %param.12) | copy-start | bytes 388
  1.5 7.4 %collective-permute-start = (bf16[1,128,128]{2,1,0:T(8,128)(2,1)S(1)}, bf16[1,128,128]{2,1,0:T(8,128)(2,1)S(1)}, u32[]{:S(2)}, u32[]{:S(2)}) collective-permute-start(bf16[1,128,128]{2,1,0:T(8,128)(2,1)S(1)} %get-tuple-element.18), channel_id=1, source_target_pairs={{0,32},{32,64},{64,96},{96,128},{128,160},{160,192},{192,224},{224... | collective-permute-start | bytes 98312 | tf_op jit(solution)/shard_map/ppermute | solution.py:20
  5.9 8.2 %collective-permute-start.1 = (bf16[1,128,128]{2,1,0:T(8,128)(2,1)S(1)}, bf16[1,128,128]{2,1,0:T(8,128)(2,1)S(1)}, u32[]{:S(2)}, u32[]{:S(2)}) collective-permute-start(bf16[1,128,128]{2,1,0:T(8,128)(2,1)S(1)} %get-tuple-element.17), channel_id=1, source_target_pairs={{32,0},{64,32},{96,64},{128,96},{160,128},{192,160},{224,192},{256... | collective-permute-start | bytes 98312 | tf_op jit(solution)/shard_map/ppermute | solution.py:21
  8.9 12.5 %copy-start.8 = (bf16[128,128]{1,0:T(8,128)(2,1)S(1)}, bf16[128,128]{1,0:T(8,128)(2,1)}, u32[]{:S(2)}) copy-start(bf16[128,128]{1,0:T(8,128)(2,1)} %param.10) | copy-start | bytes 98308
  14.1 2.6 %collective-permute-start.2 = (bf16[26,1,128]{2,1,0:T(2,128)(2,1)S(1)}, bf16[26,1,128]{2,1,0:T(2,128)(2,1)S(1)}, u32[]{:S(2)}, u32[]{:S(2)}) collective-permute-start(bf16[26,1,128]{2,1,0:T(2,128)(2,1)S(1)} %get-tuple-element.11), channel_id=1, source_target_pairs={{0,1},{1,2},{2,3},{3,4},{4,5},{5,6},{6,7},{7,8},{8,9},{9,10},{10,1... | collective-permute-start | bytes 19976 | tf_op jit(solution)/shard_map/ppermute | solution.py:20
  15.4 5.7 %collective-permute-start.3 = (bf16[26,1,128]{2,1,0:T(2,128)(2,1)S(1)}, bf16[26,1,128]{2,1,0:T(2,128)(2,1)S(1)}, u32[]{:S(2)}, u32[]{:S(2)}) collective-permute-start(bf16[26,1,128]{2,1,0:T(2,128)(2,1)S(1)} %get-tuple-element.12), channel_id=1, source_target_pairs={{1,0},{2,1},{3,2},{4,3},{5,4},{6,5},{7,6},{8,7},{9,8},{10,9},{11,1... | collective-permute-start | bytes 19976 | tf_op jit(solution)/shard_map/ppermute | solution.py:21
  22.3 7.5 %collective-permute-start.4 = (bf16[1,128,128]{2,1,0:T(8,128)(2,1)S(1)}, bf16[1,128,128]{2,1,0:T(8,128)(2,1)S(1)}, u32[]{:S(2)}, u32[]{:S(2)}) collective-permute-start(bf16[1,128,128]{2,1,0:T(8,128)(2,1)S(1)} %get-tuple-element.15), channel_id=1, source_target_pairs={{0,32},{32,64},{64,96},{96,128},{128,160},{160,192},{192,224},{224... | collective-permute-start | bytes 98312 | tf_op jit(solution)/shard_map/ppermute | solution.py:20
  25.6 9.4 %collective-permute-start.5 = (bf16[1,128,128]{2,1,0:T(8,128)(2,1)S(1)}, bf16[1,128,128]{2,1,0:T(8,128)(2,1)S(1)}, u32[]{:S(2)}, u32[]{:S(2)}) collective-permute-start(bf16[1,128,128]{2,1,0:T(8,128)(2,1)S(1)} %get-tuple-element.16), channel_id=1, source_target_pairs={{32,0},{64,32},{96,64},{128,96},{160,128},{192,160},{224,192},{256... | collective-permute-start | bytes 98312 | tf_op jit(solution)/shard_map/ppermute | solution.py:21
  35.0 28.5 %collective-permute-start.6 = (bf16[26,1,128]{2,1,0:T(2,128)(2,1)S(1)}, bf16[26,1,128]{2,1,0:T(2,128)(2,1)S(1)}, u32[]{:S(2)}, u32[]{:S(2)}) collective-permute-start(bf16[26,1,128]{2,1,0:T(2,128)(2,1)S(1)} %get-tuple-element.9), channel_id=1, source_target_pairs={{0,1},{1,2},{2,3},{3,4},{4,5},{5,6},{6,7},{7,8},{8,9},{9,10},{10,1... | collective-permute-start | bytes 19976 | tf_op jit(solution)/shard_map/ppermute | solution.py:20
  38.3 25.3 %collective-permute-start.7 = (bf16[26,1,128]{2,1,0:T(2,128)(2,1)S(1)}, bf16[26,1,128]{2,1,0:T(2,128)(2,1)S(1)}, u32[]{:S(2)}, u32[]{:S(2)}) collective-permute-start(bf16[26,1,128]{2,1,0:T(2,128)(2,1)S(1)} %get-tuple-element.10), channel_id=1, source_target_pairs={{1,0},{2,1},{3,2},{4,3},{5,4},{6,5},{7,6},{8,7},{9,8},{10,9},{11,1... | collective-permute-start | bytes 19976 | tf_op jit(solution)/shard_map/ppermute | solution.py:21
  41.0 54.8 %all-to-all-start = ((s32[32,1,2]{2,1,0:T(1,128)}), s32[32,1,2]{2,1,0:T(1,128)S(1)}, u32[]{:S(2)}, u32[]{:S(2)}) async-start(s32[32,1,2]{2,1,0:T(1,128)} %bitcast.2), calls=%async_computation | async-start | bytes 32768 | tf_op jit(solution)/shard_map/all_to_all | solution.py:87
  63.9 8.3 %copy-start.7 = (s32[32]{0:T(128)S(1)}, s32[32]{0:T(128)}, u32[]{:S(2)}) copy-start(s32[32]{0:T(128)} %param.11) | copy-start | bytes 388
  64.9 7.4 %collective-permute-start.8 = (bf16[1,128,128]{2,1,0:T(8,128)(2,1)S(1)}, bf16[1,128,128]{2,1,0:T(8,128)(2,1)S(1)}, u32[]{:S(2)}, u32[]{:S(2)}) collective-permute-start(bf16[1,128,128]{2,1,0:T(8,128)(2,1)S(1)} %get-tuple-element.13), channel_id=1, source_target_pairs={{0,32},{32,64},{64,96},{96,128},{128,160},{160,192},{192,224},{224... | collective-permute-start | bytes 98312 | tf_op jit(solution)/shard_map/ppermute | solution.py:20
  70.3 8.2 %collective-permute-start.9 = (bf16[1,128,128]{2,1,0:T(8,128)(2,1)S(1)}, bf16[1,128,128]{2,1,0:T(8,128)(2,1)S(1)}, u32[]{:S(2)}, u32[]{:S(2)}) collective-permute-start(bf16[1,128,128]{2,1,0:T(8,128)(2,1)S(1)} %get-tuple-element.14), channel_id=1, source_target_pairs={{32,0},{64,32},{96,64},{128,96},{160,128},{192,160},{224,192},{256... | collective-permute-start | bytes 98312 | tf_op jit(solution)/shard_map/ppermute | solution.py:21
  78.5 2.6 %collective-permute-start.10 = (bf16[26,1,128]{2,1,0:T(2,128)(2,1)S(1)}, bf16[26,1,128]{2,1,0:T(2,128)(2,1)S(1)}, u32[]{:S(2)}, u32[]{:S(2)}) collective-permute-start(bf16[26,1,128]{2,1,0:T(2,128)(2,1)S(1)} %get-tuple-element.7), channel_id=1, source_target_pairs={{0,1},{1,2},{2,3},{3,4},{4,5},{5,6},{6,7},{7,8},{8,9},{9,10},{10,1... | collective-permute-start | bytes 19976 | tf_op jit(solution)/shard_map/ppermute | solution.py:20
  79.8 5.1 %collective-permute-start.11 = (bf16[26,1,128]{2,1,0:T(2,128)(2,1)S(1)}, bf16[26,1,128]{2,1,0:T(2,128)(2,1)S(1)}, u32[]{:S(2)}, u32[]{:S(2)}) collective-permute-start(bf16[26,1,128]{2,1,0:T(2,128)(2,1)S(1)} %get-tuple-element.8), channel_id=1, source_target_pairs={{1,0},{2,1},{3,2},{4,3},{5,4},{6,5},{7,6},{8,7},{9,8},{10,9},{11,1... | collective-permute-start | bytes 19976 | tf_op jit(solution)/shard_map/ppermute | solution.py:21
  86.2 0.9 copy-start.1
  95.8 14.4 %copy-start.6 = (s32[8,128]{1,0:T(8,128)S(1)}, s32[8,128]{1,0:T(8,128)}, u32[]{:S(2)}) copy-start(s32[8,128]{1,0:T(8,128)} %param.17) | copy-start | bytes 12292
  95.8 14.4 %copy-start.2 = (bf16[8,128,128]{2,1,0:T(8,128)(2,1)S(1)}, bf16[8,128,128]{2,1,0:T(8,128)(2,1)}, u32[]{:S(2)}) copy-start(bf16[8,128,128]{2,1,0:T(8,128)(2,1)} %param.14) | copy-start | bytes 786436
  95.8 14.4 %copy-start.4 = (bf16[128,128]{1,0:T(8,128)(2,1)S(1)}, bf16[128,128]{1,0:T(8,128)(2,1)}, u32[]{:S(2)}) copy-start(bf16[128,128]{1,0:T(8,128)(2,1)} %param.16) | copy-start | bytes 98308
  95.8 113.6 %all-to-all-start.1 = ((bf16[32,2,128,128]{3,2,1,0:T(8,128)(2,1)}), bf16[32,2,128,128]{3,2,1,0:T(8,128)(2,1)S(1)}, u32[]{:S(2)}, u32[]{:S(2)}) async-start(bf16[32,2,128,128]{3,2,1,0:T(8,128)(2,1)} %bitcast.4), calls=%async_computation.1 | async-start | bytes 4194304 | tf_op jit(solution)/shard_map/all_to_all | solution.py:86
  110.2 102.2 %copy-start.5 = (bf16[128,128]{1,0:T(8,128)(2,1)S(1)}, bf16[128,128]{1,0:T(8,128)(2,1)}, u32[]{:S(2)}) copy-start(bf16[128,128]{1,0:T(8,128)(2,1)} %param.15) | copy-start | bytes 98308
  213.9 24.5 %copy-start.3 = (bf16[8,128,128]{2,1,0:T(8,128)(2,1)}, bf16[8,128,128]{2,1,0:T(8,128)(2,1)S(1)}, u32[]{:S(2)}) copy-start(bf16[8,128,128]{2,1,0:T(8,128)(2,1)S(1)} %broadcast_select_fusion) | copy-start | bytes 786436
  218.4 19.0 %all-to-all-start.2 = ((bf16[32,2,4,128]{3,2,1,0:T(4,128)(2,1)}), bf16[32,2,4,128]{3,2,1,0:T(4,128)(2,1)S(1)}, u32[]{:S(2)}, u32[]{:S(2)}) async-start(bf16[32,2,4,128]{3,2,1,0:T(4,128)(2,1)} %broadcast_select_fusion.1), calls=%async_computation.2 | async-start | bytes 131072 | tf_op jit(solution)/shard_map/all_to_all | solution.py:113
where the time goes:
time: 240 us; the launch traced here: 239 us
  waiting for transfers between devices  134 us (56%)
  starting transfers between devices  73.2 us (30%)
  local copies, waits for them, and re-layouts  17.8 us (7%)
  matrix products  8.97 us (4%)
  other arithmetic  3.85 us (2%)
    all_to_all x1, waiting for transfers between devices, on_device(): lax.all_to_all(outgoing, 'col', split_axis=0, concat_axis=0, tiled=True)  96.5 us
    ppermute x6, waiting for transfers between devices, padded_2(): after = lax.ppermute(first, axis, down)  23.4 us
    all_to_all x1, starting transfers between devices, on_device(): lax.all_to_all(targets, 'col', split_axis=0, concat_axis=0, tiled=True)  22.6 us
    ppermute x6, starting transfers between devices, padded_2(): before = lax.ppermute(last, axis, up)  18.8 us
    all_to_all x1, waiting for transfers between devices, on_device(): lax.all_to_all(replies, 'col', split_axis=0, concat_axis=0, tiled=True)  14.4 us
    all_to_all x1, starting transfers between devices, on_device(): lax.all_to_all(outgoing, 'col', split_axis=0, concat_axis=0, tiled=True)  14.4 us
    ppermute x6, starting transfers between devices, padded_2(): after = lax.ppermute(first, axis, down)  12.9 us
  transfers between devices with their start and end apart: 15, of which 7 were waited for; matrix products, arithmetic and copies ran while one was open for 7% of the time, Pallas kernels for 0%

commit v1 on v0

v1 whole, which is shorter than its diff:
```python
import jax
import jax.numpy as jnp
from jax import lax
from jax.experimental import pallas as pl
from jax.experimental.pallas import tpu as pltpu
from jax.sharding import PartitionSpec as P

FIELDS = 4
SUB = 3
KAPPA = 0.24
PARTS = 2
BF = jnp.bfloat16
F32 = jnp.float32

VM = pl.BlockSpec(memory_space=pltpu.VMEM)
SM = pl.BlockSpec(memory_space=pltpu.SMEM)


def params(mib):
    return pltpu.CompilerParams(vmem_limit_bytes=mib * 1024 * 1024)


def edges(array, axis, dim, width):
    peers, length = lax.axis_size(axis), array.shape[dim]
    up = [(i, i + 1) for i in range(peers - 1)]
    down = [(j, i) for i, j in up]
    last = lax.slice_in_dim(array, length - width, length, axis=dim)
    first = lax.slice_in_dim(array, 0, width, axis=dim)
    return lax.ppermute(last, axis, up), lax.ppermute(first, axis, down)


def substeps(atm, vert_inverse):
    height, breadth, _ = atm.shape
    wide = SUB
    before, after = edges(atm, ("sec", "row"), 0, wide)
    tall = jnp.concatenate([before, atm, after], axis=0)
    left, right = edges(tall, "col", 1, wide)
    current = jnp.concatenate([left, tall, right], axis=1)
    row_at = lax.axis_index(("sec", "row")) * height
    col_at = lax.axis_index("col") * breadth
    rows_all = lax.axis_size(("sec", "row")) * height
    cols_all = lax.axis_size("col") * breadth
    for step in range(SUB):
        halo = wide - 1 - step
        values = current.astype(F32)
        centre = values[1:-1, 1:-1]
        spread = (
            values[2:, 1:-1] + values[:-2, 1:-1] + values[1:-1, 2:] + values[1:-1, :-2]
            - 4.0 * centre
        )
        smooth = (centre + KAPPA * spread).astype(BF)
        mixed = jnp.einsum(
            "hwc,cd->hwd", smooth, vert_inverse, preferred_element_type=F32
        ).astype(BF)
        if halo:
            rows = row_at - halo + jnp.arange(mixed.shape[0])
            cols = col_at - halo + jnp.arange(mixed.shape[1])
            inside = ((rows >= 0) & (rows < rows_all))[:, None] & (
                (cols >= 0) & (cols < cols_all)
            )[None, :]
            mixed = jnp.where(inside[:, :, None], mixed, jnp.zeros_like(mixed))
        current = mixed
    return current


def added(ref, at, block):
    ref[at] = (ref[at].astype(F32) + block.astype(F32)).astype(BF)


def contrib_kernel(
    blk, idx, tab_far, tab_mate, atm, weight, narrow, extra,
    sums, near_sums, far, near, rest, payload, q,
):
    del tab_far, tab_mate
    total = sums.shape[0]

    @pl.loop(0, total // 8)
    def _(i):
        sums[pl.ds(i * 8, 8)] = jnp.zeros((8,) + sums.shape[1:], BF)

    pairs = weight.shape[0]
    kept = None
    for p in range(pairs):
        block = jnp.dot(
            weight[p], atm[blk[p]], preferred_element_type=F32
        ).astype(BF)
        added(sums, idx[p], block)
        part = lax.dot_general(
            narrow[p % 2].astype(BF), block, (((1,), (1,)), ((), ())),
            preferred_element_type=F32,
        )
        if p % 2 == 0:
            kept = part
        else:
            q[pl.ds((p // 2) * 8, 8)] = kept + part
    payload[pl.ds(0, q.shape[0])] = q[...].astype(BF)
    payload[pl.ds(q.shape[0], extra.shape[0])] = extra[...]
    n_near, n_far, n_first, n_rest = (
        near_sums.shape[0], far.shape[0], near.shape[0], rest.shape[0]
    )
    base = total - n_near - n_far - n_first - n_rest
    for i in range(n_near):
        near_sums[i] = sums[base + i]
    base += n_near
    for i in range(n_far):
        far[i] = sums[base + i]
    base += n_far
    for i in range(n_rest):
        rest[i] = sums[base + i]
    base += n_rest
    for i in range(n_first):
        near[i] = sums[base + i]


def first_kernel(tab_far, tab_mate, near_sums, far, near, *outs_scratch):
    outs, held = outs_scratch[:-1], outs_scratch[-1]
    held[...] = near_sums[...]
    n_far, n_near = far.shape[0], near.shape[0]
    slots = tab_mate.shape[0]
    low = slots - n_far - n_near
    for i in range(n_far):
        added(held, tab_far[i], far[i])
    for i in range(n_near):
        added(held, tab_mate[n_far + low + i], near[i])
    each = outs[0].shape[0]
    for m, out in enumerate(outs):
        out[...] = held[m * each:(m + 1) * each]


def rest_kernel(tab_mate, sums, rest, *outs_scratch, n_far):
    outs, held = outs_scratch[:-1], outs_scratch[-1]
    n = held.shape[0]

    @pl.loop(0, n // 8)
    def _(i):
        held[pl.ds(i * 8, 8)] = sums[pl.ds(i * 8, 8)]

    for i in range(rest.shape[0]):
        added(held, tab_mate[n_far + i], rest[i])
    each = outs[0].shape[0]
    for m, out in enumerate(outs):
        out[...] = held[m * each:(m + 1) * each]


def ocean_kernel(adv, state, wet, coupling, *rest):
    parts = (len(rest) - 1) // 2
    mine, swapped, out = rest[:parts], rest[parts:-1], rest[-1]
    each = mine[0].shape[0]
    for b in range(out.shape[0]):
        m, i = b // each, b % each
        forcing = (mine[m][i].astype(F32) + swapped[m][i].astype(F32)).astype(BF)
        pushed = jnp.dot(forcing, coupling[...], preferred_element_type=F32)
        updated = (adv[b].astype(F32) + pushed).astype(BF).astype(F32)
        keep = wet[b].astype(F32) > 0.5
        out[b] = jnp.where(keep, updated, state[b].astype(F32)).astype(BF)


def reply_kernel(blk, ids, gathered, weight, out, held, acc):
    devices, _, lanes = gathered.shape
    pairs = weight.shape[0]
    own = ids[...]
    row_f = lax.broadcasted_iota(jnp.int32, (lanes, lanes), 0) % FIELDS
    lane = lax.broadcasted_iota(jnp.int32, (lanes, lanes), 1)
    same_f = row_f == lane % FIELDS
    tail = gathered.shape[1] - lanes
    lane_t = lax.broadcasted_iota(jnp.int32, (lanes, tail), 1)
    row_t = lax.broadcasted_iota(jnp.int32, (lanes, tail), 0) % FIELDS
    blocks = lanes // 4 // FIELDS
    is_adv = (lane_t < blocks * FIELDS) & (row_t == lane_t % FIELDS)
    is_mask = (lane_t >= blocks * FIELDS) & (lane_t < blocks * (FIELDS + 1))
    local = jnp.where(lane_t < blocks * FIELDS, lane_t // FIELDS, lane_t - blocks * FIELDS)
    zero = jnp.zeros((lanes, lanes), F32)

    def step(d, carry):
        pushed, adv, wet = carry
        id_row = gathered[d, pl.ds(lanes + 32, 16)].astype(F32)[8:9]
        pick = jnp.where(same_f & (own.astype(F32) == id_row), 1.0, 0.0).astype(BF)
        pushed += jnp.dot(pick, gathered[d, pl.ds(0, lanes)], preferred_element_type=F32)
        match = own == local + d * blocks
        low = gathered[d, pl.ds(lanes, tail)]
        adv += jnp.dot(
            jnp.where(match & is_adv, 1.0, 0.0).astype(BF), low, preferred_element_type=F32
        )
        wet += jnp.dot(
            jnp.where(match & is_mask, 1.0, 0.0).astype(BF), low, preferred_element_type=F32
        )
        return pushed, adv, wet

    pushed, adv, wet = lax.fori_loop(0, devices, step, (zero, zero, zero), unroll=4)
    surface = jnp.where(wet > 0.5, (adv + pushed).astype(BF).astype(F32), 0.0)
    held[...] = surface
    acc[...] = jnp.zeros_like(acc)
    low_rows = lax.broadcasted_iota(jnp.int32, (8, lanes), 0) < FIELDS
    for j in range(pairs // 2):
        rows = held[pl.ds(j * 8, 8)].astype(BF)
        even = jnp.dot(rows, weight[2 * j], preferred_element_type=F32)
        odd = jnp.dot(rows, weight[2 * j + 1], preferred_element_type=F32)
        acc[blk[2 * j]] += jnp.where(low_rows, even, 0.0)
        acc[blk[2 * j + 1]] += jnp.where(low_rows, 0.0, odd)
    for f in range(FIELDS):
        out[f] = acc[:, f, :] + acc[:, f + FIELDS, :]


def on_device(
    atm_state,
    vert_inverse,
    pair_block,
    pair_ocean,
    pair_weight,
    ocean_state,
    flux_coupling,
    ocean_mix,
    land_mask,
):
    height, breadth, channels = atm_state.shape
    blocks = ocean_state.shape[0]
    pairs = pair_block.shape[0]
    devices = lax.axis_size("col")
    cap = 2 * pairs // devices
    chips = devices // 2
    half = chips // 2
    me = lax.axis_index("col")
    chip, core = me // 2, me % 2
    onward = [(i, (i + 2 - 4 * (i % 2)) % devices) for i in range(devices)]
    mate = [(i, i ^ 1) for i in range(devices)]

    owner = pair_ocean // blocks
    local = pair_ocean - owner * blocks
    at = jnp.arange(pairs)
    rank = jnp.sum(
        ((owner[None, :] == owner[:, None]) & (at[None, :] < at[:, None])).astype(jnp.int32),
        axis=1,
    )
    offset = ((owner // 2 - chip) * (1 - 2 * core)) % chips
    other = (owner % 2) ^ core
    wide = 2 * blocks
    n_far = 2 * cap
    n_slots = n_far + 2 * cap * (half - 1)
    dense = half * wide
    back = chips - offset
    target = jnp.where(
        offset < half,
        offset * wide + other * blocks + local,
        jnp.where(
            offset == half,
            dense + other * cap + rank,
            dense + n_far + ((back - 1) * 2 + (1 - other)) * cap + rank,
        ),
    )
    value = jnp.where(
        offset == half,
        other * blocks + local,
        jnp.where(back == half - 1, 0, back * wide) + (1 - other) * blocks + local,
    )
    slot_at = dense + jnp.arange(n_slots)
    table = jnp.sum(
        jnp.where(target[:, None] == slot_at[None, :], value[:, None], 0), axis=0
    ).astype(jnp.int32)
    table_far = lax.ppermute(table, "col", onward)
    table_mate = lax.ppermute(table, "col", mate)

    ocean_adv = jnp.einsum(
        "boc,cd->bod", ocean_state, ocean_mix, preferred_element_type=F32
    ).astype(BF)
    adv_rows = jnp.einsum(
        "cf,boc->bfo", ocean_mix[:, :FIELDS], ocean_state, preferred_element_type=F32
    ).astype(BF)
    id_row = jnp.broadcast_to(pair_ocean[:, None], (pairs, FIELDS)).reshape(1, pairs * FIELDS)
    extra = jnp.concatenate(
        [
            adv_rows.reshape(blocks * FIELDS, breadth),
            (land_mask == 1).astype(BF),
            id_row.astype(BF),
            jnp.zeros((7, breadth), BF),
        ],
        axis=0,
    )
    narrow = jnp.zeros((2, 8, channels), F32)
    narrow = narrow.at[0, :FIELDS].set(flux_coupling[:, :FIELDS].T.astype(F32))
    narrow = narrow.at[1, FIELDS:].set(flux_coupling[:, :FIELDS].T.astype(F32))

    wet = jnp.broadcast_to(
        (land_mask == 1).astype(BF)[:, :, None], (blocks, breadth, channels)
    )
    current = substeps(atm_state, vert_inverse)
    current, ocean_adv, wet = lax.optimization_barrier((current, ocean_adv, wet))

    def blocks_of(n):
        return jax.ShapeDtypeStruct((n, breadth, channels), BF)

    n_rest = n_slots - n_far - 2 * cap
    sums, near_sums, far, near, rest, payload = pl.pallas_call(
        contrib_kernel,
        out_shape=(
            blocks_of(dense + n_slots),
            blocks_of(wide),
            blocks_of(n_far),
            blocks_of(2 * cap),
            blocks_of(n_rest),
            jax.ShapeDtypeStruct((pairs * FIELDS + extra.shape[0], breadth), BF),
        ),
        in_specs=[SM] * 4 + [VM] * 4,
        out_specs=(VM,) * 6,
        scratch_shapes=[pltpu.VMEM((pairs * FIELDS, breadth), F32)],
        compiler_params=params(48),
        cost_estimate=pl.CostEstimate(
            flops=2 * pairs * breadth * breadth * channels,
            bytes_accessed=8 * 1024 * 1024,
            transcendentals=0,
        ),
    )(pair_block, target, table_far, table_mate, current, pair_weight, narrow, extra)

    gathered = lax.all_gather(payload, "col", axis=0)
    far = lax.ppermute(far, "col", onward)
    near = lax.ppermute(near, "col", mate)
    rest = lax.ppermute(rest, "col", mate)

    chains = 2 * PARTS
    each = wide // chains
    held = pl.pallas_call(
        first_kernel,
        out_shape=(blocks_of(each),) * chains,
        in_specs=[SM, SM, VM, VM, VM],
        out_specs=(VM,) * chains,
        scratch_shapes=[pltpu.VMEM((wide, breadth, channels), BF)],
        compiler_params=params(16),
        cost_estimate=pl.CostEstimate(
            flops=wide * breadth * channels, bytes_accessed=2 * 1024 * 1024, transcendentals=0
        ),
    )(table_far, table_mate, near_sums, far, near)
    held = list(held)

    here = pl.pallas_call(
        lambda *refs: rest_kernel(*refs, n_far=n_far),
        out_shape=(blocks_of(each),) * (chains * (half - 1)),
        in_specs=[SM, VM, VM],
        out_specs=(VM,) * (chains * (half - 1)),
        scratch_shapes=[pltpu.VMEM((dense - wide, breadth, channels), BF)],
        compiler_params=params(32),
        cost_estimate=pl.CostEstimate(
            flops=n_rest * breadth * channels, bytes_accessed=4 * 1024 * 1024, transcendentals=0
        ),
    )(table_mate, sums, rest)

    order = list(range(PARTS, chains)) + list(range(PARTS))
    for hop in range(half - 1, 0, -1):
        for m in order:
            came = lax.ppermute(held[m], "col", onward)
            total = came.astype(F32) + here[(hop - 1) * chains + m].astype(F32)
            held[m] = total.astype(BF)

    swapped = [lax.ppermute(held[PARTS + m], "col", mate) for m in range(PARTS)]
    ocean_next = pl.pallas_call(
        ocean_kernel,
        out_shape=blocks_of(blocks),
        in_specs=[VM] * (4 + 2 * PARTS),
        out_specs=VM,
        compiler_params=params(16),
        cost_estimate=pl.CostEstimate(
            flops=2 * blocks * breadth * channels * channels,
            bytes_accessed=2 * 1024 * 1024,
            transcendentals=0,
        ),
    )(ocean_adv, ocean_state, wet, flux_coupling, *held[:PARTS], *swapped)

    ids = jnp.broadcast_to(pair_ocean[:, None], (pairs, FIELDS)).reshape(pairs * FIELDS, 1)
    surface_on_atm = pl.pallas_call(
        reply_kernel,
        out_shape=jax.ShapeDtypeStruct((FIELDS, height, breadth), F32),
        in_specs=[SM, VM, VM, VM],
        out_specs=VM,
        scratch_shapes=[
            pltpu.VMEM((pairs * FIELDS, breadth), F32),
            pltpu.VMEM((height, 8, breadth), F32),
        ],
        compiler_params=params(32),
        cost_estimate=pl.CostEstimate(
            flops=3 * 2 * devices * 128 ** 3,
            bytes_accessed=3 * 1024 * 1024,
            transcendentals=0,
        ),
    )(pair_block, ids, gathered, pair_weight)
    return (current, ocean_next, surface_on_atm)


def solution(mesh):
    rows = P(("sec", "row", "col"))
    return jax.shard_map(
        on_device,
        mesh=mesh,
        in_specs=(
            P(("sec", "row"), "col", None),
            P(),
            rows,
            rows,
            P(("sec", "row", "col"), None, None),
            P(("sec", "row", "col"), None, None),
            P(),
            P(),
            P(("sec", "row", "col"), None),
        ),
        out_specs=(
            P(("sec", "row"), "col", None),
            P(("sec", "row", "col"), None, None),
            P(None, ("sec", "row"), "col"),
        ),
        check_vma=False,
    )
```

time: 240 us -> 190 us (0.79)
  the two profiles are of different devices: /device:TPU:22 before, /device:TPU:31 now
where the time goes in v1:
time: 190 us; the launch traced here: 189 us
  starting transfers between devices  134 us (71%)
  between operations  15.1 us (8%)
  Pallas kernels  14.1 us (7%)
  waiting for transfers between devices  7.06 us (4%)
  other arithmetic  6.49 us (3%)
  local copies, waits for them, and re-layouts  6.4 us (3%)
  matrix products  6.14 us (3%)
    ppermute x28, starting transfers between devices, on_device(): came = lax.ppermute(held[m], 'col', onward)  78 us
    ppermute x1, starting transfers between devices, on_device(): table_far = lax.ppermute(table, 'col', onward)  17.9 us
    ppermute x2, starting transfers between devices, on_device(): swapped = [lax.ppermute(held[PARTS + m], 'col', mate) for m in range(PARTS)]  15.3 us
    ppermute x4, starting transfers between devices, edges(): return (lax.ppermute(last, axis, up), lax.ppermute(first, axis, down))  12.3 us
    pallas_call x1, Pallas kernels, on_device(): pl.pallas_call(contrib_kernel, out_shape=(blocks_of(dense + n_slots), blo...  5.76 us
    unnamed x25, local copies, waits for them, and re-layouts  4.77 us
    ppermute x4, waiting for transfers between devices, edges(): return (lax.ppermute(last, axis, up), lax.ppermute(first, axis, down))  4.46 us
    pallas_call x1, Pallas kernels, on_device(): pl.pallas_call(reply_kernel, out_shape=jax.ShapeDtypeStruct((FIELDS, heig...  4.37 us
  transfers between devices with their start and end apart: 40, of which 4 were waited for; matrix products, arithmetic and copies ran while one was open for 6% of the time, Pallas kernels for 2%

profile of v1, /device:TPU:31, one launch (start us, length us, event | category | flops | bytes accessed | tf_op | source)
XLA Modules:
  0.0 188.8 jit_solution(18103862453756104288)
XLA Ops:
  9.7 17.9 %collective-permute-start.4 = (s32[32]{0:T(128)S(1)}, s32[32]{0:T(128)S(1)}, u32[]{:S(2)}, u32[]{:S(2)}) collective-permute-start(s32[32]{0:T(128)S(1)} %select_reduce_fusion), channel_id=1, source_target_pairs={{0,2},{1,31},{2,4},{3,1},{4,6},{5,3},{6,8},{7,5},{8,10},{9,7},{10,... | collective-permute-start | bytes 392 | tf_op jit(solution)/shard_map/ppermute | solution.py:259
  30.5 5.3 %collective-permute-start = (bf16[3,128,128]{2,1,0:T(8,128)(2,1)S(1)}, bf16[3,128,128]{2,1,0:T(8,128)(2,1)S(1)}, u32[]{:S(2)}, u32[]{:S(2)}) collective-permute-start(bf16[3,128,128]{2,1,0:T(8,128)(2,1)S(1)} %get-tuple-element.115), channel_id=1, source_target_pairs={{0,32},{32,64},{64,96},{96,128},{128,160},{160,192},{192,224},{224... | collective-permute-start | bytes 294920 | tf_op jit(solution)/shard_map/ppermute | solution.py:29
  42.3 2.5 %collective-permute-done.1 = bf16[3,128,128]{2,1,0:T(8,128)(2,1)S(1)} collective-permute-done((bf16[3,128,128]{2,1,0:T(8,128)(2,1)S(1)}, bf16[3,128,128]{2,1,0:T(8,128)(2,1)S(1)}, u32[]{:S(2)}, u32[]{:S(2)}) %collective-permute-start.1) | collective-permute-done | bytes 98336 | tf_op jit(solution)/shard_map/ppermute | solution.py:29
  46.8 3.2 %collective-permute-start.3 = (bf16[30,3,128]{2,1,0:T(4,128)(2,1)S(1)}, bf16[30,3,128]{2,1,0:T(4,128)(2,1)S(1)}, u32[]{:S(2)}, u32[]{:S(2)}) collective-permute-start(bf16[30,3,128]{2,1,0:T(4,128)(2,1)S(1)} %get-tuple-element.113), channel_id=1, source_target_pairs={{1,0},{2,1},{3,2},{4,3},{5,4},{6,5},{7,6},{8,7},{9,8},{10,9},{11,1... | collective-permute-start | bytes 69128 | tf_op jit(solution)/shard_map/ppermute | solution.py:29
  50.0 2.0 %collective-permute-done.3 = bf16[30,3,128]{2,1,0:T(4,128)(2,1)S(1)} collective-permute-done((bf16[30,3,128]{2,1,0:T(4,128)(2,1)S(1)}, bf16[30,3,128]{2,1,0:T(4,128)(2,1)S(1)}, u32[]{:S(2)}, u32[]{:S(2)}) %collective-permute-start.3) | collective-permute-done | bytes 23072 | tf_op jit(solution)/shard_map/ppermute | solution.py:29
  56.5 5.8 %shard_map.112 = (bf16[160,128,128]{2,1,0:T(8,128)(2,1)}, bf16[16,128,128]{2,1,0:T(8,128)(2,1)S(1)}, bf16[4,128,128]{2,1,0:T(8,128)(2,1)S(1)}, bf16[4,128,128]{2...) custom-call(s32[32]{0:T(128)S(1)} %copy-done.7, s32[32]{0:T(128)S(1)} %get-tuple-element.109.idx, ...), custom_call_target="tpu_custom_call" | custom-call | flops 134217728 | bytes 8388608 | tf_op jit(solution)/shard_map/pallas_call | solution.py:292
  64.1 4.3 %collective-permute-start.6 = (bf16[4,128,128]{2,1,0:T(8,128)(2,1)S(1)}, bf16[4,128,128]{2,1,0:T(8,128)(2,1)S(1)}, u32[]{:S(2)}, u32[]{:S(2)}) collective-permute-start(bf16[4,128,128]{2,1,0:T(8,128)(2,1)S(1)} %get-tuple-element.72), channel_id=1, source_target_pairs={{0,2},{1,31},{2,4},{3,1},{4,6},{5,3},{6,8},{7,5},{8,10},{9,7},{10,... | collective-permute-start | bytes 393224 | tf_op jit(solution)/shard_map/ppermute | solution.py:314
  73.7 3.7 %collective-permute-start.31 = (bf16[4,128,128]{2,1,0:T(8,128)(2,1)}, bf16[4,128,128]{2,1,0:T(8,128)(2,1)}, u32[]{:S(2)}, u32[]{:S(2)}) collective-permute-start(bf16[4,128,128]{2,1,0:T(8,128)(2,1)} %get-tuple-element.100), channel_id=1, source_target_pairs={{0,2},{1,31},{2,4},{3,1},{4,6},{5,3},{6,8},{7,5},{8,10},{9,7},{10,... | collective-permute-start | bytes 393224 | tf_op jit(solution)/shard_map/ppermute | solution.py:348
  77.6 3.2 %collective-permute-start.23 = (bf16[4,128,128]{2,1,0:T(8,128)(2,1)}, bf16[4,128,128]{2,1,0:T(8,128)(2,1)S(1)}, u32[]{:S(2)}, u32[]{:S(2)}) collective-permute-start(bf16[4,128,128]{2,1,0:T(8,128)(2,1)} %copy-done.8), channel_id=1, source_target_pairs={{0,2},{1,31},{2,4},{3,1},{4,6},{5,3},{6,8},{7,5},{8,10},{9,7},{10,... | collective-permute-start | bytes 393224 | tf_op jit(solution)/shard_map/ppermute | solution.py:348
  80.8 2.8 %collective-permute-start.16 = (bf16[4,128,128]{2,1,0:T(8,128)(2,1)S(1)}, bf16[4,128,128]{2,1,0:T(8,128)(2,1)S(1)}, u32[]{:S(2)}, u32[]{:S(2)}) collective-permute-start(bf16[4,128,128]{2,1,0:T(8,128)(2,1)S(1)} %get-tuple-element.84), channel_id=1, source_target_pairs={{0,2},{1,31},{2,4},{3,1},{4,6},{5,3},{6,8},{7,5},{8,10},{9,7},{10,... | collective-permute-start | bytes 393224 | tf_op jit(solution)/shard_map/ppermute | solution.py:348
  83.6 4.0 %collective-permute-start.8 = (bf16[4,128,128]{2,1,0:T(8,128)(2,1)S(1)}, bf16[4,128,128]{2,1,0:T(8,128)(2,1)S(1)}, u32[]{:S(2)}, u32[]{:S(2)}) collective-permute-start(bf16[4,128,128]{2,1,0:T(8,128)(2,1)S(1)} %get-tuple-element.74), channel_id=1, source_target_pairs={{0,2},{1,31},{2,4},{3,1},{4,6},{5,3},{6,8},{7,5},{8,10},{9,7},{10,... | collective-permute-start | bytes 393224 | tf_op jit(solution)/shard_map/ppermute | solution.py:348
  87.6 2.5 %copy-done.1 = bf16[160,128,128]{2,1,0:T(8,128)(2,1)S(1)} copy-done((bf16[160,128,128]{2,1,0:T(8,128)(2,1)S(1)}, bf16[160,128,128]{2,1,0:T(8,128)(2,1)}, u32[]{:S(2)}) %copy-start.1) | copy-done | bytes 5242904
  92.8 3.7 %collective-permute-start.32 = (bf16[4,128,128]{2,1,0:T(8,128)(2,1)S(1)}, bf16[4,128,128]{2,1,0:T(8,128)(2,1)S(1)}, u32[]{:S(2)}, u32[]{:S(2)}) collective-permute-start(bf16[4,128,128]{2,1,0:T(8,128)(2,1)S(1)} %add_convert_fusion.6), channel_id=1, source_target_pairs={{0,2},{1,31},{2,4},{3,1},{4,6},{5,3},{6,8},{7,5},{8,10},{9,7},{10,... | collective-permute-start | bytes 393224 | tf_op jit(solution)/shard_map/ppermute | solution.py:348
  96.5 2.0 %collective-permute-start.24 = (bf16[4,128,128]{2,1,0:T(8,128)(2,1)S(1)}, bf16[4,128,128]{2,1,0:T(8,128)(2,1)S(1)}, u32[]{:S(2)}, u32[]{:S(2)}) collective-permute-start(bf16[4,128,128]{2,1,0:T(8,128)(2,1)S(1)} %add_convert_fusion.13), channel_id=1, source_target_pairs={{0,2},{1,31},{2,4},{3,1},{4,6},{5,3},{6,8},{7,5},{8,10},{9,7},{10,... | collective-permute-start | bytes 393224 | tf_op jit(solution)/shard_map/ppermute | solution.py:348
  100.6 2.3 %collective-permute-start.10 = (bf16[4,128,128]{2,1,0:T(8,128)(2,1)S(1)}, bf16[4,128,128]{2,1,0:T(8,128)(2,1)S(1)}, u32[]{:S(2)}, u32[]{:S(2)}) collective-permute-start(bf16[4,128,128]{2,1,0:T(8,128)(2,1)S(1)} %add_convert_fusion.27), channel_id=1, source_target_pairs={{0,2},{1,31},{2,4},{3,1},{4,6},{5,3},{6,8},{7,5},{8,10},{9,7},{10,... | collective-permute-start | bytes 393224 | tf_op jit(solution)/shard_map/ppermute | solution.py:348
  103.0 3.7 %collective-permute-start.33 = (bf16[4,128,128]{2,1,0:T(8,128)(2,1)S(1)}, bf16[4,128,128]{2,1,0:T(8,128)(2,1)S(1)}, u32[]{:S(2)}, u32[]{:S(2)}) collective-permute-start(bf16[4,128,128]{2,1,0:T(8,128)(2,1)S(1)} %add_convert_fusion.5), channel_id=1, source_target_pairs={{0,2},{1,31},{2,4},{3,1},{4,6},{5,3},{6,8},{7,5},{8,10},{9,7},{10,... | collective-permute-start | bytes 393224 | tf_op jit(solution)/shard_map/ppermute | solution.py:348
  106.7 2.0 %collective-permute-start.25 = (bf16[4,128,128]{2,1,0:T(8,128)(2,1)S(1)}, bf16[4,128,128]{2,1,0:T(8,128)(2,1)S(1)}, u32[]{:S(2)}, u32[]{:S(2)}) collective-permute-start(bf16[4,128,128]{2,1,0:T(8,128)(2,1)S(1)} %add_convert_fusion.12), channel_id=1, source_target_pairs={{0,2},{1,31},{2,4},{3,1},{4,6},{5,3},{6,8},{7,5},{8,10},{9,7},{10,... | collective-permute-start | bytes 393224 | tf_op jit(solution)/shard_map/ppermute | solution.py:348
  114.8 2.0 %collective-permute-start.26 = (bf16[4,128,128]{2,1,0:T(8,128)(2,1)S(1)}, bf16[4,128,128]{2,1,0:T(8,128)(2,1)S(1)}, u32[]{:S(2)}, u32[]{:S(2)}) collective-permute-start(bf16[4,128,128]{2,1,0:T(8,128)(2,1)S(1)} %add_convert_fusion.11), channel_id=1, source_target_pairs={{0,2},{1,31},{2,4},{3,1},{4,6},{5,3},{6,8},{7,5},{8,10},{9,7},{10,... | collective-permute-start | bytes 393224 | tf_op jit(solution)/shard_map/ppermute | solution.py:348
  116.8 3.3 %collective-permute-start.19 = (bf16[4,128,128]{2,1,0:T(8,128)(2,1)S(1)}, bf16[4,128,128]{2,1,0:T(8,128)(2,1)S(1)}, u32[]{:S(2)}, u32[]{:S(2)}) collective-permute-start(bf16[4,128,128]{2,1,0:T(8,128)(2,1)S(1)} %add_convert_fusion.18), channel_id=1, source_target_pairs={{0,2},{1,31},{2,4},{3,1},{4,6},{5,3},{6,8},{7,5},{8,10},{9,7},{10,... | collective-permute-start | bytes 393224 | tf_op jit(solution)/shard_map/ppermute | solution.py:348
  120.2 4.3 %collective-permute-start.12 = (bf16[4,128,128]{2,1,0:T(8,128)(2,1)S(1)}, bf16[4,128,128]{2,1,0:T(8,128)(2,1)S(1)}, u32[]{:S(2)}, u32[]{:S(2)}) collective-permute-start(bf16[4,128,128]{2,1,0:T(8,128)(2,1)S(1)} %add_convert_fusion.25), channel_id=1, source_target_pairs={{0,2},{1,31},{2,4},{3,1},{4,6},{5,3},{6,8},{7,5},{8,10},{9,7},{10,... | collective-permute-start | bytes 393224 | tf_op jit(solution)/shard_map/ppermute | solution.py:348
  124.5 3.7 %collective-permute-start.35 = (bf16[4,128,128]{2,1,0:T(8,128)(2,1)S(1)}, bf16[4,128,128]{2,1,0:T(8,128)(2,1)S(1)}, u32[]{:S(2)}, u32[]{:S(2)}) collective-permute-start(bf16[4,128,128]{2,1,0:T(8,128)(2,1)S(1)} %add_convert_fusion.3), channel_id=1, source_target_pairs={{0,2},{1,31},{2,4},{3,1},{4,6},{5,3},{6,8},{7,5},{8,10},{9,7},{10,... | collective-permute-start | bytes 393224 | tf_op jit(solution)/shard_map/ppermute | solution.py:348
  128.3 3.2 %collective-permute-start.27 = (bf16[4,128,128]{2,1,0:T(8,128)(2,1)S(1)}, bf16[4,128,128]{2,1,0:T(8,128)(2,1)S(1)}, u32[]{:S(2)}, u32[]{:S(2)}) collective-permute-start(bf16[4,128,128]{2,1,0:T(8,128)(2,1)S(1)} %add_convert_fusion.10), channel_id=1, source_target_pairs={{0,2},{1,31},{2,4},{3,1},{4,6},{5,3},{6,8},{7,5},{8,10},{9,7},{10,... | collective-permute-start | bytes 393224 | tf_op jit(solution)/shard_map/ppermute | solution.py:348
  131.6 2.7 %collective-permute-start.20 = (bf16[4,128,128]{2,1,0:T(8,128)(2,1)S(1)}, bf16[4,128,128]{2,1,0:T(8,128)(2,1)S(1)}, u32[]{:S(2)}, u32[]{:S(2)}) collective-permute-start(bf16[4,128,128]{2,1,0:T(8,128)(2,1)S(1)} %add_convert_fusion.17), channel_id=1, source_target_pairs={{0,2},{1,31},{2,4},{3,1},{4,6},{5,3},{6,8},{7,5},{8,10},{9,7},{10,... | collective-permute-start | bytes 393224 | tf_op jit(solution)/shard_map/ppermute | solution.py:348
  134.4 4.0 %collective-permute-start.13 = (bf16[4,128,128]{2,1,0:T(8,128)(2,1)S(1)}, bf16[4,128,128]{2,1,0:T(8,128)(2,1)S(1)}, u32[]{:S(2)}, u32[]{:S(2)}) collective-permute-start(bf16[4,128,128]{2,1,0:T(8,128)(2,1)S(1)} %add_convert_fusion.24), channel_id=1, source_target_pairs={{0,2},{1,31},{2,4},{3,1},{4,6},{5,3},{6,8},{7,5},{8,10},{9,7},{10,... | collective-permute-start | bytes 393224 | tf_op jit(solution)/shard_map/ppermute | solution.py:348
  138.5 3.7 %collective-permute-start.36 = (bf16[4,128,128]{2,1,0:T(8,128)(2,1)S(1)}, bf16[4,128,128]{2,1,0:T(8,128)(2,1)S(1)}, u32[]{:S(2)}, u32[]{:S(2)}) collective-permute-start(bf16[4,128,128]{2,1,0:T(8,128)(2,1)S(1)} %add_convert_fusion.2), channel_id=1, source_target_pairs={{0,2},{1,31},{2,4},{3,1},{4,6},{5,3},{6,8},{7,5},{8,10},{9,7},{10,... | collective-permute-start | bytes 393224 | tf_op jit(solution)/shard_map/ppermute | solution.py:348
  142.3 2.0 %collective-permute-start.28 = (bf16[4,128,128]{2,1,0:T(8,128)(2,1)S(1)}, bf16[4,128,128]{2,1,0:T(8,128)(2,1)S(1)}, u32[]{:S(2)}, u32[]{:S(2)}) collective-permute-start(bf16[4,128,128]{2,1,0:T(8,128)(2,1)S(1)} %add_convert_fusion.9), channel_id=1, source_target_pairs={{0,2},{1,31},{2,4},{3,1},{4,6},{5,3},{6,8},{7,5},{8,10},{9,7},{10,... | collective-permute-start | bytes 393224 | tf_op jit(solution)/shard_map/ppermute | solution.py:348
  144.4 2.1 %collective-permute-start.21 = (bf16[4,128,128]{2,1,0:T(8,128)(2,1)S(1)}, bf16[4,128,128]{2,1,0:T(8,128)(2,1)S(1)}, u32[]{:S(2)}, u32[]{:S(2)}) collective-permute-start(bf16[4,128,128]{2,1,0:T(8,128)(2,1)S(1)} %add_convert_fusion.16), channel_id=1, source_target_pairs={{0,2},{1,31},{2,4},{3,1},{4,6},{5,3},{6,8},{7,5},{8,10},{9,7},{10,... | collective-permute-start | bytes 393224 | tf_op jit(solution)/shard_map/ppermute | solution.py:348
  146.5 2.3 %collective-permute-start.14 = (bf16[4,128,128]{2,1,0:T(8,128)(2,1)S(1)}, bf16[4,128,128]{2,1,0:T(8,128)(2,1)S(1)}, u32[]{:S(2)}, u32[]{:S(2)}) collective-permute-start(bf16[4,128,128]{2,1,0:T(8,128)(2,1)S(1)} %add_convert_fusion.23), channel_id=1, source_target_pairs={{0,2},{1,31},{2,4},{3,1},{4,6},{5,3},{6,8},{7,5},{8,10},{9,7},{10,... | collective-permute-start | bytes 393224 | tf_op jit(solution)/shard_map/ppermute | solution.py:348
  148.9 3.7 %collective-permute-start.37 = (bf16[4,128,128]{2,1,0:T(8,128)(2,1)S(1)}, bf16[4,128,128]{2,1,0:T(8,128)(2,1)S(1)}, u32[]{:S(2)}, u32[]{:S(2)}) collective-permute-start(bf16[4,128,128]{2,1,0:T(8,128)(2,1)S(1)} %add_convert_fusion.1), channel_id=1, source_target_pairs={{0,2},{1,31},{2,4},{3,1},{4,6},{5,3},{6,8},{7,5},{8,10},{9,7},{10,... | collective-permute-start | bytes 393224 | tf_op jit(solution)/shard_map/ppermute | solution.py:348
  152.6 2.0 %collective-permute-start.29 = (bf16[4,128,128]{2,1,0:T(8,128)(2,1)S(1)}, bf16[4,128,128]{2,1,0:T(8,128)(2,1)S(1)}, u32[]{:S(2)}, u32[]{:S(2)}) collective-permute-start(bf16[4,128,128]{2,1,0:T(8,128)(2,1)S(1)} %add_convert_fusion.8), channel_id=1, source_target_pairs={{0,2},{1,31},{2,4},{3,1},{4,6},{5,3},{6,8},{7,5},{8,10},{9,7},{10,... | collective-permute-start | bytes 393224 | tf_op jit(solution)/shard_map/ppermute | solution.py:348
  158.7 13.3 %collective-permute-start.38 = (bf16[4,128,128]{2,1,0:T(8,128)(2,1)S(1)}, bf16[4,128,128]{2,1,0:T(8,128)(2,1)S(1)}, u32[]{:S(2)}, u32[]{:S(2)}) collective-permute-start(bf16[4,128,128]{2,1,0:T(8,128)(2,1)S(1)} %add_convert_fusion), channel_id=1, source_target_pairs={{0,1},{1,0},{2,3},{3,2},{4,5},{5,4},{6,7},{7,6},{8,9},{9,8},{10,11... | collective-permute-start | bytes 393224 | tf_op jit(solution)/shard_map/ppermute | solution.py:352
  177.6 4.4 %shard_map.116 = f32[4,24,128]{2,1,0:T(8,128)} custom-call(s32[32]{0:T(128)S(1)} %copy-done.7, s32[128,1]{1,0:T(8,128)S(1)} %reshape.196.ids, bf16[32,176,128]{2,1,0:T(8,128)(2,1)S(1)} %bitcast.24, bf16[32,128,128]{2,1,0:T(8,128)(2,1)S(1)} %copy-done.2), custom_call_target="tpu_custom_call" | custom-call | flops 402653184 | bytes 3145728 | tf_op jit(solution)/shard_map/pallas_call | solution.py:367
  (139 shorter events, 46.2 us)
Async XLA Ops:
  7.2 169.1 %all-gather.3.cloned.1.call-start = ((), (), s32[]{:S(2)}) async-start(), calls=%async_computation | async-start | bytes 1486848 | tf_op jit(solution)/shard_map/all_gather | solution.py:313
  9.7 46.7 %collective-permute-start.4 = (s32[32]{0:T(128)S(1)}, s32[32]{0:T(128)S(1)}, u32[]{:S(2)}, u32[]{:S(2)}) collective-permute-start(s32[32]{0:T(128)S(1)} %select_reduce_fusion), channel_id=1, source_target_pairs={{0,2},{1,31},{2,4},{3,1},{4,6},{5,3},{6,8},{7,5},{8,10},{9,7},{10,... | collective-permute-start | bytes 392 | tf_op jit(solution)/shard_map/ppermute | solution.py:259
  27.6 28.8 %collective-permute-start.5 = (s32[32]{0:T(128)S(1)}, s32[32]{0:T(128)S(1)}, u32[]{:S(2)}, u32[]{:S(2)}) collective-permute-start(s32[32]{0:T(128)S(1)} %select_reduce_fusion), channel_id=1, source_target_pairs={{0,1},{1,0},{2,3},{3,2},{4,5},{5,4},{6,7},{7,6},{8,9},{9,8},{10,11... | collective-permute-start | bytes 392 | tf_op jit(solution)/shard_map/ppermute | solution.py:260
  30.5 11.6 %collective-permute-start = (bf16[3,128,128]{2,1,0:T(8,128)(2,1)S(1)}, bf16[3,128,128]{2,1,0:T(8,128)(2,1)S(1)}, u32[]{:S(2)}, u32[]{:S(2)}) collective-permute-start(bf16[3,128,128]{2,1,0:T(8,128)(2,1)S(1)} %get-tuple-element.115), channel_id=1, source_target_pairs={{0,32},{32,64},{64,96},{96,128},{128,160},{160,192},{192,224},{224... | collective-permute-start | bytes 294920 | tf_op jit(solution)/shard_map/ppermute | solution.py:29
  62.2 25.4 %collective-permute-start.9 = (bf16[24,128,128]{2,1,0:T(8,128)(2,1)}, bf16[24,128,128]{2,1,0:T(8,128)(2,1)S(1)}, u32[]{:S(2)}, u32[]{:S(2)}) collective-permute-start(bf16[24,128,128]{2,1,0:T(8,128)(2,1)} %get-tuple-element.76), channel_id=1, source_target_pairs={{0,1},{1,0},{2,3},{3,2},{4,5},{5,4},{6,7},{7,6},{8,9},{9,8},{10,11... | collective-permute-start | bytes 2359304 | tf_op jit(solution)/shard_map/ppermute | solution.py:316
  73.7 18.1 %collective-permute-start.31 = (bf16[4,128,128]{2,1,0:T(8,128)(2,1)}, bf16[4,128,128]{2,1,0:T(8,128)(2,1)}, u32[]{:S(2)}, u32[]{:S(2)}) collective-permute-start(bf16[4,128,128]{2,1,0:T(8,128)(2,1)} %get-tuple-element.100), channel_id=1, source_target_pairs={{0,2},{1,31},{2,4},{3,1},{4,6},{5,3},{6,8},{7,5},{8,10},{9,7},{10,... | collective-permute-start | bytes 393224 | tf_op jit(solution)/shard_map/ppermute | solution.py:348
  77.6 18.9 %collective-permute-start.23 = (bf16[4,128,128]{2,1,0:T(8,128)(2,1)}, bf16[4,128,128]{2,1,0:T(8,128)(2,1)S(1)}, u32[]{:S(2)}, u32[]{:S(2)}) collective-permute-start(bf16[4,128,128]{2,1,0:T(8,128)(2,1)} %copy-done.8), channel_id=1, source_target_pairs={{0,2},{1,31},{2,4},{3,1},{4,6},{5,3},{6,8},{7,5},{8,10},{9,7},{10,... | collective-permute-start | bytes 393224 | tf_op jit(solution)/shard_map/ppermute | solution.py:348
  80.8 17.7 %collective-permute-start.16 = (bf16[4,128,128]{2,1,0:T(8,128)(2,1)S(1)}, bf16[4,128,128]{2,1,0:T(8,128)(2,1)S(1)}, u32[]{:S(2)}, u32[]{:S(2)}) collective-permute-start(bf16[4,128,128]{2,1,0:T(8,128)(2,1)S(1)} %get-tuple-element.84), channel_id=1, source_target_pairs={{0,2},{1,31},{2,4},{3,1},{4,6},{5,3},{6,8},{7,5},{8,10},{9,7},{10,... | collective-permute-start | bytes 393224 | tf_op jit(solution)/shard_map/ppermute | solution.py:348
  83.6 17.0 %collective-permute-start.8 = (bf16[4,128,128]{2,1,0:T(8,128)(2,1)S(1)}, bf16[4,128,128]{2,1,0:T(8,128)(2,1)S(1)}, u32[]{:S(2)}, u32[]{:S(2)}) collective-permute-start(bf16[4,128,128]{2,1,0:T(8,128)(2,1)S(1)} %get-tuple-element.74), channel_id=1, source_target_pairs={{0,2},{1,31},{2,4},{3,1},{4,6},{5,3},{6,8},{7,5},{8,10},{9,7},{10,... | collective-permute-start | bytes 393224 | tf_op jit(solution)/shard_map/ppermute | solution.py:348
  92.8 10.1 %collective-permute-start.32 = (bf16[4,128,128]{2,1,0:T(8,128)(2,1)S(1)}, bf16[4,128,128]{2,1,0:T(8,128)(2,1)S(1)}, u32[]{:S(2)}, u32[]{:S(2)}) collective-permute-start(bf16[4,128,128]{2,1,0:T(8,128)(2,1)S(1)} %add_convert_fusion.6), channel_id=1, source_target_pairs={{0,2},{1,31},{2,4},{3,1},{4,6},{5,3},{6,8},{7,5},{8,10},{9,7},{10,... | collective-permute-start | bytes 393224 | tf_op jit(solution)/shard_map/ppermute | solution.py:348
  96.5 10.1 %collective-permute-start.24 = (bf16[4,128,128]{2,1,0:T(8,128)(2,1)S(1)}, bf16[4,128,128]{2,1,0:T(8,128)(2,1)S(1)}, u32[]{:S(2)}, u32[]{:S(2)}) collective-permute-start(bf16[4,128,128]{2,1,0:T(8,128)(2,1)S(1)} %add_convert_fusion.13), channel_id=1, source_target_pairs={{0,2},{1,31},{2,4},{3,1},{4,6},{5,3},{6,8},{7,5},{8,10},{9,7},{10,... | collective-permute-start | bytes 393224 | tf_op jit(solution)/shard_map/ppermute | solution.py:348
  98.6 10.2 %collective-permute-start.17 = (bf16[4,128,128]{2,1,0:T(8,128)(2,1)S(1)}, bf16[4,128,128]{2,1,0:T(8,128)(2,1)S(1)}, u32[]{:S(2)}, u32[]{:S(2)}) collective-permute-start(bf16[4,128,128]{2,1,0:T(8,128)(2,1)S(1)} %add_convert_fusion.20), channel_id=1, source_target_pairs={{0,2},{1,31},{2,4},{3,1},{4,6},{5,3},{6,8},{7,5},{8,10},{9,7},{10,... | collective-permute-start | bytes 393224 | tf_op jit(solution)/shard_map/ppermute | solution.py:348
  100.6 10.1 %collective-permute-start.10 = (bf16[4,128,128]{2,1,0:T(8,128)(2,1)S(1)}, bf16[4,128,128]{2,1,0:T(8,128)(2,1)S(1)}, u32[]{:S(2)}, u32[]{:S(2)}) collective-permute-start(bf16[4,128,128]{2,1,0:T(8,128)(2,1)S(1)} %add_convert_fusion.27), channel_id=1, source_target_pairs={{0,2},{1,31},{2,4},{3,1},{4,6},{5,3},{6,8},{7,5},{8,10},{9,7},{10,... | collective-permute-start | bytes 393224 | tf_op jit(solution)/shard_map/ppermute | solution.py:348
  103.0 9.8 %collective-permute-start.33 = (bf16[4,128,128]{2,1,0:T(8,128)(2,1)S(1)}, bf16[4,128,128]{2,1,0:T(8,128)(2,1)S(1)}, u32[]{:S(2)}, u32[]{:S(2)}) collective-permute-start(bf16[4,128,128]{2,1,0:T(8,128)(2,1)S(1)} %add_convert_fusion.5), channel_id=1, source_target_pairs={{0,2},{1,31},{2,4},{3,1},{4,6},{5,3},{6,8},{7,5},{8,10},{9,7},{10,... | collective-permute-start | bytes 393224 | tf_op jit(solution)/shard_map/ppermute | solution.py:348
  110.8 9.3 %collective-permute-start.11 = (bf16[4,128,128]{2,1,0:T(8,128)(2,1)S(1)}, bf16[4,128,128]{2,1,0:T(8,128)(2,1)S(1)}, u32[]{:S(2)}, u32[]{:S(2)}) collective-permute-start(bf16[4,128,128]{2,1,0:T(8,128)(2,1)S(1)} %add_convert_fusion.26), channel_id=1, source_target_pairs={{0,2},{1,31},{2,4},{3,1},{4,6},{5,3},{6,8},{7,5},{8,10},{9,7},{10,... | collective-permute-start | bytes 393224 | tf_op jit(solution)/shard_map/ppermute | solution.py:348
  112.8 11.7 %collective-permute-start.34 = (bf16[4,128,128]{2,1,0:T(8,128)(2,1)S(1)}, bf16[4,128,128]{2,1,0:T(8,128)(2,1)S(1)}, u32[]{:S(2)}, u32[]{:S(2)}) collective-permute-start(bf16[4,128,128]{2,1,0:T(8,128)(2,1)S(1)} %add_convert_fusion.4), channel_id=1, source_target_pairs={{0,2},{1,31},{2,4},{3,1},{4,6},{5,3},{6,8},{7,5},{8,10},{9,7},{10,... | collective-permute-start | bytes 393224 | tf_op jit(solution)/shard_map/ppermute | solution.py:348
  114.8 13.5 %collective-permute-start.26 = (bf16[4,128,128]{2,1,0:T(8,128)(2,1)S(1)}, bf16[4,128,128]{2,1,0:T(8,128)(2,1)S(1)}, u32[]{:S(2)}, u32[]{:S(2)}) collective-permute-start(bf16[4,128,128]{2,1,0:T(8,128)(2,1)S(1)} %add_convert_fusion.11), channel_id=1, source_target_pairs={{0,2},{1,31},{2,4},{3,1},{4,6},{5,3},{6,8},{7,5},{8,10},{9,7},{10,... | collective-permute-start | bytes 393224 | tf_op jit(solution)/shard_map/ppermute | solution.py:348
  116.8 14.7 %collective-permute-start.19 = (bf16[4,128,128]{2,1,0:T(8,128)(2,1)S(1)}, bf16[4,128,128]{2,1,0:T(8,128)(2,1)S(1)}, u32[]{:S(2)}, u32[]{:S(2)}) collective-permute-start(bf16[4,128,128]{2,1,0:T(8,128)(2,1)S(1)} %add_convert_fusion.18), channel_id=1, source_target_pairs={{0,2},{1,31},{2,4},{3,1},{4,6},{5,3},{6,8},{7,5},{8,10},{9,7},{10,... | collective-permute-start | bytes 393224 | tf_op jit(solution)/shard_map/ppermute | solution.py:348
  120.2 14.2 %collective-permute-start.12 = (bf16[4,128,128]{2,1,0:T(8,128)(2,1)S(1)}, bf16[4,128,128]{2,1,0:T(8,128)(2,1)S(1)}, u32[]{:S(2)}, u32[]{:S(2)}) collective-permute-start(bf16[4,128,128]{2,1,0:T(8,128)(2,1)S(1)} %add_convert_fusion.25), channel_id=1, source_target_pairs={{0,2},{1,31},{2,4},{3,1},{4,6},{5,3},{6,8},{7,5},{8,10},{9,7},{10,... | collective-permute-start | bytes 393224 | tf_op jit(solution)/shard_map/ppermute | solution.py:348
  124.5 13.9 %collective-permute-start.35 = (bf16[4,128,128]{2,1,0:T(8,128)(2,1)S(1)}, bf16[4,128,128]{2,1,0:T(8,128)(2,1)S(1)}, u32[]{:S(2)}, u32[]{:S(2)}) collective-permute-start(bf16[4,128,128]{2,1,0:T(8,128)(2,1)S(1)} %add_convert_fusion.3), channel_id=1, source_target_pairs={{0,2},{1,31},{2,4},{3,1},{4,6},{5,3},{6,8},{7,5},{8,10},{9,7},{10,... | collective-permute-start | bytes 393224 | tf_op jit(solution)/shard_map/ppermute | solution.py:348
  128.3 13.9 %collective-permute-start.27 = (bf16[4,128,128]{2,1,0:T(8,128)(2,1)S(1)}, bf16[4,128,128]{2,1,0:T(8,128)(2,1)S(1)}, u32[]{:S(2)}, u32[]{:S(2)}) collective-permute-start(bf16[4,128,128]{2,1,0:T(8,128)(2,1)S(1)} %add_convert_fusion.10), channel_id=1, source_target_pairs={{0,2},{1,31},{2,4},{3,1},{4,6},{5,3},{6,8},{7,5},{8,10},{9,7},{10,... | collective-permute-start | bytes 393224 | tf_op jit(solution)/shard_map/ppermute | solution.py:348
  131.6 12.7 %collective-permute-start.20 = (bf16[4,128,128]{2,1,0:T(8,128)(2,1)S(1)}, bf16[4,128,128]{2,1,0:T(8,128)(2,1)S(1)}, u32[]{:S(2)}, u32[]{:S(2)}) collective-permute-start(bf16[4,128,128]{2,1,0:T(8,128)(2,1)S(1)} %add_convert_fusion.17), channel_id=1, source_target_pairs={{0,2},{1,31},{2,4},{3,1},{4,6},{5,3},{6,8},{7,5},{8,10},{9,7},{10,... | collective-permute-start | bytes 393224 | tf_op jit(solution)/shard_map/ppermute | solution.py:348
  134.4 12.0 %collective-permute-start.13 = (bf16[4,128,128]{2,1,0:T(8,128)(2,1)S(1)}, bf16[4,128,128]{2,1,0:T(8,128)(2,1)S(1)}, u32[]{:S(2)}, u32[]{:S(2)}) collective-permute-start(bf16[4,128,128]{2,1,0:T(8,128)(2,1)S(1)} %add_convert_fusion.24), channel_id=1, source_target_pairs={{0,2},{1,31},{2,4},{3,1},{4,6},{5,3},{6,8},{7,5},{8,10},{9,7},{10,... | collective-permute-start | bytes 393224 | tf_op jit(solution)/shard_map/ppermute | solution.py:348
  138.5 10.3 %collective-permute-start.36 = (bf16[4,128,128]{2,1,0:T(8,128)(2,1)S(1)}, bf16[4,128,128]{2,1,0:T(8,128)(2,1)S(1)}, u32[]{:S(2)}, u32[]{:S(2)}) collective-permute-start(bf16[4,128,128]{2,1,0:T(8,128)(2,1)S(1)} %add_convert_fusion.2), channel_id=1, source_target_pairs={{0,2},{1,31},{2,4},{3,1},{4,6},{5,3},{6,8},{7,5},{8,10},{9,7},{10,... | collective-permute-start | bytes 393224 | tf_op jit(solution)/shard_map/ppermute | solution.py:348
  142.3 10.3 %collective-permute-start.28 = (bf16[4,128,128]{2,1,0:T(8,128)(2,1)S(1)}, bf16[4,128,128]{2,1,0:T(8,128)(2,1)S(1)}, u32[]{:S(2)}, u32[]{:S(2)}) collective-permute-start(bf16[4,128,128]{2,1,0:T(8,128)(2,1)S(1)} %add_convert_fusion.9), channel_id=1, source_target_pairs={{0,2},{1,31},{2,4},{3,1},{4,6},{5,3},{6,8},{7,5},{8,10},{9,7},{10,... | collective-permute-start | bytes 393224 | tf_op jit(solution)/shard_map/ppermute | solution.py:348
  144.4 10.3 %collective-permute-start.21 = (bf16[4,128,128]{2,1,0:T(8,128)(2,1)S(1)}, bf16[4,128,128]{2,1,0:T(8,128)(2,1)S(1)}, u32[]{:S(2)}, u32[]{:S(2)}) collective-permute-start(bf16[4,128,128]{2,1,0:T(8,128)(2,1)S(1)} %add_convert_fusion.16), channel_id=1, source_target_pairs={{0,2},{1,31},{2,4},{3,1},{4,6},{5,3},{6,8},{7,5},{8,10},{9,7},{10,... | collective-permute-start | bytes 393224 | tf_op jit(solution)/shard_map/ppermute | solution.py:348
  146.5 10.1 %collective-permute-start.14 = (bf16[4,128,128]{2,1,0:T(8,128)(2,1)S(1)}, bf16[4,128,128]{2,1,0:T(8,128)(2,1)S(1)}, u32[]{:S(2)}, u32[]{:S(2)}) collective-permute-start(bf16[4,128,128]{2,1,0:T(8,128)(2,1)S(1)} %add_convert_fusion.23), channel_id=1, source_target_pairs={{0,2},{1,31},{2,4},{3,1},{4,6},{5,3},{6,8},{7,5},{8,10},{9,7},{10,... | collective-permute-start | bytes 393224 | tf_op jit(solution)/shard_map/ppermute | solution.py:348
  148.9 9.8 %collective-permute-start.37 = (bf16[4,128,128]{2,1,0:T(8,128)(2,1)S(1)}, bf16[4,128,128]{2,1,0:T(8,128)(2,1)S(1)}, u32[]{:S(2)}, u32[]{:S(2)}) collective-permute-start(bf16[4,128,128]{2,1,0:T(8,128)(2,1)S(1)} %add_convert_fusion.1), channel_id=1, source_target_pairs={{0,2},{1,31},{2,4},{3,1},{4,6},{5,3},{6,8},{7,5},{8,10},{9,7},{10,... | collective-permute-start | bytes 393224 | tf_op jit(solution)/shard_map/ppermute | solution.py:348
  152.6 19.4 %collective-permute-start.29 = (bf16[4,128,128]{2,1,0:T(8,128)(2,1)S(1)}, bf16[4,128,128]{2,1,0:T(8,128)(2,1)S(1)}, u32[]{:S(2)}, u32[]{:S(2)}) collective-permute-start(bf16[4,128,128]{2,1,0:T(8,128)(2,1)S(1)} %add_convert_fusion.8), channel_id=1, source_target_pairs={{0,2},{1,31},{2,4},{3,1},{4,6},{5,3},{6,8},{7,5},{8,10},{9,7},{10,... | collective-permute-start | bytes 393224 | tf_op jit(solution)/shard_map/ppermute | solution.py:348
  154.7 19.3 %collective-permute-start.22 = (bf16[4,128,128]{2,1,0:T(8,128)(2,1)S(1)}, bf16[4,128,128]{2,1,0:T(8,128)(2,1)S(1)}, u32[]{:S(2)}, u32[]{:S(2)}) collective-permute-start(bf16[4,128,128]{2,1,0:T(8,128)(2,1)S(1)} %add_convert_fusion.15), channel_id=1, source_target_pairs={{0,2},{1,31},{2,4},{3,1},{4,6},{5,3},{6,8},{7,5},{8,10},{9,7},{10,... | collective-permute-start | bytes 393224 | tf_op jit(solution)/shard_map/ppermute | solution.py:348
  156.7 17.4 %collective-permute-start.15 = (bf16[4,128,128]{2,1,0:T(8,128)(2,1)S(1)}, bf16[4,128,128]{2,1,0:T(8,128)(2,1)S(1)}, u32[]{:S(2)}, u32[]{:S(2)}) collective-permute-start(bf16[4,128,128]{2,1,0:T(8,128)(2,1)S(1)} %add_convert_fusion.22), channel_id=1, source_target_pairs={{0,2},{1,31},{2,4},{3,1},{4,6},{5,3},{6,8},{7,5},{8,10},{9,7},{10,... | collective-permute-start | bytes 393224 | tf_op jit(solution)/shard_map/ppermute | solution.py:348
  158.7 15.4 %collective-permute-start.38 = (bf16[4,128,128]{2,1,0:T(8,128)(2,1)S(1)}, bf16[4,128,128]{2,1,0:T(8,128)(2,1)S(1)}, u32[]{:S(2)}, u32[]{:S(2)}) collective-permute-start(bf16[4,128,128]{2,1,0:T(8,128)(2,1)S(1)} %add_convert_fusion), channel_id=1, source_target_pairs={{0,1},{1,0},{2,3},{3,2},{4,5},{5,4},{6,7},{7,6},{8,9},{9,8},{10,11... | collective-permute-start | bytes 393224 | tf_op jit(solution)/shard_map/ppermute | solution.py:352
  (19 other events, 254.0 us)
Sparse Core Ops, SparseCore 0:
  77.7 69.8 all-gather.2

commit v2 on v1

v2 whole, which is shorter than its diff:
```python
import jax
import jax.numpy as jnp
from jax import lax
from jax.experimental import pallas as pl
from jax.experimental.pallas import tpu as pltpu
from jax.sharding import PartitionSpec as P

FIELDS = 4
SUB = 3
KAPPA = 0.24
GROUP = 4
PAYLOAD = 176
BF = jnp.bfloat16
F32 = jnp.float32

VM = pl.BlockSpec(memory_space=pltpu.VMEM)
SM = pl.BlockSpec(memory_space=pltpu.SMEM)


def params(mib):
    return pltpu.CompilerParams(vmem_limit_bytes=mib * 1024 * 1024)


def edges(array, axis, dim, width):
    peers, length = lax.axis_size(axis), array.shape[dim]
    up = [(i, i + 1) for i in range(peers - 1)]
    down = [(j, i) for i, j in up]
    last = lax.slice_in_dim(array, length - width, length, axis=dim)
    first = lax.slice_in_dim(array, 0, width, axis=dim)
    return lax.ppermute(last, axis, up), lax.ppermute(first, axis, down)


def tall_patch(atm):
    before, after = edges(atm, ("sec", "row"), 0, SUB)
    return jnp.concatenate([before, atm, after], axis=0)


def substeps(tall, notes, vert_inverse):
    wide = SUB
    height, breadth = tall.shape[0] - 2 * wide, tall.shape[1]
    line = jnp.broadcast_to(notes.astype(BF), (1, wide, breadth))
    peers = lax.axis_size("col")
    up = [(i, i + 1) for i in range(peers - 1)]
    down = [(j, i) for i, j in up]
    left = lax.ppermute(jnp.concatenate([tall[:, breadth - wide:], line], axis=0), "col", up)
    right = lax.ppermute(jnp.concatenate([tall[:, :wide], line], axis=0), "col", down)
    told = jnp.where(lax.axis_index("col") % 2 == 0, right[-1, 0], left[-1, 0])
    told = told.astype(jnp.int32)
    current = jnp.concatenate([left[:-1], tall, right[:-1]], axis=1)
    row_at = lax.axis_index(("sec", "row")) * height
    col_at = lax.axis_index("col") * breadth
    rows_all = lax.axis_size(("sec", "row")) * height
    cols_all = lax.axis_size("col") * breadth
    for step in range(SUB):
        halo = wide - 1 - step
        values = current.astype(F32)
        centre = values[1:-1, 1:-1]
        spread = (
            values[2:, 1:-1] + values[:-2, 1:-1] + values[1:-1, 2:] + values[1:-1, :-2]
            - 4.0 * centre
        )
        smooth = (centre + KAPPA * spread).astype(BF)
        mixed = jnp.einsum(
            "hwc,cd->hwd", smooth, vert_inverse, preferred_element_type=F32
        ).astype(BF)
        if halo:
            rows = row_at - halo + jnp.arange(mixed.shape[0])
            cols = col_at - halo + jnp.arange(mixed.shape[1])
            inside = ((rows >= 0) & (rows < rows_all))[:, None] & (
                (cols >= 0) & (cols < cols_all)
            )[None, :]
            mixed = jnp.where(inside[:, :, None], mixed, jnp.zeros_like(mixed))
        current = mixed
    return current, told


def added(ref, at, block):
    ref[at] = (ref[at].astype(F32) + block.astype(F32)).astype(BF)


def contrib_kernel(
    blk, idx, atm, weight, narrow, extra,
    sums, near_sums, far, near, rest, q,
):
    total, size = sums.shape[0], sums.shape[1]

    @pl.loop(0, total // 8)
    def _(i):
        sums[pl.ds(i * 8, 8)] = jnp.zeros((8,) + sums.shape[1:], BF)

    pairs = weight.shape[0]
    for p in range(0, pairs, GROUP):
        blocks = [
            jnp.dot(weight[p + i], atm[blk[p + i]], preferred_element_type=F32).astype(BF)
            for i in range(GROUP)
        ]
        parts = [
            lax.dot_general(
                narrow[i % 2].astype(BF), blocks[i], (((1,), (1,)), ((), ())),
                preferred_element_type=F32,
            )
            for i in range(GROUP)
        ]
        for i in range(0, GROUP, 2):
            q[pl.ds((p + i) * FIELDS, 8)] = parts[i] + parts[i + 1]
        for i in range(GROUP):
            added(sums, idx[p + i], blocks[i])
    n_near, n_rest = near_sums.shape[0], rest.shape[0]
    n_slots = (far.shape[0] - q.shape[0] - extra.shape[0]) // size
    base = total - n_near - 2 * n_slots - n_rest
    for i in range(n_near):
        near_sums[i] = sums[base + i]
    base += n_near
    for i in range(n_slots):
        far[pl.ds(i * size, size)] = sums[base + i]
    base += n_slots
    for i in range(n_rest):
        rest[i] = sums[base + i]
    base += n_rest
    for i in range(n_slots):
        near[pl.ds(i * size, size)] = sums[base + i]
    for out in (far, near):
        out[pl.ds(n_slots * size, q.shape[0])] = q[...].astype(BF)
        out[pl.ds(n_slots * size + q.shape[0], extra.shape[0])] = extra[...]


def first_kernel(tab_mate, near_sums, far, near, same, other):
    size = near_sums.shape[1]
    blocks = near_sums.shape[0] // 2
    payload = same.shape[0] - blocks * size
    n_slots = (far.shape[0] - payload) // size
    cap = n_slots // 2
    low = tab_mate.shape[0] - n_slots
    told = far[pl.ds(far.shape[0] - 16, 16)].astype(F32)[10:11]
    lane = lax.broadcasted_iota(jnp.int32, told.shape, 1)
    for j, (out, source) in enumerate(((same, far), (other, near))):
        for b in range(blocks):
            out[pl.ds(b * size, size)] = near_sums[j * blocks + b]
        out[pl.ds(blocks * size, payload)] = source[pl.ds(n_slots * size, payload)]
        for r in range(cap):
            slot = j * cap + r
            far_at = jnp.sum(jnp.where(lane == slot, told, 0.0)).astype(jnp.int32)
            for at, held in ((far_at, far), (tab_mate[low + slot], near)):
                to = pl.multiple_of(lax.rem(at, blocks) * size, size)
                added(out, pl.ds(to, size), held[pl.ds(slot * size, size)])


def rest_kernel(tab_mate, sums, rest, *outs, cap, n_far):
    size = sums.shape[1]
    blocks = (outs[0].shape[0] - PAYLOAD) // size
    payload = PAYLOAD
    for m, out in enumerate(outs):
        for b in range(blocks):
            out[pl.ds(b * size, size)] = sums[m * blocks + b]
        out[pl.ds(blocks * size, payload)] = jnp.zeros((payload, out.shape[1]), BF)
        if m >= 2:
            for r in range(cap):
                slot = (m - 2) * cap + r
                to = pl.multiple_of(lax.rem(tab_mate[n_far + slot], blocks) * size, size)
                added(out, pl.ds(to, size), rest[slot])


def ocean_kernel(adv, state, wet, coupling, mine, swapped, out):
    size = out.shape[1]
    for b in range(out.shape[0]):
        rows = pl.ds(b * size, size)
        forcing = (mine[rows].astype(F32) + swapped[rows].astype(F32)).astype(BF)
        pushed = jnp.dot(forcing, coupling[...], preferred_element_type=F32)
        updated = (adv[b].astype(F32) + pushed).astype(BF).astype(F32)
        keep = wet[b].astype(F32) > 0.5
        out[b] = jnp.where(keep, updated, state[b].astype(F32)).astype(BF)


def picked(ids, message, sums):
    lanes = message.shape[1]
    rows = ids.shape[0]
    first = message.shape[0] - PAYLOAD
    tail = PAYLOAD - lanes
    id_rows = message[pl.ds(message.shape[0] - 16, 16)].astype(F32)
    row_f = lax.broadcasted_iota(jnp.int32, (rows, lanes), 0) % FIELDS
    lane = lax.broadcasted_iota(jnp.int32, (rows, lanes), 1)
    same_f = row_f == lane % FIELDS
    half = lanes // FIELDS
    match = ids == id_rows[8:9]
    match_t = (ids == id_rows[9:10])[:, :tail]
    is_adv = (lane < half) & same_f
    is_wet = (lane >= half) & (lane < half + half // FIELDS)

    def take(mask, block):
        return jnp.dot(
            jnp.where(mask, 1.0, 0.0).astype(BF), block, preferred_element_type=F32
        )

    low = message[pl.ds(first + lanes, tail)]
    pushed, adv, wet = sums
    return (
        pushed + take(match & same_f, message[pl.ds(first, lanes)]),
        adv + take(match_t & is_adv[:, :tail], low),
        wet + take(match_t & is_wet[:, :tail], low),
    )


def early_kernel(ids, both, *refs):
    local, messages, out = refs[:2], refs[2:-1], refs[-1]
    rows, lanes = ids.shape[0], out.shape[2]
    zero = jnp.zeros((rows, lanes), F32)
    mine = (zero,) * 3
    for message in local:
        mine = picked(ids[...], message, mine)
    for i in range(3):
        out[i, pl.ds(0, rows)] = mine[i]
        out[i, pl.ds(rows, rows)] = zero
    for message in messages:
        sums = picked(both[...], message, tuple(out[i] for i in range(3)))
        for i in range(3):
            out[i] = sums[i]


def late_kernel(both, early, *refs):
    messages, mine, mate = refs[:-2], refs[-2], refs[-1]
    sums = tuple(early[i] for i in range(3))
    for message in messages:
        sums = picked(both[...], message, sums)
    rows = mine.shape[1]
    for i in range(3):
        mine[i] = sums[i][:rows]
        mate[pl.ds(i * rows, rows)] = sums[i][rows:].astype(BF)


def reply_kernel(blk, mine, mate, weight, out, held, acc):
    pairs, lanes = weight.shape[0], weight.shape[2]
    rows = mine.shape[1]
    pushed, adv, wet = (
        mine[i] + mate[pl.ds(i * rows, rows)].astype(F32) for i in range(3)
    )
    held[...] = jnp.where(wet > 0.5, (adv + pushed).astype(BF).astype(F32), 0.0)
    acc[...] = jnp.zeros_like(acc)
    low_rows = lax.broadcasted_iota(jnp.int32, (8, lanes), 0) < FIELDS
    for j in range(0, pairs // 2, 4):
        parts = []
        for i in range(j, j + 4):
            surface = held[pl.ds(i * 8, 8)].astype(BF)
            parts.append(
                jnp.where(
                    low_rows,
                    jnp.dot(surface, weight[2 * i], preferred_element_type=F32),
                    0.0,
                )
            )
            parts.append(
                jnp.where(
                    low_rows,
                    0.0,
                    jnp.dot(surface, weight[2 * i + 1], preferred_element_type=F32),
                )
            )
        for i, part in enumerate(parts):
            acc[blk[2 * j + i]] += part
    for f in range(FIELDS):
        out[f] = acc[:, f, :] + acc[:, f + FIELDS, :]


def on_device(
    atm_state,
    vert_inverse,
    pair_block,
    pair_ocean,
    pair_weight,
    ocean_state,
    flux_coupling,
    ocean_mix,
    land_mask,
):
    height, breadth, channels = atm_state.shape
    blocks = ocean_state.shape[0]
    pairs = pair_block.shape[0]
    devices = lax.axis_size("col")
    cap = 2 * pairs // devices
    chips = devices // 2
    half = chips // 2
    me = lax.axis_index("col")
    chip, core = me // 2, me % 2
    onward = [(i, (i + 2 - 4 * (i % 2)) % devices) for i in range(devices)]
    mate = [(i, i ^ 1) for i in range(devices)]

    owner = pair_ocean // blocks
    local = pair_ocean - owner * blocks
    at = jnp.arange(pairs)
    rank = jnp.sum(
        ((owner[None, :] == owner[:, None]) & (at[None, :] < at[:, None])).astype(jnp.int32),
        axis=1,
    )
    offset = ((owner // 2 - chip) * (1 - 2 * core)) % chips
    other = (owner % 2) ^ core
    wide = 2 * blocks
    n_far = 2 * cap
    n_slots = n_far + 2 * cap * (half - 1)
    dense = half * wide
    back = chips - offset
    target = jnp.where(
        offset < half,
        offset * wide + other * blocks + local,
        jnp.where(
            offset == half,
            dense + other * cap + rank,
            dense + n_far + ((back - 1) * 2 + (1 - other)) * cap + rank,
        ),
    )
    value = jnp.where(
        offset == half,
        other * blocks + local,
        jnp.where(back == half - 1, 0, back * wide) + (1 - other) * blocks + local,
    )
    slot_at = dense + jnp.arange(n_slots)
    table = jnp.sum(
        jnp.where(target[:, None] == slot_at[None, :], value[:, None], 0), axis=0
    ).astype(jnp.int32)

    ocean_adv = jnp.einsum(
        "boc,cd->bod", ocean_state, ocean_mix, preferred_element_type=F32
    ).astype(BF)
    adv_rows = jnp.einsum(
        "cf,boc->bfo", ocean_mix[:, :FIELDS], ocean_state, preferred_element_type=F32
    ).astype(BF)
    lane = jnp.arange(breadth)
    width = blocks * FIELDS
    id_row = jnp.broadcast_to(pair_ocean[:, None], (pairs, FIELDS)).reshape(1, pairs * FIELDS)
    base_row = me * blocks + jnp.where(lane < width, lane // FIELDS, lane % width)
    extra = jnp.concatenate(
        [
            adv_rows.reshape(blocks * FIELDS, breadth),
            (land_mask == 1).astype(BF),
            id_row.astype(BF),
            jnp.minimum(base_row, 255)[None, :].astype(BF),
            jnp.pad(table, (0, breadth - n_slots))[None, :].astype(BF),
            jnp.zeros((5, breadth), BF),
        ],
        axis=0,
    )
    narrow = jnp.zeros((2, 8, channels), F32)
    narrow = narrow.at[0, :FIELDS].set(flux_coupling[:, :FIELDS].T.astype(F32))
    narrow = narrow.at[1, FIELDS:].set(flux_coupling[:, :FIELDS].T.astype(F32))

    wet = jnp.broadcast_to(
        (land_mask == 1).astype(BF)[:, :, None], (blocks, breadth, channels)
    )
    tall = tall_patch(atm_state)
    notes = jnp.concatenate(
        [table, pair_ocean, jnp.zeros((breadth - n_slots - pairs,), jnp.int32)]
    )
    current, told = substeps(tall, notes, vert_inverse)
    current, ocean_adv, wet = lax.optimization_barrier((current, ocean_adv, wet))
    theirs = told[n_slots:n_slots + pairs]
    table_mate = told[:n_slots]

    def blocks_of(n):
        return jax.ShapeDtypeStruct((n, breadth, channels), BF)

    def rows_of(n, dtype=BF):
        return jax.ShapeDtypeStruct((n, breadth), dtype)

    def column(ids):
        return jnp.broadcast_to(ids[:, None], (pairs, FIELDS)).reshape(pairs * FIELDS, 1)

    def cost(flops, mib):
        return pl.CostEstimate(
            flops=flops, bytes_accessed=mib * 1024 * 1024, transcendentals=0
        )

    n_rest = n_slots - 2 * n_far
    sums, near_sums, far, near, rest = pl.pallas_call(
        contrib_kernel,
        out_shape=(
            blocks_of(dense + n_slots),
            blocks_of(wide),
            rows_of(n_far * breadth + PAYLOAD),
            rows_of(n_far * breadth + PAYLOAD),
            blocks_of(n_rest),
        ),
        in_specs=[SM] * 2 + [VM] * 4,
        out_specs=(VM,) * 5,
        scratch_shapes=[pltpu.VMEM((pairs * FIELDS, breadth), F32)],
        compiler_params=params(4),
        cost_estimate=cost(2 * pairs * breadth * breadth * channels, 8),
    )(pair_block, target, current, pair_weight, narrow, extra)

    far_in = lax.ppermute(far, "col", onward)
    near_in = lax.ppermute(near, "col", mate)

    length = blocks * breadth + PAYLOAD
    held = pl.pallas_call(
        first_kernel,
        out_shape=(rows_of(length),) * 2,
        in_specs=[SM, VM, VM, VM],
        out_specs=(VM,) * 2,
        compiler_params=params(4),
        cost_estimate=cost(wide * breadth * channels, 2),
    )(table_mate, near_sums, far_in, near_in)
    held = list(held)

    rest, held[0] = lax.optimization_barrier((rest, held[0]))
    rest = lax.ppermute(rest, "col", mate)
    here = pl.pallas_call(
        lambda *refs: rest_kernel(*refs, cap=cap, n_far=n_far),
        out_shape=(rows_of(length),) * (2 * (half - 1)),
        in_specs=[SM, VM, VM],
        out_specs=(VM,) * (2 * (half - 1)),
        compiler_params=params(4),
        cost_estimate=cost(n_rest * breadth * channels, 4),
    )(table_mate, sums, rest)

    messages = []
    for hop in range(half - 1, 0, -1):
        for j in (1, 0):
            came = lax.ppermute(held[j], "col", onward)
            total = came.astype(F32) + here[(hop - 1) * 2 + j].astype(F32)
            held[j] = total.astype(BF)
            messages.append(held[j])

    ids = column(pair_ocean.astype(F32))
    both = jnp.concatenate([ids, column(theirs.astype(F32))], axis=0)
    early = pl.pallas_call(
        early_kernel,
        out_shape=jax.ShapeDtypeStruct((3, 2 * pairs * FIELDS, breadth), F32),
        in_specs=[VM] * (2 + 3 + len(messages) - 2),
        out_specs=VM,
        compiler_params=params(4),
        cost_estimate=cost(len(messages) * 6 * 128 ** 3, 2),
    )(ids, both, near, near_in, far_in, *messages[:-2])
    mine, for_mate = pl.pallas_call(
        late_kernel,
        out_shape=(
            jax.ShapeDtypeStruct((3, pairs * FIELDS, breadth), F32),
            rows_of(3 * pairs * FIELDS),
        ),
        in_specs=[VM] * 4,
        out_specs=(VM,) * 2,
        compiler_params=params(4),
        cost_estimate=cost(12 * 128 ** 3, 1),
    )(both, early, *messages[-2:])

    swapped = lax.ppermute(held[1], "col", mate)
    from_mate = lax.ppermute(for_mate, "col", mate)
    ocean_next = pl.pallas_call(
        ocean_kernel,
        out_shape=blocks_of(blocks),
        in_specs=[VM] * 6,
        out_specs=VM,
        compiler_params=params(4),
        cost_estimate=cost(2 * blocks * breadth * channels * channels, 2),
    )(ocean_adv, ocean_state, wet, flux_coupling, held[0], swapped)

    surface_on_atm = pl.pallas_call(
        reply_kernel,
        out_shape=jax.ShapeDtypeStruct((FIELDS, height, breadth), F32),
        in_specs=[SM, VM, VM, VM],
        out_specs=VM,
        scratch_shapes=[
            pltpu.VMEM((pairs * FIELDS, breadth), F32),
            pltpu.VMEM((height, 8, breadth), F32),
        ],
        compiler_params=params(4),
        cost_estimate=cost(2 * pairs * 8 * 128 ** 2, 2),
    )(pair_block, mine, from_mate, pair_weight)
    return (current, ocean_next, surface_on_atm)


def solution(mesh):
    rows = P(("sec", "row", "col"))
    return jax.shard_map(
        on_device,
        mesh=mesh,
        in_specs=(
            P(("sec", "row"), "col", None),
            P(),
            rows,
            rows,
            P(("sec", "row", "col"), None, None),
            P(("sec", "row", "col"), None, None),
            P(),
            P(),
            P(("sec", "row", "col"), None),
        ),
        out_specs=(
            P(("sec", "row"), "col", None),
            P(("sec", "row", "col"), None, None),
            P(None, ("sec", "row"), "col"),
        ),
        check_vma=False,
    )
```

time: 190 us -> 145 us (0.76)
  the two profiles are of different devices: /device:TPU:31 before, /device:TPU:33 now
where the time goes in v2:
time: 145 us; the launch traced here: 144 us
  starting transfers between devices  105 us (72%)
  Pallas kernels  10.3 us (7%)
  waiting for transfers between devices  9.67 us (7%)
  local copies, waits for them, and re-layouts  8.56 us (6%)
  other arithmetic  4.28 us (3%)
  matrix products  4.18 us (3%)
    ppermute x14, starting transfers between devices, on_device(): came = lax.ppermute(held[j], 'col', onward)  55 us
    ppermute x1, starting transfers between devices, on_device(): far_in = lax.ppermute(far, 'col', onward)  16.2 us
    ppermute x1, starting transfers between devices, on_device(): swapped = lax.ppermute(held[1], 'col', mate)  10.1 us
    unnamed x26, local copies, waits for them, and re-layouts  7.37 us
    ppermute x2, starting transfers between devices, edges(): return (lax.ppermute(last, axis, up), lax.ppermute(first, axis, down))  6.79 us
    ppermute x2, waiting for transfers between devices, edges(): return (lax.ppermute(last, axis, up), lax.ppermute(first, axis, down))  5.78 us
    ppermute x1, starting transfers between devices, on_device(): rest = lax.ppermute(rest, 'col', mate)  4.36 us
    ppermute x1, starting transfers between devices, substeps(): lax.ppermute(jnp.concatenate([tall[:, :wide], line], axis=0), 'col', down)  4.01 us
  transfers between devices with their start and end apart: 23, of which 6 were waited for; matrix products, arithmetic and copies ran while one was open for 3% of the time, Pallas kernels for 3%

profile of v2, /device:TPU:33, one launch (start us, length us, event | category | flops | bytes accessed | tf_op | source)
XLA Modules:
  0.0 143.7 jit_solution(16601609868062304787)
XLA Ops:
  0.7 1.7 %copy.31 = bf16[24,128,128]{2,0,1:T(8,128)(2,1)S(1)} copy(bf16[24,128,128]{2,1,0:T(8,128)(2,1)} %param.13) | data formatting | bytes 1572864 | tf_op args[0]
  2.5 4.5 %collective-permute-start.1 = (bf16[3,128,128]{2,0,1:T(4,128)(2,1)S(1)}, bf16[3,128,128]{2,0,1:T(4,128)(2,1)S(1)}, u32[]{:S(2)}, u32[]{:S(2)}) collective-permute-start(bf16[3,128,128]{2,0,1:T(4,128)(2,1)S(1)} %get-tuple-element.89), channel_id=1, source_target_pairs={{32,0},{64,32},{96,64},{128,96},{160,128},{192,160},{224,192},{256... | collective-permute-start | bytes 294920 | tf_op jit(solution)/shard_map/ppermute | solution.py:30
  7.0 2.2 %collective-permute-start = (bf16[3,128,128]{2,0,1:T(4,128)(2,1)S(1)}, bf16[3,128,128]{2,0,1:T(4,128)(2,1)S(1)}, u32[]{:S(2)}, u32[]{:S(2)}) collective-permute-start(bf16[3,128,128]{2,0,1:T(4,128)(2,1)S(1)} %get-tuple-element.88), channel_id=1, source_target_pairs={{0,32},{32,64},{64,96},{96,128},{128,160},{160,192},{192,224},{224... | collective-permute-start | bytes 294920 | tf_op jit(solution)/shard_map/ppermute | solution.py:30
  10.6 5.8 %collective-permute-done = bf16[3,128,128]{2,0,1:T(4,128)(2,1)S(1)} collective-permute-done((bf16[3,128,128]{2,0,1:T(4,128)(2,1)S(1)}, bf16[3,128,128]{2,0,1:T(4,128)(2,1)S(1)}, u32[]{:S(2)}, u32[]{:S(2)}) %collective-permute-start) | collective-permute-done | bytes 98336 | tf_op jit(solution)/shard_map/ppermute | solution.py:30
  16.4 4.0 %collective-permute-start.3 = (bf16[31,3,128]{2,0,1:T(8,128)(2,1)S(1)}, bf16[31,3,128]{2,0,1:T(8,128)(2,1)S(1)}, u32[]{:S(2)}, u32[]{:S(2)}) collective-permute-start(bf16[31,3,128]{2,0,1:T(8,128)(2,1)S(1)} %get-tuple-element.87), channel_id=1, source_target_pairs={{1,0},{2,1},{3,2},{4,3},{5,4},{6,5},{7,6},{8,7},{9,8},{10,9},{11,1... | collective-permute-start | bytes 71432 | tf_op jit(solution)/shard_map/ppermute | solution.py:46
  20.4 3.9 %collective-permute-start.2 = (bf16[31,3,128]{2,0,1:T(8,128)(2,1)S(1)}, bf16[31,3,128]{2,0,1:T(8,128)(2,1)S(1)}, u32[]{:S(2)}, u32[]{:S(2)}) collective-permute-start(bf16[31,3,128]{2,0,1:T(8,128)(2,1)S(1)} %get-tuple-element.86), channel_id=1, source_target_pairs={{0,1},{1,2},{2,3},{3,4},{4,5},{5,6},{6,7},{7,8},{8,9},{9,10},{10,1... | collective-permute-start | bytes 71432 | tf_op jit(solution)/shard_map/ppermute | solution.py:45
  26.6 1.6 %fusion.13 = f32[28,132,128]{2,1,0:T(8,128)S(1)} fusion(bf16[28,132,128]{2,0,1:T(8,128)(2,1)S(1)} %fusion.3, pred[28,132]{1,0:T(8,128)(4,1)S(1)} %broadcast_and_fusion, bf16[128,128]{1,0:T(8,128)(2,1)S(1)} %copy-done), kind=kOutput, calls=%fused_computation.25 | convolution fusion | flops 122529792 | bytes 2874992 | tf_op jit(solution)/shard_map/hwc,cd->hwd/dot_general | solution.py:63
  28.3 1.2 fusion.15
  30.7 4.0 %shard_map.112 = (bf16[160,128,128]{2,1,0:T(8,128)(2,1)S(1)}, bf16[16,128,128]{2,1,0:T(8,128)(2,1)S(1)}, bf16[688,128]{1,0:T(8,128)(2,1)S(1)}, bf16[688,128]{1,0:T(8,128)(2,1)S(1)}, bf16[24,128,128]{2,1,0:T(8,128)(2,1)}) custom-call(s32[32]{0:T(128)S(1)} %copy-done.7, s32[32]{0:T(128)S(1)} %get-tuple-element.83.idx, ...), custom_call_target="tpu_custom_call" | custom-call | flops 134217728 | bytes 8388608 | tf_op jit(solution)/shard_map/pallas_call | solution.py:371
  34.7 2.3 %copy-done.1 = bf16[160,128,128]{2,1,0:T(8,128)(2,1)} copy-done((bf16[160,128,128]{2,1,0:T(8,128)(2,1)}, bf16[160,128,128]{2,1,0:T(8,128)(2,1)S(1)}, u32[]{:S(2)}) %copy-start.1) | copy-done | bytes 5242904
  37.1 16.2 %collective-permute-start.4 = (bf16[688,128]{1,0:T(8,128)(2,1)S(1)}, bf16[688,128]{1,0:T(8,128)(2,1)S(1)}, u32[]{:S(2)}, u32[]{:S(2)}) collective-permute-start(bf16[688,128]{1,0:T(8,128)(2,1)S(1)} %get-tuple-element.60), channel_id=1, source_target_pairs={{0,2},{1,31},{2,4},{3,1},{4,6},{5,3},{6,8},{7,5},{8,10},{9,7},{10,... | collective-permute-start | bytes 528392 | tf_op jit(solution)/shard_map/ppermute | solution.py:387
  53.3 1.9 %collective-permute-start.5 = (bf16[688,128]{1,0:T(8,128)(2,1)S(1)}, bf16[688,128]{1,0:T(8,128)(2,1)S(1)}, u32[]{:S(2)}, u32[]{:S(2)}) collective-permute-start(bf16[688,128]{1,0:T(8,128)(2,1)S(1)} %get-tuple-element.61.refs_0_), channel_id=1, source_target_pairs={{0,1},{1,0},{2,3},{3,2},{4,5},{5,4},{6,7},{7,6},{8,9},{9,8},{10,11... | collective-permute-start | bytes 528392 | tf_op jit(solution)/shard_map/ppermute | solution.py:388
  56.6 1.5 %shard_map.113 = (bf16[1200,128]{1,0:T(8,128)(2,1)S(1)}, bf16[1200,128]{1,0:T(8,128)(2,1)}) custom-call(s32[32]{0:T(128)S(1)} %get-tuple-element.94.tab_mate.refs_0_, bf16[16,128,128]{2,1,0:T(8,128)(2,1)S(1)} %get-tuple-element.59.near_sums, bf16[688,128]{1,0:T(8,128)(2,1)S(1)} %collective-permute-done.4.far.refs_2_, ...), custom_call_target="tpu_custom_call" | custom-call | flops 262144 | bytes 2097152 | tf_op jit(solution)/shard_map/pallas_call | solution.py:391
  58.7 4.4 %collective-permute-start.7 = (bf16[24,128,128]{2,1,0:T(8,128)(2,1)}, bf16[24,128,128]{2,1,0:T(8,128)(2,1)S(1)}, u32[]{:S(2)}, u32[]{:S(2)}) collective-permute-start(bf16[24,128,128]{2,1,0:T(8,128)(2,1)} %get-tuple-element.65), channel_id=1, source_target_pairs={{0,1},{1,0},{2,3},{3,2},{4,5},{5,4},{6,7},{7,6},{8,9},{9,8},{10,11... | collective-permute-start | bytes 2359304 | tf_op jit(solution)/shard_map/ppermute | solution.py:402
  63.1 3.6 %collective-permute-start.14 = (bf16[1200,128]{1,0:T(8,128)(2,1)}, bf16[1200,128]{1,0:T(8,128)(2,1)}, u32[]{:S(2)}, u32[]{:S(2)}) collective-permute-start(bf16[1200,128]{1,0:T(8,128)(2,1)} %get-tuple-element.73), channel_id=1, source_target_pairs={{0,2},{1,31},{2,4},{3,1},{4,6},{5,3},{6,8},{7,5},{8,10},{9,7},{10,... | collective-permute-start | bytes 921608 | tf_op jit(solution)/shard_map/ppermute | solution.py:415
  67.4 2.2 %collective-permute-start.6 = (bf16[1200,128]{1,0:T(8,128)(2,1)}, bf16[1200,128]{1,0:T(8,128)(2,1)S(1)}, u32[]{:S(2)}, u32[]{:S(2)}) collective-permute-start(bf16[1200,128]{1,0:T(8,128)(2,1)} %copy-done.8), channel_id=1, source_target_pairs={{0,2},{1,31},{2,4},{3,1},{4,6},{5,3},{6,8},{7,5},{8,10},{9,7},{10,... | collective-permute-start | bytes 921608 | tf_op jit(solution)/shard_map/ppermute | solution.py:415
  69.6 2.5 %copy-done.2 = bf16[160,128,128]{2,1,0:T(8,128)(2,1)S(1)} copy-done((bf16[160,128,128]{2,1,0:T(8,128)(2,1)S(1)}, bf16[160,128,128]{2,1,0:T(8,128)(2,1)}, u32[]{:S(2)}) %copy-start.2) | copy-done | bytes 5242904
  74.1 2.8 %collective-permute-start.15 = (bf16[1200,128]{1,0:T(8,128)(2,1)S(1)}, bf16[1200,128]{1,0:T(8,128)(2,1)S(1)}, u32[]{:S(2)}, u32[]{:S(2)}) collective-permute-start(bf16[1200,128]{1,0:T(8,128)(2,1)S(1)} %add_convert_fusion.6.refs_3_), channel_id=1, source_target_pairs={{0,2},{1,31},{2,4},{3,1},{4,6},{5,3},{6,8},{7,5},{8,10},{9,7},{10,... | collective-permute-start | bytes 921608 | tf_op jit(solution)/shard_map/ppermute | solution.py:415
  77.0 4.0 %collective-permute-start.8 = (bf16[1200,128]{1,0:T(8,128)(2,1)S(1)}, bf16[1200,128]{1,0:T(8,128)(2,1)S(1)}, u32[]{:S(2)}, u32[]{:S(2)}) collective-permute-start(bf16[1200,128]{1,0:T(8,128)(2,1)S(1)} %add_convert_fusion.13.refs_4_), channel_id=1, source_target_pairs={{0,2},{1,31},{2,4},{3,1},{4,6},{5,3},{6,8},{7,5},{8,10},{9,7},{10,... | collective-permute-start | bytes 921608 | tf_op jit(solution)/shard_map/ppermute | solution.py:415
  82.1 3.7 %collective-permute-start.16 = (bf16[1200,128]{1,0:T(8,128)(2,1)S(1)}, bf16[1200,128]{1,0:T(8,128)(2,1)S(1)}, u32[]{:S(2)}, u32[]{:S(2)}) collective-permute-start(bf16[1200,128]{1,0:T(8,128)(2,1)S(1)} %add_convert_fusion.5.refs_5_), channel_id=1, source_target_pairs={{0,2},{1,31},{2,4},{3,1},{4,6},{5,3},{6,8},{7,5},{8,10},{9,7},{10,... | collective-permute-start | bytes 921608 | tf_op jit(solution)/shard_map/ppermute | solution.py:415
  85.9 4.0 %collective-permute-start.9 = (bf16[1200,128]{1,0:T(8,128)(2,1)S(1)}, bf16[1200,128]{1,0:T(8,128)(2,1)S(1)}, u32[]{:S(2)}, u32[]{:S(2)}) collective-permute-start(bf16[1200,128]{1,0:T(8,128)(2,1)S(1)} %add_convert_fusion.12.refs_6_), channel_id=1, source_target_pairs={{0,2},{1,31},{2,4},{3,1},{4,6},{5,3},{6,8},{7,5},{8,10},{9,7},{10,... | collective-permute-start | bytes 921608 | tf_op jit(solution)/shard_map/ppermute | solution.py:415
  90.0 4.7 %collective-permute-start.17 = (bf16[1200,128]{1,0:T(8,128)(2,1)S(1)}, bf16[1200,128]{1,0:T(8,128)(2,1)S(1)}, u32[]{:S(2)}, u32[]{:S(2)}) collective-permute-start(bf16[1200,128]{1,0:T(8,128)(2,1)S(1)} %add_convert_fusion.4.refs_7_), channel_id=1, source_target_pairs={{0,2},{1,31},{2,4},{3,1},{4,6},{5,3},{6,8},{7,5},{8,10},{9,7},{10,... | collective-permute-start | bytes 921608 | tf_op jit(solution)/shard_map/ppermute | solution.py:415
  94.8 4.0 %collective-permute-start.10 = (bf16[1200,128]{1,0:T(8,128)(2,1)S(1)}, bf16[1200,128]{1,0:T(8,128)(2,1)S(1)}, u32[]{:S(2)}, u32[]{:S(2)}) collective-permute-start(bf16[1200,128]{1,0:T(8,128)(2,1)S(1)} %add_convert_fusion.11.refs_8_), channel_id=1, source_target_pairs={{0,2},{1,31},{2,4},{3,1},{4,6},{5,3},{6,8},{7,5},{8,10},{9,7},{10,... | collective-permute-start | bytes 921608 | tf_op jit(solution)/shard_map/ppermute | solution.py:415
  98.9 4.7 %collective-permute-start.18 = (bf16[1200,128]{1,0:T(8,128)(2,1)S(1)}, bf16[1200,128]{1,0:T(8,128)(2,1)S(1)}, u32[]{:S(2)}, u32[]{:S(2)}) collective-permute-start(bf16[1200,128]{1,0:T(8,128)(2,1)S(1)} %add_convert_fusion.3.refs_9_), channel_id=1, source_target_pairs={{0,2},{1,31},{2,4},{3,1},{4,6},{5,3},{6,8},{7,5},{8,10},{9,7},{10,... | collective-permute-start | bytes 921608 | tf_op jit(solution)/shard_map/ppermute | solution.py:415
  103.7 4.0 %collective-permute-start.11 = (bf16[1200,128]{1,0:T(8,128)(2,1)S(1)}, bf16[1200,128]{1,0:T(8,128)(2,1)S(1)}, u32[]{:S(2)}, u32[]{:S(2)}) collective-permute-start(bf16[1200,128]{1,0:T(8,128)(2,1)S(1)} %add_convert_fusion.10.refs_10_), channel_id=1, source_target_pairs={{0,2},{1,31},{2,4},{3,1},{4,6},{5,3},{6,8},{7,5},{8,10},{9,7},{10,... | collective-permute-start | bytes 921608 | tf_op jit(solution)/shard_map/ppermute | solution.py:415
  107.8 4.7 %collective-permute-start.19 = (bf16[1200,128]{1,0:T(8,128)(2,1)S(1)}, bf16[1200,128]{1,0:T(8,128)(2,1)S(1)}, u32[]{:S(2)}, u32[]{:S(2)}) collective-permute-start(bf16[1200,128]{1,0:T(8,128)(2,1)S(1)} %add_convert_fusion.2.refs_11_), channel_id=1, source_target_pairs={{0,2},{1,31},{2,4},{3,1},{4,6},{5,3},{6,8},{7,5},{8,10},{9,7},{10,... | collective-permute-start | bytes 921608 | tf_op jit(solution)/shard_map/ppermute | solution.py:415
  112.6 4.0 %collective-permute-start.12 = (bf16[1200,128]{1,0:T(8,128)(2,1)S(1)}, bf16[1200,128]{1,0:T(8,128)(2,1)S(1)}, u32[]{:S(2)}, u32[]{:S(2)}) collective-permute-start(bf16[1200,128]{1,0:T(8,128)(2,1)S(1)} %add_convert_fusion.9.refs_12_), channel_id=1, source_target_pairs={{0,2},{1,31},{2,4},{3,1},{4,6},{5,3},{6,8},{7,5},{8,10},{9,7},{10,... | collective-permute-start | bytes 921608 | tf_op jit(solution)/shard_map/ppermute | solution.py:415
  116.7 4.7 %collective-permute-start.20 = (bf16[1200,128]{1,0:T(8,128)(2,1)S(1)}, bf16[1200,128]{1,0:T(8,128)(2,1)S(1)}, u32[]{:S(2)}, u32[]{:S(2)}) collective-permute-start(bf16[1200,128]{1,0:T(8,128)(2,1)S(1)} %add_convert_fusion.1.refs_13_), channel_id=1, source_target_pairs={{0,2},{1,31},{2,4},{3,1},{4,6},{5,3},{6,8},{7,5},{8,10},{9,7},{10,... | collective-permute-start | bytes 921608 | tf_op jit(solution)/shard_map/ppermute | solution.py:415
  121.5 4.0 %collective-permute-start.13 = (bf16[1200,128]{1,0:T(8,128)(2,1)S(1)}, bf16[1200,128]{1,0:T(8,128)(2,1)S(1)}, u32[]{:S(2)}, u32[]{:S(2)}) collective-permute-start(bf16[1200,128]{1,0:T(8,128)(2,1)S(1)} %add_convert_fusion.8.refs_14_), channel_id=1, source_target_pairs={{0,2},{1,31},{2,4},{3,1},{4,6},{5,3},{6,8},{7,5},{8,10},{9,7},{10,... | collective-permute-start | bytes 921608 | tf_op jit(solution)/shard_map/ppermute | solution.py:415
  126.6 10.1 %collective-permute-start.21 = (bf16[1200,128]{1,0:T(8,128)(2,1)S(1)}, bf16[1200,128]{1,0:T(8,128)(2,1)S(1)}, u32[]{:S(2)}, u32[]{:S(2)}) collective-permute-start(bf16[1200,128]{1,0:T(8,128)(2,1)S(1)} %add_convert_fusion.refs_0_), channel_id=1, source_target_pairs={{0,1},{1,0},{2,3},{3,2},{4,5},{5,4},{6,7},{7,6},{8,9},{9,8},{10,11... | collective-permute-start | bytes 921608 | tf_op jit(solution)/shard_map/ppermute | solution.py:442
  137.1 3.2 %collective-permute-start.22 = (bf16[384,128]{1,0:T(8,128)(2,1)S(1)}, bf16[384,128]{1,0:T(8,128)(2,1)S(1)}, u32[]{:S(2)}, u32[]{:S(2)}) collective-permute-start(bf16[384,128]{1,0:T(8,128)(2,1)S(1)} %get-tuple-element.82), channel_id=1, source_target_pairs={{0,1},{1,0},{2,3},{3,2},{4,5},{5,4},{6,7},{7,6},{8,9},{9,8},{10,11... | collective-permute-start | bytes 294920 | tf_op jit(solution)/shard_map/ppermute | solution.py:443
  141.2 1.6 %shard_map.118 = f32[4,24,128]{2,1,0:T(8,128)} custom-call(s32[32]{0:T(128)S(1)} %copy-done.7, f32[3,128,128]{2,1,0:T(8,128)S(1)} %get-tuple-element.81.mine, bf16[384,128]{1,0:T(8,128)(2,1)S(1)} %collective-permute-done.22.mate, bf16[32,128,128]{2,1,0:T(8,128)(2,1)S(1)} %copy-done.3), custom_call_target="tpu_custom_call" | custom-call | flops 8388608 | bytes 2097152 | tf_op jit(solution)/shard_map/pallas_call | solution.py:453
  (104 shorter events, 14.8 us)
Async XLA Ops:
  0.6 26.0 %copy-start = (bf16[128,128]{1,0:T(8,128)(2,1)S(1)}, bf16[128,128]{1,0:T(8,128)(2,1)}, u32[]{:S(2)}) copy-start(bf16[128,128]{1,0:T(8,128)(2,1)} %param.14) | copy-start | bytes 98308
  0.6 8.7 %copy-start.4 = (bf16[8,128,128]{2,1,0:T(8,128)(2,1)S(1)}, bf16[8,128,128]{2,1,0:T(8,128)(2,1)}, u32[]{:S(2)}) copy-start(bf16[8,128,128]{2,1,0:T(8,128)(2,1)} %state.1) | copy-start | bytes 786436
  0.7 8.7 %copy-start.9 = (bf16[128,128]{1,0:T(8,128)(2,1)S(1)}, bf16[128,128]{1,0:T(8,128)(2,1)}, u32[]{:S(2)}) copy-start(bf16[128,128]{1,0:T(8,128)(2,1)} %param.20) | copy-start | bytes 98308
  0.7 9.1 %copy-start.11 = (s32[32]{0:T(128)S(1)}, s32[32]{0:T(128)}, u32[]{:S(2)}) copy-start(s32[32]{0:T(128)} %param.16) | copy-start | bytes 388
  0.7 9.5 %copy-start.10 = (s32[8,128]{1,0:T(8,128)S(1)}, s32[8,128]{1,0:T(8,128)}, u32[]{:S(2)}) copy-start(s32[8,128]{1,0:T(8,128)} %param.21) | copy-start | bytes 12292
  0.7 9.5 %copy-start.6 = (bf16[128,128]{1,0:T(8,128)(2,1)S(1)}, bf16[128,128]{1,0:T(8,128)(2,1)}, u32[]{:S(2)}) copy-start(bf16[128,128]{1,0:T(8,128)(2,1)} %coupling.1) | copy-start | bytes 98308
  2.5 8.1 %collective-permute-start.1 = (bf16[3,128,128]{2,0,1:T(4,128)(2,1)S(1)}, bf16[3,128,128]{2,0,1:T(4,128)(2,1)S(1)}, u32[]{:S(2)}, u32[]{:S(2)}) collective-permute-start(bf16[3,128,128]{2,0,1:T(4,128)(2,1)S(1)} %get-tuple-element.89), channel_id=1, source_target_pairs={{32,0},{64,32},{96,64},{128,96},{160,128},{192,160},{224,192},{256... | collective-permute-start | bytes 294920 | tf_op jit(solution)/shard_map/ppermute | solution.py:30
  7.0 9.3 %collective-permute-start = (bf16[3,128,128]{2,0,1:T(4,128)(2,1)S(1)}, bf16[3,128,128]{2,0,1:T(4,128)(2,1)S(1)}, u32[]{:S(2)}, u32[]{:S(2)}) collective-permute-start(bf16[3,128,128]{2,0,1:T(4,128)(2,1)S(1)} %get-tuple-element.88), channel_id=1, source_target_pairs={{0,32},{32,64},{64,96},{96,128},{128,160},{160,192},{192,224},{224... | collective-permute-start | bytes 294920 | tf_op jit(solution)/shard_map/ppermute | solution.py:30
  16.4 8.2 %collective-permute-start.3 = (bf16[31,3,128]{2,0,1:T(8,128)(2,1)S(1)}, bf16[31,3,128]{2,0,1:T(8,128)(2,1)S(1)}, u32[]{:S(2)}, u32[]{:S(2)}) collective-permute-start(bf16[31,3,128]{2,0,1:T(8,128)(2,1)S(1)} %get-tuple-element.87), channel_id=1, source_target_pairs={{1,0},{2,1},{3,2},{4,3},{5,4},{6,5},{7,6},{8,7},{9,8},{10,9},{11,1... | collective-permute-start | bytes 71432 | tf_op jit(solution)/shard_map/ppermute | solution.py:46
  20.4 4.8 %collective-permute-start.2 = (bf16[31,3,128]{2,0,1:T(8,128)(2,1)S(1)}, bf16[31,3,128]{2,0,1:T(8,128)(2,1)S(1)}, u32[]{:S(2)}, u32[]{:S(2)}) collective-permute-start(bf16[31,3,128]{2,0,1:T(8,128)(2,1)S(1)} %get-tuple-element.86), channel_id=1, source_target_pairs={{0,1},{1,2},{2,3},{3,4},{4,5},{5,6},{6,7},{7,8},{8,9},{9,10},{10,1... | collective-permute-start | bytes 71432 | tf_op jit(solution)/shard_map/ppermute | solution.py:45
  30.5 28.3 %copy-start.5 = (bf16[24,128,128]{2,1,0:T(8,128)(2,1)}, bf16[24,128,128]{2,1,0:T(8,128)(2,1)S(1)}, u32[]{:S(2)}) copy-start(bf16[24,128,128]{2,1,0:T(8,128)(2,1)S(1)} %convolution_convert_fusion.2.atm) | copy-start | bytes 2359300
  34.7 2.3 %copy-start.1 = (bf16[160,128,128]{2,1,0:T(8,128)(2,1)}, bf16[160,128,128]{2,1,0:T(8,128)(2,1)S(1)}, u32[]{:S(2)}) copy-start(bf16[160,128,128]{2,1,0:T(8,128)(2,1)S(1)} %get-tuple-element.64.refs_1_) | copy-start | bytes 15728644
  37.1 18.6 %collective-permute-start.4 = (bf16[688,128]{1,0:T(8,128)(2,1)S(1)}, bf16[688,128]{1,0:T(8,128)(2,1)S(1)}, u32[]{:S(2)}, u32[]{:S(2)}) collective-permute-start(bf16[688,128]{1,0:T(8,128)(2,1)S(1)} %get-tuple-element.60), channel_id=1, source_target_pairs={{0,2},{1,31},{2,4},{3,1},{4,6},{5,3},{6,8},{7,5},{8,10},{9,7},{10,... | collective-permute-start | bytes 528392 | tf_op jit(solution)/shard_map/ppermute | solution.py:387
  53.3 3.3 %collective-permute-start.5 = (bf16[688,128]{1,0:T(8,128)(2,1)S(1)}, bf16[688,128]{1,0:T(8,128)(2,1)S(1)}, u32[]{:S(2)}, u32[]{:S(2)}) collective-permute-start(bf16[688,128]{1,0:T(8,128)(2,1)S(1)} %get-tuple-element.61.refs_0_), channel_id=1, source_target_pairs={{0,1},{1,0},{2,3},{3,2},{4,5},{5,4},{6,7},{7,6},{8,9},{9,8},{10,11... | collective-permute-start | bytes 528392 | tf_op jit(solution)/shard_map/ppermute | solution.py:388
  58.7 10.8 %collective-permute-start.7 = (bf16[24,128,128]{2,1,0:T(8,128)(2,1)}, bf16[24,128,128]{2,1,0:T(8,128)(2,1)S(1)}, u32[]{:S(2)}, u32[]{:S(2)}) collective-permute-start(bf16[24,128,128]{2,1,0:T(8,128)(2,1)} %get-tuple-element.65), channel_id=1, source_target_pairs={{0,1},{1,0},{2,3},{3,2},{4,5},{5,4},{6,7},{7,6},{8,9},{9,8},{10,11... | collective-permute-start | bytes 2359304 | tf_op jit(solution)/shard_map/ppermute | solution.py:402
  63.1 9.9 %collective-permute-start.14 = (bf16[1200,128]{1,0:T(8,128)(2,1)}, bf16[1200,128]{1,0:T(8,128)(2,1)}, u32[]{:S(2)}, u32[]{:S(2)}) collective-permute-start(bf16[1200,128]{1,0:T(8,128)(2,1)} %get-tuple-element.73), channel_id=1, source_target_pairs={{0,2},{1,31},{2,4},{3,1},{4,6},{5,3},{6,8},{7,5},{8,10},{9,7},{10,... | collective-permute-start | bytes 921608 | tf_op jit(solution)/shard_map/ppermute | solution.py:415
  67.4 9.5 %collective-permute-start.6 = (bf16[1200,128]{1,0:T(8,128)(2,1)}, bf16[1200,128]{1,0:T(8,128)(2,1)S(1)}, u32[]{:S(2)}, u32[]{:S(2)}) collective-permute-start(bf16[1200,128]{1,0:T(8,128)(2,1)} %copy-done.8), channel_id=1, source_target_pairs={{0,2},{1,31},{2,4},{3,1},{4,6},{5,3},{6,8},{7,5},{8,10},{9,7},{10,... | collective-permute-start | bytes 921608 | tf_op jit(solution)/shard_map/ppermute | solution.py:415
  69.6 2.5 %copy-start.2 = (bf16[160,128,128]{2,1,0:T(8,128)(2,1)S(1)}, bf16[160,128,128]{2,1,0:T(8,128)(2,1)}, u32[]{:S(2)}) copy-start(bf16[160,128,128]{2,1,0:T(8,128)(2,1)} %copy-done.1) | copy-start | bytes 15728644
  74.1 7.9 %collective-permute-start.15 = (bf16[1200,128]{1,0:T(8,128)(2,1)S(1)}, bf16[1200,128]{1,0:T(8,128)(2,1)S(1)}, u32[]{:S(2)}, u32[]{:S(2)}) collective-permute-start(bf16[1200,128]{1,0:T(8,128)(2,1)S(1)} %add_convert_fusion.6.refs_3_), channel_id=1, source_target_pairs={{0,2},{1,31},{2,4},{3,1},{4,6},{5,3},{6,8},{7,5},{8,10},{9,7},{10,... | collective-permute-start | bytes 921608 | tf_op jit(solution)/shard_map/ppermute | solution.py:415
  77.0 8.8 %collective-permute-start.8 = (bf16[1200,128]{1,0:T(8,128)(2,1)S(1)}, bf16[1200,128]{1,0:T(8,128)(2,1)S(1)}, u32[]{:S(2)}, u32[]{:S(2)}) collective-permute-start(bf16[1200,128]{1,0:T(8,128)(2,1)S(1)} %add_convert_fusion.13.refs_4_), channel_id=1, source_target_pairs={{0,2},{1,31},{2,4},{3,1},{4,6},{5,3},{6,8},{7,5},{8,10},{9,7},{10,... | collective-permute-start | bytes 921608 | tf_op jit(solution)/shard_map/ppermute | solution.py:415
  82.1 7.8 %collective-permute-start.16 = (bf16[1200,128]{1,0:T(8,128)(2,1)S(1)}, bf16[1200,128]{1,0:T(8,128)(2,1)S(1)}, u32[]{:S(2)}, u32[]{:S(2)}) collective-permute-start(bf16[1200,128]{1,0:T(8,128)(2,1)S(1)} %add_convert_fusion.5.refs_5_), channel_id=1, source_target_pairs={{0,2},{1,31},{2,4},{3,1},{4,6},{5,3},{6,8},{7,5},{8,10},{9,7},{10,... | collective-permute-start | bytes 921608 | tf_op jit(solution)/shard_map/ppermute | solution.py:415
  85.9 8.8 %collective-permute-start.9 = (bf16[1200,128]{1,0:T(8,128)(2,1)S(1)}, bf16[1200,128]{1,0:T(8,128)(2,1)S(1)}, u32[]{:S(2)}, u32[]{:S(2)}) collective-permute-start(bf16[1200,128]{1,0:T(8,128)(2,1)S(1)} %add_convert_fusion.12.refs_6_), channel_id=1, source_target_pairs={{0,2},{1,31},{2,4},{3,1},{4,6},{5,3},{6,8},{7,5},{8,10},{9,7},{10,... | collective-permute-start | bytes 921608 | tf_op jit(solution)/shard_map/ppermute | solution.py:415
  90.0 8.8 %collective-permute-start.17 = (bf16[1200,128]{1,0:T(8,128)(2,1)S(1)}, bf16[1200,128]{1,0:T(8,128)(2,1)S(1)}, u32[]{:S(2)}, u32[]{:S(2)}) collective-permute-start(bf16[1200,128]{1,0:T(8,128)(2,1)S(1)} %add_convert_fusion.4.refs_7_), channel_id=1, source_target_pairs={{0,2},{1,31},{2,4},{3,1},{4,6},{5,3},{6,8},{7,5},{8,10},{9,7},{10,... | collective-permute-start | bytes 921608 | tf_op jit(solution)/shard_map/ppermute | solution.py:415
  94.8 8.8 %collective-permute-start.10 = (bf16[1200,128]{1,0:T(8,128)(2,1)S(1)}, bf16[1200,128]{1,0:T(8,128)(2,1)S(1)}, u32[]{:S(2)}, u32[]{:S(2)}) collective-permute-start(bf16[1200,128]{1,0:T(8,128)(2,1)S(1)} %add_convert_fusion.11.refs_8_), channel_id=1, source_target_pairs={{0,2},{1,31},{2,4},{3,1},{4,6},{5,3},{6,8},{7,5},{8,10},{9,7},{10,... | collective-permute-start | bytes 921608 | tf_op jit(solution)/shard_map/ppermute | solution.py:415
  98.9 8.8 %collective-permute-start.18 = (bf16[1200,128]{1,0:T(8,128)(2,1)S(1)}, bf16[1200,128]{1,0:T(8,128)(2,1)S(1)}, u32[]{:S(2)}, u32[]{:S(2)}) collective-permute-start(bf16[1200,128]{1,0:T(8,128)(2,1)S(1)} %add_convert_fusion.3.refs_9_), channel_id=1, source_target_pairs={{0,2},{1,31},{2,4},{3,1},{4,6},{5,3},{6,8},{7,5},{8,10},{9,7},{10,... | collective-permute-start | bytes 921608 | tf_op jit(solution)/shard_map/ppermute | solution.py:415
  103.7 8.8 %collective-permute-start.11 = (bf16[1200,128]{1,0:T(8,128)(2,1)S(1)}, bf16[1200,128]{1,0:T(8,128)(2,1)S(1)}, u32[]{:S(2)}, u32[]{:S(2)}) collective-permute-start(bf16[1200,128]{1,0:T(8,128)(2,1)S(1)} %add_convert_fusion.10.refs_10_), channel_id=1, source_target_pairs={{0,2},{1,31},{2,4},{3,1},{4,6},{5,3},{6,8},{7,5},{8,10},{9,7},{10,... | collective-permute-start | bytes 921608 | tf_op jit(solution)/shard_map/ppermute | solution.py:415
  107.8 8.8 %collective-permute-start.19 = (bf16[1200,128]{1,0:T(8,128)(2,1)S(1)}, bf16[1200,128]{1,0:T(8,128)(2,1)S(1)}, u32[]{:S(2)}, u32[]{:S(2)}) collective-permute-start(bf16[1200,128]{1,0:T(8,128)(2,1)S(1)} %add_convert_fusion.2.refs_11_), channel_id=1, source_target_pairs={{0,2},{1,31},{2,4},{3,1},{4,6},{5,3},{6,8},{7,5},{8,10},{9,7},{10,... | collective-permute-start | bytes 921608 | tf_op jit(solution)/shard_map/ppermute | solution.py:415
  112.6 8.8 %collective-permute-start.12 = (bf16[1200,128]{1,0:T(8,128)(2,1)S(1)}, bf16[1200,128]{1,0:T(8,128)(2,1)S(1)}, u32[]{:S(2)}, u32[]{:S(2)}) collective-permute-start(bf16[1200,128]{1,0:T(8,128)(2,1)S(1)} %add_convert_fusion.9.refs_12_), channel_id=1, source_target_pairs={{0,2},{1,31},{2,4},{3,1},{4,6},{5,3},{6,8},{7,5},{8,10},{9,7},{10,... | collective-permute-start | bytes 921608 | tf_op jit(solution)/shard_map/ppermute | solution.py:415
  116.7 9.8 %collective-permute-start.20 = (bf16[1200,128]{1,0:T(8,128)(2,1)S(1)}, bf16[1200,128]{1,0:T(8,128)(2,1)S(1)}, u32[]{:S(2)}, u32[]{:S(2)}) collective-permute-start(bf16[1200,128]{1,0:T(8,128)(2,1)S(1)} %add_convert_fusion.1.refs_13_), channel_id=1, source_target_pairs={{0,2},{1,31},{2,4},{3,1},{4,6},{5,3},{6,8},{7,5},{8,10},{9,7},{10,... | collective-permute-start | bytes 921608 | tf_op jit(solution)/shard_map/ppermute | solution.py:415
  121.5 15.1 %collective-permute-start.13 = (bf16[1200,128]{1,0:T(8,128)(2,1)S(1)}, bf16[1200,128]{1,0:T(8,128)(2,1)S(1)}, u32[]{:S(2)}, u32[]{:S(2)}) collective-permute-start(bf16[1200,128]{1,0:T(8,128)(2,1)S(1)} %add_convert_fusion.8.refs_14_), channel_id=1, source_target_pairs={{0,2},{1,31},{2,4},{3,1},{4,6},{5,3},{6,8},{7,5},{8,10},{9,7},{10,... | collective-permute-start | bytes 921608 | tf_op jit(solution)/shard_map/ppermute | solution.py:415
  126.6 16.2 %collective-permute-start.21 = (bf16[1200,128]{1,0:T(8,128)(2,1)S(1)}, bf16[1200,128]{1,0:T(8,128)(2,1)S(1)}, u32[]{:S(2)}, u32[]{:S(2)}) collective-permute-start(bf16[1200,128]{1,0:T(8,128)(2,1)S(1)} %add_convert_fusion.refs_0_), channel_id=1, source_target_pairs={{0,1},{1,0},{2,3},{3,2},{4,5},{5,4},{6,7},{7,6},{8,9},{9,8},{10,11... | collective-permute-start | bytes 921608 | tf_op jit(solution)/shard_map/ppermute | solution.py:442
  137.1 4.1 %collective-permute-start.22 = (bf16[384,128]{1,0:T(8,128)(2,1)S(1)}, bf16[384,128]{1,0:T(8,128)(2,1)S(1)}, u32[]{:S(2)}, u32[]{:S(2)}) collective-permute-start(bf16[384,128]{1,0:T(8,128)(2,1)S(1)} %get-tuple-element.82), channel_id=1, source_target_pairs={{0,1},{1,0},{2,3},{3,2},{4,5},{5,4},{6,7},{7,6},{8,9},{9,8},{10,11... | collective-permute-start | bytes 294920 | tf_op jit(solution)/shard_map/ppermute | solution.py:443
  (3 other events, 3.2 us)

commit v3 on v2

--- a/solution.py
+++ b/solution.py
@@ -9,6 +9,7 @@
 SUB = 3
 KAPPA = 0.24
 GROUP = 4
+HALVES = 1
 PAYLOAD = 176
 BF = jnp.bfloat16
 F32 = jnp.float32
@@ -80,7 +81,7 @@
 
 def contrib_kernel(
     blk, idx, atm, weight, narrow, extra,
-    sums, near_sums, far, near, rest, q,
+    sums, near_sums, far, far_back, near, rest, payload, q,
 ):
     total, size = sums.shape[0], sums.shape[1]
 
@@ -105,66 +106,88 @@
             q[pl.ds((p + i) * FIELDS, 8)] = parts[i] + parts[i + 1]
         for i in range(GROUP):
             added(sums, idx[p + i], blocks[i])
-    n_near, n_rest = near_sums.shape[0], rest.shape[0]
-    n_slots = (far.shape[0] - q.shape[0] - extra.shape[0]) // size
+    payload[pl.ds(0, q.shape[0])] = q[...].astype(BF)
+    payload[pl.ds(q.shape[0], extra.shape[0])] = extra[...]
+    n_near, n_rest, n_slots = near_sums.shape[0], rest.shape[0], near.shape[0]
+    cap = n_slots // 2
     base = total - n_near - 2 * n_slots - n_rest
     for i in range(n_near):
         near_sums[i] = sums[base + i]
     base += n_near
-    for i in range(n_slots):
+    for i in range(cap):
         far[pl.ds(i * size, size)] = sums[base + i]
+        far_back[pl.ds(i * size, size)] = sums[base + cap + i]
     base += n_slots
     for i in range(n_rest):
         rest[i] = sums[base + i]
     base += n_rest
     for i in range(n_slots):
-        near[pl.ds(i * size, size)] = sums[base + i]
-    for out in (far, near):
-        out[pl.ds(n_slots * size, q.shape[0])] = q[...].astype(BF)
-        out[pl.ds(n_slots * size + q.shape[0], extra.shape[0])] = extra[...]
-
-
-def first_kernel(tab_mate, near_sums, far, near, same, other):
+        near[i] = sums[base + i]
+    far[pl.ds(cap * size, PAYLOAD)] = payload[...]
+    far_back[pl.ds(cap * size, 16)] = payload[pl.ds(PAYLOAD - 16, 16)]
+
+
+def split_out(outs, held, tail):
+    body = held.shape[0] // HALVES
+    at = 0
+    for h, out in enumerate(outs):
+        out[pl.ds(0, body)] = held[pl.ds(h * body, body)]
+        left = out.shape[0] - body
+        out[pl.ds(body, left)] = tail(at, left)
+        at += left
+
+
+def first_kernel(tab_mate, near_sums, far, far_back, near, payload, rest, *outs_scratch):
+    outs, passed, held = outs_scratch[:-2], outs_scratch[-2], outs_scratch[-1]
+    passed[...] = rest[...]
     size = near_sums.shape[1]
     blocks = near_sums.shape[0] // 2
-    payload = same.shape[0] - blocks * size
-    n_slots = (far.shape[0] - payload) // size
-    cap = n_slots // 2
-    low = tab_mate.shape[0] - n_slots
-    told = far[pl.ds(far.shape[0] - 16, 16)].astype(F32)[10:11]
-    lane = lax.broadcasted_iota(jnp.int32, told.shape, 1)
-    for j, (out, source) in enumerate(((same, far), (other, near))):
+    cap = near.shape[0] // 2
+    low = tab_mate.shape[0] - near.shape[0]
+    lane = lax.broadcasted_iota(jnp.int32, (1, near_sums.shape[2]), 1)
+    for j, came in enumerate((far, far_back)):
+        told = came[pl.ds(came.shape[0] - 16, 16)].astype(F32)[10:11]
         for b in range(blocks):
-            out[pl.ds(b * size, size)] = near_sums[j * blocks + b]
-        out[pl.ds(blocks * size, payload)] = source[pl.ds(n_slots * size, payload)]
+            held[pl.ds(b * size, size)] = near_sums[j * blocks + b]
         for r in range(cap):
             slot = j * cap + r
             far_at = jnp.sum(jnp.where(lane == slot, told, 0.0)).astype(jnp.int32)
-            for at, held in ((far_at, far), (tab_mate[low + slot], near)):
-                to = pl.multiple_of(lax.rem(at, blocks) * size, size)
-                added(out, pl.ds(to, size), held[pl.ds(slot * size, size)])
-
-
-def rest_kernel(tab_mate, sums, rest, *outs, cap, n_far):
+            to = pl.multiple_of(lax.rem(far_at, blocks) * size, size)
+            added(held, pl.ds(to, size), came[pl.ds(r * size, size)])
+            to = pl.multiple_of(lax.rem(tab_mate[low + slot], blocks) * size, size)
+            added(held, pl.ds(to, size), near[slot])
+        if j == 0:
+            split_out(outs[:HALVES], held, lambda at, n: far[pl.ds(cap * size + at, n)])
+        else:
+            split_out(outs[HALVES:], held, lambda at, n: payload[pl.ds(at, n)])
+
+
+def rest_kernel(tab_mate, sums, rest, *outs_scratch, cap, n_far):
+    outs, held = outs_scratch[:-1], outs_scratch[-1]
     size = sums.shape[1]
-    blocks = (outs[0].shape[0] - PAYLOAD) // size
-    payload = PAYLOAD
-    for m, out in enumerate(outs):
+    blocks = held.shape[0] // size
+    for m in range(len(outs) // HALVES):
         for b in range(blocks):
-            out[pl.ds(b * size, size)] = sums[m * blocks + b]
-        out[pl.ds(blocks * size, payload)] = jnp.zeros((payload, out.shape[1]), BF)
+            held[pl.ds(b * size, size)] = sums[m * blocks + b]
         if m >= 2:
             for r in range(cap):
                 slot = (m - 2) * cap + r
                 to = pl.multiple_of(lax.rem(tab_mate[n_far + slot], blocks) * size, size)
-                added(out, pl.ds(to, size), rest[slot])
-
-
-def ocean_kernel(adv, state, wet, coupling, mine, swapped, out):
+                added(held, pl.ds(to, size), rest[slot])
+        split_out(
+            outs[m * HALVES:(m + 1) * HALVES],
+            held,
+            lambda at, n: jnp.zeros((n, sums.shape[2]), BF),
+        )
+
+
+def ocean_kernel(adv, state, wet, coupling, *refs):
+    mine, swapped, out = refs[:HALVES], refs[HALVES:-1], refs[-1]
     size = out.shape[1]
+    each = out.shape[0] // HALVES
     for b in range(out.shape[0]):
-        rows = pl.ds(b * size, size)
-        forcing = (mine[rows].astype(F32) + swapped[rows].astype(F32)).astype(BF)
+        h, rows = b // each, pl.ds((b % each) * size, size)
+        forcing = (mine[h][rows].astype(F32) + swapped[h][rows].astype(F32)).astype(BF)
         pushed = jnp.dot(forcing, coupling[...], preferred_element_type=F32)
         updated = (adv[b].astype(F32) + pushed).astype(BF).astype(F32)
         keep = wet[b].astype(F32) > 0.5
@@ -172,11 +195,12 @@
 
 
 def picked(ids, message, sums):
-    lanes = message.shape[1]
+    lanes = message[0].shape[1]
     rows = ids.shape[0]
-    first = message.shape[0] - PAYLOAD
     tail = PAYLOAD - lanes
-    id_rows = message[pl.ds(message.shape[0] - 16, 16)].astype(F32)
+    first, last = message[0], message[-1]
+    begin = first.shape[0] - (PAYLOAD if len(message) == 1 else lanes)
+    id_rows = last[pl.ds(last.shape[0] - 16, 16)].astype(F32)
     row_f = lax.broadcasted_iota(jnp.int32, (rows, lanes), 0) % FIELDS
     lane = lax.broadcasted_iota(jnp.int32, (rows, lanes), 1)
     same_f = row_f == lane % FIELDS
@@ -191,35 +215,32 @@
             jnp.where(mask, 1.0, 0.0).astype(BF), block, preferred_element_type=F32
         )
 
-    low = message[pl.ds(first + lanes, tail)]
+    low = last[pl.ds(last.shape[0] - tail, tail)]
     pushed, adv, wet = sums
     return (
-        pushed + take(match & same_f, message[pl.ds(first, lanes)]),
+        pushed + take(match & same_f, first[pl.ds(begin, lanes)]),
         adv + take(match_t & is_adv[:, :tail], low),
         wet + take(match_t & is_wet[:, :tail], low),
     )
 
 
-def early_kernel(ids, both, *refs):
-    local, messages, out = refs[:2], refs[2:-1], refs[-1]
-    rows, lanes = ids.shape[0], out.shape[2]
-    zero = jnp.zeros((rows, lanes), F32)
-    mine = (zero,) * 3
-    for message in local:
-        mine = picked(ids[...], message, mine)
-    for i in range(3):
-        out[i, pl.ds(0, rows)] = mine[i]
-        out[i, pl.ds(rows, rows)] = zero
-    for message in messages:
+def grouped(refs):
+    return [refs[i:i + HALVES] for i in range(0, len(refs), HALVES)]
+
+
+def early_kernel(both, payload, far, *refs):
+    out = refs[-1]
+    out[...] = jnp.zeros_like(out)
+    for message in [(payload,), (far,)] + grouped(refs[:-1]):
         sums = picked(both[...], message, tuple(out[i] for i in range(3)))
         for i in range(3):
             out[i] = sums[i]
 
 
 def late_kernel(both, early, *refs):
-    messages, mine, mate = refs[:-2], refs[-2], refs[-1]
+    mine, mate = refs[-2], refs[-1]
     sums = tuple(early[i] for i in range(3))
-    for message in messages:
+    for message in grouped(refs[:-2]):
         sums = picked(both[...], message, sums)
     rows = mine.shape[1]
     for i in range(3):
@@ -280,7 +301,8 @@
     half = chips // 2
     me = lax.axis_index("col")
     chip, core = me // 2, me % 2
-    onward = [(i, (i + 2 - 4 * (i % 2)) % devices) for i in range(devices)]
+    onward = [(i, (i + 2) % devices) for i in range(devices)]
+    backward = [(j, i) for i, j in onward]
     mate = [(i, i ^ 1) for i in range(devices)]
 
     owner = pair_ocean // blocks
@@ -290,27 +312,27 @@
         ((owner[None, :] == owner[:, None]) & (at[None, :] < at[:, None])).astype(jnp.int32),
         axis=1,
     )
-    offset = ((owner // 2 - chip) * (1 - 2 * core)) % chips
-    other = (owner % 2) ^ core
+    offset = (owner // 2 - chip) % chips
+    same = owner % 2 == core
     wide = 2 * blocks
     n_far = 2 * cap
     n_slots = n_far + 2 * cap * (half - 1)
     dense = half * wide
-    back = chips - offset
+    ahead = offset < half
+    steps = jnp.where(ahead, offset, chips - offset)
+    by_core = (offset == 0) | (offset == half)
+    chain = jnp.where(by_core, jnp.where(same, 0, 1), jnp.where(ahead, 0, 1))
+    here_too = by_core | (same == (chain == 0))
     target = jnp.where(
-        offset < half,
-        offset * wide + other * blocks + local,
+        offset == half,
+        dense + chain * cap + rank,
         jnp.where(
-            offset == half,
-            dense + other * cap + rank,
-            dense + n_far + ((back - 1) * 2 + (1 - other)) * cap + rank,
+            here_too,
+            steps * wide + chain * blocks + local,
+            dense + n_far + ((steps - 1) * 2 + chain) * cap + rank,
         ),
     )
-    value = jnp.where(
-        offset == half,
-        other * blocks + local,
-        jnp.where(back == half - 1, 0, back * wide) + (1 - other) * blocks + local,
-    )
+    value = local
     slot_at = dense + jnp.arange(n_slots)
     table = jnp.sum(
         jnp.where(target[:, None] == slot_at[None, :], value[:, None], 0), axis=0
@@ -359,96 +381,103 @@
     def rows_of(n, dtype=BF):
         return jax.ShapeDtypeStruct((n, breadth), dtype)
 
-    def column(ids):
-        return jnp.broadcast_to(ids[:, None], (pairs, FIELDS)).reshape(pairs * FIELDS, 1)
-
     def cost(flops, mib):
         return pl.CostEstimate(
             flops=flops, bytes_accessed=mib * 1024 * 1024, transcendentals=0
         )
 
     n_rest = n_slots - 2 * n_far
-    sums, near_sums, far, near, rest = pl.pallas_call(
+    sums, near_sums, far, far_back, near, rest, payload = pl.pallas_call(
         contrib_kernel,
         out_shape=(
             blocks_of(dense + n_slots),
             blocks_of(wide),
-            rows_of(n_far * breadth + PAYLOAD),
-            rows_of(n_far * breadth + PAYLOAD),
+            rows_of(cap * breadth + PAYLOAD),
+            rows_of(cap * breadth + 16),
+            blocks_of(n_far),
             blocks_of(n_rest),
+            rows_of(PAYLOAD),
         ),
         in_specs=[SM] * 2 + [VM] * 4,
-        out_specs=(VM,) * 5,
+        out_specs=(VM,) * 7,
         scratch_shapes=[pltpu.VMEM((pairs * FIELDS, breadth), F32)],
         compiler_params=params(4),
         cost_estimate=cost(2 * pairs * breadth * breadth * channels, 8),
     )(pair_block, target, current, pair_weight, narrow, extra)
 
-    far_in = lax.ppermute(far, "col", onward)
-    near_in = lax.ppermute(near, "col", mate)
-
-    length = blocks * breadth + PAYLOAD
-    held = pl.pallas_call(
+    far = lax.ppermute(far, "col", onward)
+    far_back = lax.ppermute(far_back, "col", backward)
+    near = lax.ppermute(near, "col", mate)
+
+    body = blocks * breadth // HALVES
+    tails = (PAYLOAD,) if HALVES == 1 else (breadth, PAYLOAD - breadth)
+    shapes = tuple(rows_of(body + tail) for tail in tails)
+    whole = [pltpu.VMEM((blocks * breadth, channels), BF)]
+    *held, rest = pl.pallas_call(
         first_kernel,
-        out_shape=(rows_of(length),) * 2,
-        in_specs=[SM, VM, VM, VM],
-        out_specs=(VM,) * 2,
+        out_shape=shapes * 2 + (blocks_of(n_rest),),
+        in_specs=[SM] + [VM] * 6,
+        out_specs=(VM,) * (2 * HALVES + 1),
+        scratch_shapes=whole,
         compiler_params=params(4),
         cost_estimate=cost(wide * breadth * channels, 2),
-    )(table_mate, near_sums, far_in, near_in)
-    held = list(held)
-
-    rest, held[0] = lax.optimization_barrier((rest, held[0]))
+    )(table_mate, near_sums, far, far_back, near, payload, rest)
+
     rest = lax.ppermute(rest, "col", mate)
     here = pl.pallas_call(
         lambda *refs: rest_kernel(*refs, cap=cap, n_far=n_far),
-        out_shape=(rows_of(length),) * (2 * (half - 1)),
+        out_shape=shapes * (2 * (half - 1)),
         in_specs=[SM, VM, VM],
-        out_specs=(VM,) * (2 * (half - 1)),
+        out_specs=(VM,) * (2 * HALVES * (half - 1)),
+        scratch_shapes=whole,
         compiler_params=params(4),
         cost_estimate=cost(n_rest * breadth * channels, 4),
     )(table_mate, sums, rest)
 
+    chains = 2 * HALVES
+    order = [j * HALVES + h for h in range(HALVES) for j in (1, 0)]
     messages = []
     for hop in range(half - 1, 0, -1):
-        for j in (1, 0):
-            came = lax.ppermute(held[j], "col", onward)
-            total = came.astype(F32) + here[(hop - 1) * 2 + j].astype(F32)
-            held[j] = total.astype(BF)
-            messages.append(held[j])
-
-    ids = column(pair_ocean.astype(F32))
-    both = jnp.concatenate([ids, column(theirs.astype(F32))], axis=0)
+        for m in order:
+            came = lax.ppermute(held[m], "col", backward if m >= HALVES else onward)
+            total = came.astype(F32) + here[(hop - 1) * chains + m].astype(F32)
+            held[m] = total.astype(BF)
+        messages.extend(held)
+
+    def column(ids):
+        return jnp.broadcast_to(ids[:, None], (pairs, FIELDS)).reshape(pairs * FIELDS, 1)
+
+    both = jnp.concatenate([column(pair_ocean), column(theirs)], axis=0).astype(F32)
     early = pl.pallas_call(
         early_kernel,
         out_shape=jax.ShapeDtypeStruct((3, 2 * pairs * FIELDS, breadth), F32),
-        in_specs=[VM] * (2 + 3 + len(messages) - 2),
+        in_specs=[VM] * (3 + len(messages) - chains),
         out_specs=VM,
         compiler_params=params(4),
         cost_estimate=cost(len(messages) * 6 * 128 ** 3, 2),
-    )(ids, both, near, near_in, far_in, *messages[:-2])
+    )(both, payload, far, *messages[:-chains])
     mine, for_mate = pl.pallas_call(
         late_kernel,
         out_shape=(
             jax.ShapeDtypeStruct((3, pairs * FIELDS, breadth), F32),
             rows_of(3 * pairs * FIELDS),
         ),
-        in_specs=[VM] * 4,
+        in_specs=[VM] * (2 + chains),
         out_specs=(VM,) * 2,
         compiler_params=params(4),
         cost_estimate=cost(12 * 128 ** 3, 1),
-    )(both, early, *messages[-2:])
-
-    swapped = lax.ppermute(held[1], "col", mate)
+    )(both, early, *messages[-chains:])
+
+    swapped = [lax.ppermute(message, "col", mate) for message in held[HALVES:]]
     from_mate = lax.ppermute(for_mate, "col", mate)
     ocean_next = pl.pallas_call(
         ocean_kernel,
         out_shape=blocks_of(blocks),
-        in_specs=[VM] * 6,
+        in_specs=[VM] * (4 + chains),
         out_specs=VM,
         compiler_params=params(4),
         cost_estimate=cost(2 * blocks * breadth * channels * channels, 2),
-    )(ocean_adv, ocean_state, wet, flux_coupling, held[0], swapped)
+    )(ocean_adv, ocean_state, wet, flux_coupling, *held[:HALVES], *swapped)
 
     surface_on_atm = pl.pallas_call(
         reply_kernel,

time: 145 us -> 152 us (1.048)
  waiting for transfers between devices: 9.67 us -> 21.1 us
  starting transfers between devices: 105 us -> 102 us
    ppermute x17 -> x18, waiting for transfers between devices: 2.32 us -> 13.7 us  [the longest x14 12.8 us: on_device(): came = lax.ppermute(held[m], 'col', backward if m >= HALVES else onward)]
    ppermute x17 -> x18, starting transfers between devices: 83.2 us -> 79.7 us  [the longest x14 48.8 us: on_device(): came = lax.ppermute(held[m], 'col', backward if m >= HALVES else onward)]
    ppermute x1, starting transfers between devices: 3.18 us -> 5.59 us  [on_device(): from_mate = lax.ppermute(for_mate, 'col', mate)]
    ppermute x1, starting transfers between devices: 4.36 us -> 2.26 us  [on_device(): rest = lax.ppermute(rest, 'col', mate)]
    unnamed x26 -> x32, local copies, waits for them, and re-layouts: 7.37 us -> 6.68 us
  transfers between devices with their start and end apart: 23 -> 24, of which waited for: 6 -> 11; matrix products, arithmetic and copies ran while one was open for 3% -> 3% of each run, Pallas kernels for 3% -> 3%
where the time goes in v3:
time: 152 us; the launch traced here: 151 us
  starting transfers between devices  102 us (67%)
  waiting for transfers between devices  21.1 us (14%)
  Pallas kernels  10.4 us (7%)
  local copies, waits for them, and re-layouts  7.82 us (5%)
  other arithmetic  4.19 us (3%)
  matrix products  4.18 us (3%)
    ppermute x14, starting transfers between devices, on_device(): came = lax.ppermute(held[m], 'col', backward if m >= HALVES else onward)  48.8 us
    ppermute x1, starting transfers between devices, on_device(): far_back = lax.ppermute(far_back, 'col', backward)  14.1 us
    ppermute x14, waiting for transfers between devices, on_device(): came = lax.ppermute(held[m], 'col', backward if m >= HALVES else onward)  12.8 us
    ppermute x1, starting transfers between devices, on_device(): swapped = [lax.ppermute(message, 'col', mate) for message in held[HALVES:]]  8.59 us
    ppermute x2, starting transfers between devices, edges(): return (lax.ppermute(last, axis, up), lax.ppermute(first, axis, down))  6.79 us
    unnamed x32, local copies, waits for them, and re-layouts  6.68 us
    ppermute x2, waiting for transfers between devices, edges(): return (lax.ppermute(last, axis, up), lax.ppermute(first, axis, down))  5.81 us
    ppermute x1, starting transfers between devices, on_device(): from_mate = lax.ppermute(for_mate, 'col', mate)  5.59 us
  transfers between devices with their start and end apart: 24, of which 11 were waited for; matrix products, arithmetic and copies ran while one was open for 3% of the time, Pallas kernels for 3%

profile of v3, /device:TPU:33, one launch (start us, length us, event | category | flops | bytes accessed | tf_op | source)
XLA Modules:
  0.0 151.2 jit_solution(5710716992045355960)
XLA Ops:
  2.5 4.5 %collective-permute-start.1 = (bf16[3,128,128]{2,0,1:T(4,128)(2,1)S(1)}, bf16[3,128,128]{2,0,1:T(4,128)(2,1)S(1)}, u32[]{:S(2)}, u32[]{:S(2)}) collective-permute-start(bf16[3,128,128]{2,0,1:T(4,128)(2,1)S(1)} %get-tuple-element.90), channel_id=1, source_target_pairs={{32,0},{64,32},{96,64},{128,96},{160,128},{192,160},{224,192},{256... | collective-permute-start | bytes 294920 | tf_op jit(solution)/shard_map/ppermute | solution.py:31
  7.0 2.2 %collective-permute-start = (bf16[3,128,128]{2,0,1:T(4,128)(2,1)S(1)}, bf16[3,128,128]{2,0,1:T(4,128)(2,1)S(1)}, u32[]{:S(2)}, u32[]{:S(2)}) collective-permute-start(bf16[3,128,128]{2,0,1:T(4,128)(2,1)S(1)} %get-tuple-element.89), channel_id=1, source_target_pairs={{0,32},{32,64},{64,96},{96,128},{128,160},{160,192},{192,224},{224... | collective-permute-start | bytes 294920 | tf_op jit(solution)/shard_map/ppermute | solution.py:31
  10.6 5.8 %collective-permute-done = bf16[3,128,128]{2,0,1:T(4,128)(2,1)S(1)} collective-permute-done((bf16[3,128,128]{2,0,1:T(4,128)(2,1)S(1)}, bf16[3,128,128]{2,0,1:T(4,128)(2,1)S(1)}, u32[]{:S(2)}, u32[]{:S(2)}) %collective-permute-start) | collective-permute-done | bytes 98336 | tf_op jit(solution)/shard_map/ppermute | solution.py:31
  16.4 4.0 %collective-permute-start.3 = (bf16[31,3,128]{2,0,1:T(8,128)(2,1)S(1)}, bf16[31,3,128]{2,0,1:T(8,128)(2,1)S(1)}, u32[]{:S(2)}, u32[]{:S(2)}) collective-permute-start(bf16[31,3,128]{2,0,1:T(8,128)(2,1)S(1)} %get-tuple-element.88), channel_id=1, source_target_pairs={{1,0},{2,1},{3,2},{4,3},{5,4},{6,5},{7,6},{8,7},{9,8},{10,9},{11,1... | collective-permute-start | bytes 71432 | tf_op jit(solution)/shard_map/ppermute | solution.py:47
  20.4 3.9 %collective-permute-start.2 = (bf16[31,3,128]{2,0,1:T(8,128)(2,1)S(1)}, bf16[31,3,128]{2,0,1:T(8,128)(2,1)S(1)}, u32[]{:S(2)}, u32[]{:S(2)}) collective-permute-start(bf16[31,3,128]{2,0,1:T(8,128)(2,1)S(1)} %get-tuple-element.87), channel_id=1, source_target_pairs={{0,1},{1,2},{2,3},{3,4},{4,5},{5,6},{6,7},{7,8},{8,9},{9,10},{10,1... | collective-permute-start | bytes 71432 | tf_op jit(solution)/shard_map/ppermute | solution.py:46
  30.7 3.2 %shard_map.112 = (bf16[160,128,128]{2,1,0:T(8,128)(2,1)S(1)}, bf16[16,128,128]{2,1,0:T(8,128)(2,1)S(1)}, bf16[432,128]{1,0:T(8,128)(2,1)S(1)}, bf16[272,128]{1,0...) custom-call(s32[32]{0:T(128)S(1)} %copy-done.10, ...), custom_call_target="tpu_custom_call" | custom-call | flops 134217728 | bytes 8388608 | tf_op jit(solution)/shard_map/pallas_call | solution.py:390
  34.0 2.3 %copy-done.1 = bf16[160,128,128]{2,1,0:T(8,128)(2,1)} copy-done((bf16[160,128,128]{2,1,0:T(8,128)(2,1)}, bf16[160,128,128]{2,1,0:T(8,128)(2,1)S(1)}, u32[]{:S(2)}) %copy-start.1) | copy-done | bytes 5242904
  36.3 4.0 %collective-permute-start.4 = (bf16[432,128]{1,0:T(8,128)(2,1)S(1)}, bf16[432,128]{1,0:T(8,128)(2,1)S(1)}, u32[]{:S(2)}, u32[]{:S(2)}) collective-permute-start(bf16[432,128]{1,0:T(8,128)(2,1)S(1)} %get-tuple-element.60), channel_id=1, source_target_pairs={{0,2},{1,3},{2,4},{3,5},{4,6},{5,7},{6,8},{7,9},{8,10},{9,11},{10,... | collective-permute-start | bytes 331784 | tf_op jit(solution)/shard_map/ppermute | solution.py:408
  40.3 14.1 %collective-permute-start.5 = (bf16[272,128]{1,0:T(8,128)(2,1)S(1)}, bf16[272,128]{1,0:T(8,128)(2,1)S(1)}, u32[]{:S(2)}, u32[]{:S(2)}) collective-permute-start(bf16[272,128]{1,0:T(8,128)(2,1)S(1)} %get-tuple-element.61), channel_id=1, source_target_pairs={{2,0},{3,1},{4,2},{5,3},{6,4},{7,5},{8,6},{9,7},{10,8},{11,9},{12,... | collective-permute-start | bytes 208904 | tf_op jit(solution)/shard_map/ppermute | solution.py:409
  54.4 4.3 %collective-permute-start.6 = (bf16[4,128,128]{2,1,0:T(8,128)(2,1)S(1)}, bf16[4,128,128]{2,1,0:T(8,128)(2,1)S(1)}, u32[]{:S(2)}, u32[]{:S(2)}) collective-permute-start(bf16[4,128,128]{2,1,0:T(8,128)(2,1)S(1)} %get-tuple-element.62), channel_id=1, source_target_pairs={{0,1},{1,0},{2,3},{3,2},{4,5},{5,4},{6,7},{7,6},{8,9},{9,8},{10,11... | collective-permute-start | bytes 393224 | tf_op jit(solution)/shard_map/ppermute | solution.py:410
  61.3 2.3 %collective-permute-start.8 = (bf16[24,128,128]{2,1,0:T(8,128)(2,1)}, bf16[24,128,128]{2,1,0:T(8,128)(2,1)S(1)}, u32[]{:S(2)}, u32[]{:S(2)}) collective-permute-start(bf16[24,128,128]{2,1,0:T(8,128)(2,1)} %get-tuple-element.67), channel_id=1, source_target_pairs={{0,1},{1,0},{2,3},{3,2},{4,5},{5,4},{6,7},{7,6},{8,9},{9,8},{10,11... | collective-permute-start | bytes 2359304 | tf_op jit(solution)/shard_map/ppermute | solution.py:426
  63.6 3.9 %collective-permute-start.15 = (bf16[1200,128]{1,0:T(8,128)(2,1)S(1)}, bf16[1200,128]{1,0:T(8,128)(2,1)}, u32[]{:S(2)}, u32[]{:S(2)}) collective-permute-start(bf16[1200,128]{1,0:T(8,128)(2,1)S(1)} %get-tuple-element.75), channel_id=1, source_target_pairs={{2,0},{3,1},{4,2},{5,3},{6,4},{7,5},{8,6},{9,7},{10,8},{11,9},{12,... | collective-permute-start | bytes 921608 | tf_op jit(solution)/shard_map/ppermute | solution.py:442
  68.0 1.9 %collective-permute-start.7 = (bf16[1200,128]{1,0:T(8,128)(2,1)S(1)}, bf16[1200,128]{1,0:T(8,128)(2,1)S(1)}, u32[]{:S(2)}, u32[]{:S(2)}) collective-permute-start(bf16[1200,128]{1,0:T(8,128)(2,1)S(1)} %get-tuple-element.65), channel_id=1, source_target_pairs={{0,2},{1,3},{2,4},{3,5},{4,6},{5,7},{6,8},{7,9},{8,10},{9,11},{10,... | collective-permute-start | bytes 921608 | tf_op jit(solution)/shard_map/ppermute | solution.py:442
  69.9 2.5 %copy-done.2 = bf16[160,128,128]{2,1,0:T(8,128)(2,1)S(1)} copy-done((bf16[160,128,128]{2,1,0:T(8,128)(2,1)S(1)}, bf16[160,128,128]{2,1,0:T(8,128)(2,1)}, u32[]{:S(2)}) %copy-start.2) | copy-done | bytes 5242904
  75.3 5.3 %collective-permute-start.16 = (bf16[1200,128]{1,0:T(8,128)(2,1)S(1)}, bf16[1200,128]{1,0:T(8,128)(2,1)S(1)}, u32[]{:S(2)}, u32[]{:S(2)}) collective-permute-start(bf16[1200,128]{1,0:T(8,128)(2,1)S(1)} %add_convert_fusion.6.refs_1_), channel_id=1, source_target_pairs={{2,0},{3,1},{4,2},{5,3},{6,4},{7,5},{8,6},{9,7},{10,8},{11,9},{12,... | collective-permute-start | bytes 921608 | tf_op jit(solution)/shard_map/ppermute | solution.py:442
  80.7 1.9 %collective-permute-start.9 = (bf16[1200,128]{1,0:T(8,128)(2,1)S(1)}, bf16[1200,128]{1,0:T(8,128)(2,1)S(1)}, u32[]{:S(2)}, u32[]{:S(2)}) collective-permute-start(bf16[1200,128]{1,0:T(8,128)(2,1)S(1)} %add_convert_fusion.13.refs_0_), channel_id=1, source_target_pairs={{0,2},{1,3},{2,4},{3,5},{4,6},{5,7},{6,8},{7,9},{8,10},{9,11},{10,... | collective-permute-start | bytes 921608 | tf_op jit(solution)/shard_map/ppermute | solution.py:442
  82.6 3.7 %collective-permute-done.16 = bf16[1200,128]{1,0:T(8,128)(2,1)S(1)} collective-permute-done((bf16[1200,128]{1,0:T(8,128)(2,1)S(1)}, bf16[1200,128]{1,0:T(8,128)(2,1)S(1)}, u32[]{:S(2)}, u32[]{:S(2)}) %collective-permute-start.16) | collective-permute-done | bytes 307232 | tf_op jit(solution)/shard_map/ppermute | solution.py:442
  86.5 5.3 %collective-permute-start.17 = (bf16[1200,128]{1,0:T(8,128)(2,1)S(1)}, bf16[1200,128]{1,0:T(8,128)(2,1)S(1)}, u32[]{:S(2)}, u32[]{:S(2)}) collective-permute-start(bf16[1200,128]{1,0:T(8,128)(2,1)S(1)} %add_convert_fusion.5.refs_3_), channel_id=1, source_target_pairs={{2,0},{3,1},{4,2},{5,3},{6,4},{7,5},{8,6},{9,7},{10,8},{11,9},{12,... | collective-permute-start | bytes 921608 | tf_op jit(solution)/shard_map/ppermute | solution.py:442
  91.9 1.9 %collective-permute-start.10 = (bf16[1200,128]{1,0:T(8,128)(2,1)S(1)}, bf16[1200,128]{1,0:T(8,128)(2,1)S(1)}, u32[]{:S(2)}, u32[]{:S(2)}) collective-permute-start(bf16[1200,128]{1,0:T(8,128)(2,1)S(1)} %add_convert_fusion.12.refs_2_), channel_id=1, source_target_pairs={{0,2},{1,3},{2,4},{3,5},{4,6},{5,7},{6,8},{7,9},{8,10},{9,11},{10,... | collective-permute-start | bytes 921608 | tf_op jit(solution)/shard_map/ppermute | solution.py:442
  93.8 2.8 %collective-permute-done.17 = bf16[1200,128]{1,0:T(8,128)(2,1)S(1)} collective-permute-done((bf16[1200,128]{1,0:T(8,128)(2,1)S(1)}, bf16[1200,128]{1,0:T(8,128)(2,1)S(1)}, u32[]{:S(2)}, u32[]{:S(2)}) %collective-permute-start.17) | collective-permute-done | bytes 307232 | tf_op jit(solution)/shard_map/ppermute | solution.py:442
  96.8 5.3 %collective-permute-start.18 = (bf16[1200,128]{1,0:T(8,128)(2,1)S(1)}, bf16[1200,128]{1,0:T(8,128)(2,1)S(1)}, u32[]{:S(2)}, u32[]{:S(2)}) collective-permute-start(bf16[1200,128]{1,0:T(8,128)(2,1)S(1)} %add_convert_fusion.4.refs_5_), channel_id=1, source_target_pairs={{2,0},{3,1},{4,2},{5,3},{6,4},{7,5},{8,6},{9,7},{10,8},{11,9},{12,... | collective-permute-start | bytes 921608 | tf_op jit(solution)/shard_map/ppermute | solution.py:442
  102.2 1.9 %collective-permute-start.11 = (bf16[1200,128]{1,0:T(8,128)(2,1)S(1)}, bf16[1200,128]{1,0:T(8,128)(2,1)S(1)}, u32[]{:S(2)}, u32[]{:S(2)}) collective-permute-start(bf16[1200,128]{1,0:T(8,128)(2,1)S(1)} %add_convert_fusion.11.refs_4_), channel_id=1, source_target_pairs={{0,2},{1,3},{2,4},{3,5},{4,6},{5,7},{6,8},{7,9},{8,10},{9,11},{10,... | collective-permute-start | bytes 921608 | tf_op jit(solution)/shard_map/ppermute | solution.py:442
  104.1 1.7 %collective-permute-done.18 = bf16[1200,128]{1,0:T(8,128)(2,1)S(1)} collective-permute-done((bf16[1200,128]{1,0:T(8,128)(2,1)S(1)}, bf16[1200,128]{1,0:T(8,128)(2,1)S(1)}, u32[]{:S(2)}, u32[]{:S(2)}) %collective-permute-start.18) | collective-permute-done | bytes 307232 | tf_op jit(solution)/shard_map/ppermute | solution.py:442
  105.9 5.5 %collective-permute-start.19 = (bf16[1200,128]{1,0:T(8,128)(2,1)S(1)}, bf16[1200,128]{1,0:T(8,128)(2,1)S(1)}, u32[]{:S(2)}, u32[]{:S(2)}) collective-permute-start(bf16[1200,128]{1,0:T(8,128)(2,1)S(1)} %add_convert_fusion.3.refs_7_), channel_id=1, source_target_pairs={{2,0},{3,1},{4,2},{5,3},{6,4},{7,5},{8,6},{9,7},{10,8},{11,9},{12,... | collective-permute-start | bytes 921608 | tf_op jit(solution)/shard_map/ppermute | solution.py:442
  111.5 1.9 %collective-permute-start.12 = (bf16[1200,128]{1,0:T(8,128)(2,1)S(1)}, bf16[1200,128]{1,0:T(8,128)(2,1)S(1)}, u32[]{:S(2)}, u32[]{:S(2)}) collective-permute-start(bf16[1200,128]{1,0:T(8,128)(2,1)S(1)} %add_convert_fusion.10.refs_6_), channel_id=1, source_target_pairs={{0,2},{1,3},{2,4},{3,5},{4,6},{5,7},{6,8},{7,9},{8,10},{9,11},{10,... | collective-permute-start | bytes 921608 | tf_op jit(solution)/shard_map/ppermute | solution.py:442
  113.5 1.7 %collective-permute-done.19 = bf16[1200,128]{1,0:T(8,128)(2,1)S(1)} collective-permute-done((bf16[1200,128]{1,0:T(8,128)(2,1)S(1)}, bf16[1200,128]{1,0:T(8,128)(2,1)S(1)}, u32[]{:S(2)}, u32[]{:S(2)}) %collective-permute-start.19) | collective-permute-done | bytes 307232 | tf_op jit(solution)/shard_map/ppermute | solution.py:442
  115.3 5.0 %collective-permute-start.20 = (bf16[1200,128]{1,0:T(8,128)(2,1)S(1)}, bf16[1200,128]{1,0:T(8,128)(2,1)S(1)}, u32[]{:S(2)}, u32[]{:S(2)}) collective-permute-start(bf16[1200,128]{1,0:T(8,128)(2,1)S(1)} %add_convert_fusion.2.refs_9_), channel_id=1, source_target_pairs={{2,0},{3,1},{4,2},{5,3},{6,4},{7,5},{8,6},{9,7},{10,8},{11,9},{12,... | collective-permute-start | bytes 921608 | tf_op jit(solution)/shard_map/ppermute | solution.py:442
  120.4 1.9 %collective-permute-start.13 = (bf16[1200,128]{1,0:T(8,128)(2,1)S(1)}, bf16[1200,128]{1,0:T(8,128)(2,1)S(1)}, u32[]{:S(2)}, u32[]{:S(2)}) collective-permute-start(bf16[1200,128]{1,0:T(8,128)(2,1)S(1)} %add_convert_fusion.9.refs_8_), channel_id=1, source_target_pairs={{0,2},{1,3},{2,4},{3,5},{4,6},{5,7},{6,8},{7,9},{8,10},{9,11},{10,... | collective-permute-start | bytes 921608 | tf_op jit(solution)/shard_map/ppermute | solution.py:442
  124.2 5.0 %collective-permute-start.21 = (bf16[1200,128]{1,0:T(8,128)(2,1)S(1)}, bf16[1200,128]{1,0:T(8,128)(2,1)S(1)}, u32[]{:S(2)}, u32[]{:S(2)}) collective-permute-start(bf16[1200,128]{1,0:T(8,128)(2,1)S(1)} %add_convert_fusion.1.refs_11_), channel_id=1, source_target_pairs={{2,0},{3,1},{4,2},{5,3},{6,4},{7,5},{8,6},{9,7},{10,8},{11,9},{12,... | collective-permute-start | bytes 921608 | tf_op jit(solution)/shard_map/ppermute | solution.py:442
  129.3 1.9 %collective-permute-start.14 = (bf16[1200,128]{1,0:T(8,128)(2,1)S(1)}, bf16[1200,128]{1,0:T(8,128)(2,1)S(1)}, u32[]{:S(2)}, u32[]{:S(2)}) collective-permute-start(bf16[1200,128]{1,0:T(8,128)(2,1)S(1)} %add_convert_fusion.8.refs_10_), channel_id=1, source_target_pairs={{0,2},{1,3},{2,4},{3,5},{4,6},{5,7},{6,8},{7,9},{8,10},{9,11},{10,... | collective-permute-start | bytes 921608 | tf_op jit(solution)/shard_map/ppermute | solution.py:442
  133.1 8.6 %collective-permute-start.22 = (bf16[1200,128]{1,0:T(8,128)(2,1)S(1)}, bf16[1200,128]{1,0:T(8,128)(2,1)S(1)}, u32[]{:S(2)}, u32[]{:S(2)}) collective-permute-start(bf16[1200,128]{1,0:T(8,128)(2,1)S(1)} %add_convert_fusion.refs_1_), channel_id=1, source_target_pairs={{0,1},{1,0},{2,3},{3,2},{4,5},{5,4},{6,7},{7,6},{8,9},{9,8},{10,11... | collective-permute-start | bytes 921608 | tf_op jit(solution)/shard_map/ppermute | solution.py:471
  142.1 5.6 %collective-permute-start.23 = (bf16[384,128]{1,0:T(8,128)(2,1)S(1)}, bf16[384,128]{1,0:T(8,128)(2,1)S(1)}, u32[]{:S(2)}, u32[]{:S(2)}) collective-permute-start(bf16[384,128]{1,0:T(8,128)(2,1)S(1)} %get-tuple-element.84), channel_id=1, source_target_pairs={{0,1},{1,0},{2,3},{3,2},{4,5},{5,4},{6,7},{7,6},{8,9},{9,8},{10,11... | collective-permute-start | bytes 294920 | tf_op jit(solution)/shard_map/ppermute | solution.py:472
  (111 shorter events, 23.7 us)
Async XLA Ops:
  0.6 26.0 %copy-start = (bf16[128,128]{1,0:T(8,128)(2,1)S(1)}, bf16[128,128]{1,0:T(8,128)(2,1)}, u32[]{:S(2)}) copy-start(bf16[128,128]{1,0:T(8,128)(2,1)} %param.14) | copy-start | bytes 98308
  0.7 9.5 %copy-start.13 = (s32[8,128]{1,0:T(8,128)S(1)}, s32[8,128]{1,0:T(8,128)}, u32[]{:S(2)}) copy-start(s32[8,128]{1,0:T(8,128)} %param.21) | copy-start | bytes 12292
  0.7 9.5 %copy-start.8 = (bf16[128,128]{1,0:T(8,128)(2,1)S(1)}, bf16[128,128]{1,0:T(8,128)(2,1)}, u32[]{:S(2)}) copy-start(bf16[128,128]{1,0:T(8,128)(2,1)} %coupling.1) | copy-start | bytes 98308
  2.5 8.1 %collective-permute-start.1 = (bf16[3,128,128]{2,0,1:T(4,128)(2,1)S(1)}, bf16[3,128,128]{2,0,1:T(4,128)(2,1)S(1)}, u32[]{:S(2)}, u32[]{:S(2)}) collective-permute-start(bf16[3,128,128]{2,0,1:T(4,128)(2,1)S(1)} %get-tuple-element.90), channel_id=1, source_target_pairs={{32,0},{64,32},{96,64},{128,96},{160,128},{192,160},{224,192},{256... | collective-permute-start | bytes 294920 | tf_op jit(solution)/shard_map/ppermute | solution.py:31
  7.0 9.3 %collective-permute-start = (bf16[3,128,128]{2,0,1:T(4,128)(2,1)S(1)}, bf16[3,128,128]{2,0,1:T(4,128)(2,1)S(1)}, u32[]{:S(2)}, u32[]{:S(2)}) collective-permute-start(bf16[3,128,128]{2,0,1:T(4,128)(2,1)S(1)} %get-tuple-element.89), channel_id=1, source_target_pairs={{0,32},{32,64},{64,96},{96,128},{128,160},{160,192},{192,224},{224... | collective-permute-start | bytes 294920 | tf_op jit(solution)/shard_map/ppermute | solution.py:31
  16.4 8.2 %collective-permute-start.3 = (bf16[31,3,128]{2,0,1:T(8,128)(2,1)S(1)}, bf16[31,3,128]{2,0,1:T(8,128)(2,1)S(1)}, u32[]{:S(2)}, u32[]{:S(2)}) collective-permute-start(bf16[31,3,128]{2,0,1:T(8,128)(2,1)S(1)} %get-tuple-element.88), channel_id=1, source_target_pairs={{1,0},{2,1},{3,2},{4,3},{5,4},{6,5},{7,6},{8,7},{9,8},{10,9},{11,1... | collective-permute-start | bytes 71432 | tf_op jit(solution)/shard_map/ppermute | solution.py:47
  20.4 4.8 %collective-permute-start.2 = (bf16[31,3,128]{2,0,1:T(8,128)(2,1)S(1)}, bf16[31,3,128]{2,0,1:T(8,128)(2,1)S(1)}, u32[]{:S(2)}, u32[]{:S(2)}) collective-permute-start(bf16[31,3,128]{2,0,1:T(8,128)(2,1)S(1)} %get-tuple-element.87), channel_id=1, source_target_pairs={{0,1},{1,2},{2,3},{3,4},{4,5},{5,6},{6,7},{7,8},{8,9},{9,10},{10,1... | collective-permute-start | bytes 71432 | tf_op jit(solution)/shard_map/ppermute | solution.py:46
  30.5 30.8 %copy-start.5 = (bf16[24,128,128]{2,1,0:T(8,128)(2,1)}, bf16[24,128,128]{2,1,0:T(8,128)(2,1)S(1)}, u32[]{:S(2)}) copy-start(bf16[24,128,128]{2,1,0:T(8,128)(2,1)S(1)} %convolution_convert_fusion.2.atm) | copy-start | bytes 2359300
  36.3 25.0 %copy-start.6 = (bf16[176,128]{1,0:T(8,128)(2,1)}, bf16[176,128]{1,0:T(8,128)(2,1)S(1)}, u32[]{:S(2)}) copy-start(bf16[176,128]{1,0:T(8,128)(2,1)S(1)} %get-tuple-element.63.payload) | copy-start | bytes 135172
  36.3 22.5 %collective-permute-start.4 = (bf16[432,128]{1,0:T(8,128)(2,1)S(1)}, bf16[432,128]{1,0:T(8,128)(2,1)S(1)}, u32[]{:S(2)}, u32[]{:S(2)}) collective-permute-start(bf16[432,128]{1,0:T(8,128)(2,1)S(1)} %get-tuple-element.60), channel_id=1, source_target_pairs={{0,2},{1,3},{2,4},{3,5},{4,6},{5,7},{6,8},{7,9},{8,10},{9,11},{10,... | collective-permute-start | bytes 331784 | tf_op jit(solution)/shard_map/ppermute | solution.py:408
  40.3 18.5 %collective-permute-start.5 = (bf16[272,128]{1,0:T(8,128)(2,1)S(1)}, bf16[272,128]{1,0:T(8,128)(2,1)S(1)}, u32[]{:S(2)}, u32[]{:S(2)}) collective-permute-start(bf16[272,128]{1,0:T(8,128)(2,1)S(1)} %get-tuple-element.61), channel_id=1, source_target_pairs={{2,0},{3,1},{4,2},{5,3},{6,4},{7,5},{8,6},{9,7},{10,8},{11,9},{12,... | collective-permute-start | bytes 208904 | tf_op jit(solution)/shard_map/ppermute | solution.py:409
  54.4 5.2 %collective-permute-start.6 = (bf16[4,128,128]{2,1,0:T(8,128)(2,1)S(1)}, bf16[4,128,128]{2,1,0:T(8,128)(2,1)S(1)}, u32[]{:S(2)}, u32[]{:S(2)}) collective-permute-start(bf16[4,128,128]{2,1,0:T(8,128)(2,1)S(1)} %get-tuple-element.62), channel_id=1, source_target_pairs={{0,1},{1,0},{2,3},{3,2},{4,5},{5,4},{6,7},{7,6},{8,9},{9,8},{10,11... | collective-permute-start | bytes 393224 | tf_op jit(solution)/shard_map/ppermute | solution.py:410
  61.3 8.6 %collective-permute-start.8 = (bf16[24,128,128]{2,1,0:T(8,128)(2,1)}, bf16[24,128,128]{2,1,0:T(8,128)(2,1)S(1)}, u32[]{:S(2)}, u32[]{:S(2)}) collective-permute-start(bf16[24,128,128]{2,1,0:T(8,128)(2,1)} %get-tuple-element.67), channel_id=1, source_target_pairs={{0,1},{1,0},{2,3},{3,2},{4,5},{5,4},{6,7},{7,6},{8,9},{9,8},{10,11... | collective-permute-start | bytes 2359304 | tf_op jit(solution)/shard_map/ppermute | solution.py:426
  63.6 10.7 %collective-permute-start.15 = (bf16[1200,128]{1,0:T(8,128)(2,1)S(1)}, bf16[1200,128]{1,0:T(8,128)(2,1)}, u32[]{:S(2)}, u32[]{:S(2)}) collective-permute-start(bf16[1200,128]{1,0:T(8,128)(2,1)S(1)} %get-tuple-element.75), channel_id=1, source_target_pairs={{2,0},{3,1},{4,2},{5,3},{6,4},{7,5},{8,6},{9,7},{10,8},{11,9},{12,... | collective-permute-start | bytes 921608 | tf_op jit(solution)/shard_map/ppermute | solution.py:442
  68.0 12.6 %collective-permute-start.7 = (bf16[1200,128]{1,0:T(8,128)(2,1)S(1)}, bf16[1200,128]{1,0:T(8,128)(2,1)S(1)}, u32[]{:S(2)}, u32[]{:S(2)}) collective-permute-start(bf16[1200,128]{1,0:T(8,128)(2,1)S(1)} %get-tuple-element.65), channel_id=1, source_target_pairs={{0,2},{1,3},{2,4},{3,5},{4,6},{5,7},{6,8},{7,9},{8,10},{9,11},{10,... | collective-permute-start | bytes 921608 | tf_op jit(solution)/shard_map/ppermute | solution.py:442
  75.3 11.1 %collective-permute-start.16 = (bf16[1200,128]{1,0:T(8,128)(2,1)S(1)}, bf16[1200,128]{1,0:T(8,128)(2,1)S(1)}, u32[]{:S(2)}, u32[]{:S(2)}) collective-permute-start(bf16[1200,128]{1,0:T(8,128)(2,1)S(1)} %add_convert_fusion.6.refs_1_), channel_id=1, source_target_pairs={{2,0},{3,1},{4,2},{5,3},{6,4},{7,5},{8,6},{9,7},{10,8},{11,9},{12,... | collective-permute-start | bytes 921608 | tf_op jit(solution)/shard_map/ppermute | solution.py:442
  80.7 11.1 %collective-permute-start.9 = (bf16[1200,128]{1,0:T(8,128)(2,1)S(1)}, bf16[1200,128]{1,0:T(8,128)(2,1)S(1)}, u32[]{:S(2)}, u32[]{:S(2)}) collective-permute-start(bf16[1200,128]{1,0:T(8,128)(2,1)S(1)} %add_convert_fusion.13.refs_0_), channel_id=1, source_target_pairs={{0,2},{1,3},{2,4},{3,5},{4,6},{5,7},{6,8},{7,9},{8,10},{9,11},{10,... | collective-permute-start | bytes 921608 | tf_op jit(solution)/shard_map/ppermute | solution.py:442
  86.5 10.2 %collective-permute-start.17 = (bf16[1200,128]{1,0:T(8,128)(2,1)S(1)}, bf16[1200,128]{1,0:T(8,128)(2,1)S(1)}, u32[]{:S(2)}, u32[]{:S(2)}) collective-permute-start(bf16[1200,128]{1,0:T(8,128)(2,1)S(1)} %add_convert_fusion.5.refs_3_), channel_id=1, source_target_pairs={{2,0},{3,1},{4,2},{5,3},{6,4},{7,5},{8,6},{9,7},{10,8},{11,9},{12,... | collective-permute-start | bytes 921608 | tf_op jit(solution)/shard_map/ppermute | solution.py:442
  91.9 10.2 %collective-permute-start.10 = (bf16[1200,128]{1,0:T(8,128)(2,1)S(1)}, bf16[1200,128]{1,0:T(8,128)(2,1)S(1)}, u32[]{:S(2)}, u32[]{:S(2)}) collective-permute-start(bf16[1200,128]{1,0:T(8,128)(2,1)S(1)} %add_convert_fusion.12.refs_2_), channel_id=1, source_target_pairs={{0,2},{1,3},{2,4},{3,5},{4,6},{5,7},{6,8},{7,9},{8,10},{9,11},{10,... | collective-permute-start | bytes 921608 | tf_op jit(solution)/shard_map/ppermute | solution.py:442
  96.8 9.1 %collective-permute-start.18 = (bf16[1200,128]{1,0:T(8,128)(2,1)S(1)}, bf16[1200,128]{1,0:T(8,128)(2,1)S(1)}, u32[]{:S(2)}, u32[]{:S(2)}) collective-permute-start(bf16[1200,128]{1,0:T(8,128)(2,1)S(1)} %add_convert_fusion.4.refs_5_), channel_id=1, source_target_pairs={{2,0},{3,1},{4,2},{5,3},{6,4},{7,5},{8,6},{9,7},{10,8},{11,9},{12,... | collective-permute-start | bytes 921608 | tf_op jit(solution)/shard_map/ppermute | solution.py:442
  102.2 9.3 %collective-permute-start.11 = (bf16[1200,128]{1,0:T(8,128)(2,1)S(1)}, bf16[1200,128]{1,0:T(8,128)(2,1)S(1)}, u32[]{:S(2)}, u32[]{:S(2)}) collective-permute-start(bf16[1200,128]{1,0:T(8,128)(2,1)S(1)} %add_convert_fusion.11.refs_4_), channel_id=1, source_target_pairs={{0,2},{1,3},{2,4},{3,5},{4,6},{5,7},{6,8},{7,9},{8,10},{9,11},{10,... | collective-permute-start | bytes 921608 | tf_op jit(solution)/shard_map/ppermute | solution.py:442
  105.9 9.3 %collective-permute-start.19 = (bf16[1200,128]{1,0:T(8,128)(2,1)S(1)}, bf16[1200,128]{1,0:T(8,128)(2,1)S(1)}, u32[]{:S(2)}, u32[]{:S(2)}) collective-permute-start(bf16[1200,128]{1,0:T(8,128)(2,1)S(1)} %add_convert_fusion.3.refs_7_), channel_id=1, source_target_pairs={{2,0},{3,1},{4,2},{5,3},{6,4},{7,5},{8,6},{9,7},{10,8},{11,9},{12,... | collective-permute-start | bytes 921608 | tf_op jit(solution)/shard_map/ppermute | solution.py:442
  111.5 8.8 %collective-permute-start.12 = (bf16[1200,128]{1,0:T(8,128)(2,1)S(1)}, bf16[1200,128]{1,0:T(8,128)(2,1)S(1)}, u32[]{:S(2)}, u32[]{:S(2)}) collective-permute-start(bf16[1200,128]{1,0:T(8,128)(2,1)S(1)} %add_convert_fusion.10.refs_6_), channel_id=1, source_target_pairs={{0,2},{1,3},{2,4},{3,5},{4,6},{5,7},{6,8},{7,9},{8,10},{9,11},{10,... | collective-permute-start | bytes 921608 | tf_op jit(solution)/shard_map/ppermute | solution.py:442
  115.2 16.1 %copy-start.7 = (bf16[176,128]{1,0:T(8,128)(2,1)S(1)}, bf16[176,128]{1,0:T(8,128)(2,1)}, u32[]{:S(2)}) copy-start(bf16[176,128]{1,0:T(8,128)(2,1)} %copy-done.6) | copy-start | bytes 135172
  115.3 8.8 %collective-permute-start.20 = (bf16[1200,128]{1,0:T(8,128)(2,1)S(1)}, bf16[1200,128]{1,0:T(8,128)(2,1)S(1)}, u32[]{:S(2)}, u32[]{:S(2)}) collective-permute-start(bf16[1200,128]{1,0:T(8,128)(2,1)S(1)} %add_convert_fusion.2.refs_9_), channel_id=1, source_target_pairs={{2,0},{3,1},{4,2},{5,3},{6,4},{7,5},{8,6},{9,7},{10,8},{11,9},{12,... | collective-permute-start | bytes 921608 | tf_op jit(solution)/shard_map/ppermute | solution.py:442
  120.4 8.8 %collective-permute-start.13 = (bf16[1200,128]{1,0:T(8,128)(2,1)S(1)}, bf16[1200,128]{1,0:T(8,128)(2,1)S(1)}, u32[]{:S(2)}, u32[]{:S(2)}) collective-permute-start(bf16[1200,128]{1,0:T(8,128)(2,1)S(1)} %add_convert_fusion.9.refs_8_), channel_id=1, source_target_pairs={{0,2},{1,3},{2,4},{3,5},{4,6},{5,7},{6,8},{7,9},{8,10},{9,11},{10,... | collective-permute-start | bytes 921608 | tf_op jit(solution)/shard_map/ppermute | solution.py:442
  124.2 8.8 %collective-permute-start.21 = (bf16[1200,128]{1,0:T(8,128)(2,1)S(1)}, bf16[1200,128]{1,0:T(8,128)(2,1)S(1)}, u32[]{:S(2)}, u32[]{:S(2)}) collective-permute-start(bf16[1200,128]{1,0:T(8,128)(2,1)S(1)} %add_convert_fusion.1.refs_11_), channel_id=1, source_target_pairs={{2,0},{3,1},{4,2},{5,3},{6,4},{7,5},{8,6},{9,7},{10,8},{11,9},{12,... | collective-permute-start | bytes 921608 | tf_op jit(solution)/shard_map/ppermute | solution.py:442
  129.3 12.4 %collective-permute-start.14 = (bf16[1200,128]{1,0:T(8,128)(2,1)S(1)}, bf16[1200,128]{1,0:T(8,128)(2,1)S(1)}, u32[]{:S(2)}, u32[]{:S(2)}) collective-permute-start(bf16[1200,128]{1,0:T(8,128)(2,1)S(1)} %add_convert_fusion.8.refs_10_), channel_id=1, source_target_pairs={{0,2},{1,3},{2,4},{3,5},{4,6},{5,7},{6,8},{7,9},{8,10},{9,11},{10,... | collective-permute-start | bytes 921608 | tf_op jit(solution)/shard_map/ppermute | solution.py:442
  132.3 16.4 %copy-start.11 = (s32[32]{0:T(128)S(1)}, s32[32]{0:T(128)}, u32[]{:S(2)}) copy-start(s32[32]{0:T(128)} %blk.3) | copy-start | bytes 388
  133.1 17.2 %copy-start.9 = (bf16[128,128]{1,0:T(8,128)(2,1)S(1)}, bf16[128,128]{1,0:T(8,128)(2,1)}, u32[]{:S(2)}) copy-start(bf16[128,128]{1,0:T(8,128)(2,1)} %coupling.1) | copy-start | bytes 98308
  133.1 17.2 %collective-permute-start.22 = (bf16[1200,128]{1,0:T(8,128)(2,1)S(1)}, bf16[1200,128]{1,0:T(8,128)(2,1)S(1)}, u32[]{:S(2)}, u32[]{:S(2)}) collective-permute-start(bf16[1200,128]{1,0:T(8,128)(2,1)S(1)} %add_convert_fusion.refs_1_), channel_id=1, source_target_pairs={{0,1},{1,0},{2,3},{3,2},{4,5},{5,4},{6,7},{7,6},{8,9},{9,8},{10,11... | collective-permute-start | bytes 921608 | tf_op jit(solution)/shard_map/ppermute | solution.py:471
  142.1 6.5 %collective-permute-start.23 = (bf16[384,128]{1,0:T(8,128)(2,1)S(1)}, bf16[384,128]{1,0:T(8,128)(2,1)S(1)}, u32[]{:S(2)}, u32[]{:S(2)}) collective-permute-start(bf16[384,128]{1,0:T(8,128)(2,1)S(1)} %get-tuple-element.84), channel_id=1, source_target_pairs={{0,1},{1,0},{2,3},{3,2},{4,5},{5,4},{6,7},{7,6},{8,9},{9,8},{10,11... | collective-permute-start | bytes 294920 | tf_op jit(solution)/shard_map/ppermute | solution.py:472
  (7 other events, 33.7 us)

commit v4 on v2

--- a/solution.py
+++ b/solution.py
@@ -38,15 +38,15 @@
 def substeps(tall, notes, vert_inverse):
     wide = SUB
     height, breadth = tall.shape[0] - 2 * wide, tall.shape[1]
-    line = jnp.broadcast_to(notes.astype(BF), (1, wide, breadth))
+    line = jnp.broadcast_to(notes.astype(BF), (tall.shape[0], 1, breadth))
     peers = lax.axis_size("col")
     up = [(i, i + 1) for i in range(peers - 1)]
     down = [(j, i) for i, j in up]
-    left = lax.ppermute(jnp.concatenate([tall[:, breadth - wide:], line], axis=0), "col", up)
-    right = lax.ppermute(jnp.concatenate([tall[:, :wide], line], axis=0), "col", down)
-    told = jnp.where(lax.axis_index("col") % 2 == 0, right[-1, 0], left[-1, 0])
+    left = lax.ppermute(jnp.concatenate([tall[:, breadth - wide:], line], axis=1), "col", up)
+    right = lax.ppermute(jnp.concatenate([tall[:, :wide], line], axis=1), "col", down)
+    told = jnp.where(lax.axis_index("col") % 2 == 0, right[0, wide], left[0, wide])
     told = told.astype(jnp.int32)
-    current = jnp.concatenate([left[:-1], tall, right[:-1]], axis=1)
+    current = jnp.concatenate([left[:, :wide], tall, right[:, :wide]], axis=1)
     row_at = lax.axis_index(("sec", "row")) * height
     col_at = lax.axis_index("col") * breadth
     rows_all = lax.axis_size(("sec", "row")) * height
@@ -78,15 +78,12 @@
     ref[at] = (ref[at].astype(F32) + block.astype(F32)).astype(BF)
 
 
-def contrib_kernel(
-    blk, idx, atm, weight, narrow, extra,
-    sums, near_sums, far, near, rest, q,
-):
-    total, size = sums.shape[0], sums.shape[1]
+def contrib_kernel(blk, idx, atm, weight, narrow, extra, own, far, mate, q, slots):
+    total, size = slots.shape[0], slots.shape[1]
 
     @pl.loop(0, total // 8)
     def _(i):
-        sums[pl.ds(i * 8, 8)] = jnp.zeros((8,) + sums.shape[1:], BF)
+        slots[pl.ds(i * 8, 8)] = jnp.zeros((8,) + slots.shape[1:], BF)
 
     pairs = weight.shape[0]
     for p in range(0, pairs, GROUP):
@@ -104,60 +101,57 @@
         for i in range(0, GROUP, 2):
             q[pl.ds((p + i) * FIELDS, 8)] = parts[i] + parts[i + 1]
         for i in range(GROUP):
-            added(sums, idx[p + i], blocks[i])
-    n_near, n_rest = near_sums.shape[0], rest.shape[0]
-    n_slots = (far.shape[0] - q.shape[0] - extra.shape[0]) // size
-    base = total - n_near - 2 * n_slots - n_rest
-    for i in range(n_near):
-        near_sums[i] = sums[base + i]
-    base += n_near
-    for i in range(n_slots):
-        far[pl.ds(i * size, size)] = sums[base + i]
-    base += n_slots
-    for i in range(n_rest):
-        rest[i] = sums[base + i]
-    base += n_rest
-    for i in range(n_slots):
-        near[pl.ds(i * size, size)] = sums[base + i]
-    for out in (far, near):
-        out[pl.ds(n_slots * size, q.shape[0])] = q[...].astype(BF)
-        out[pl.ds(n_slots * size + q.shape[0], extra.shape[0])] = extra[...]
-
-
-def first_kernel(tab_mate, near_sums, far, near, same, other):
-    size = near_sums.shape[1]
-    blocks = near_sums.shape[0] // 2
-    payload = same.shape[0] - blocks * size
-    n_slots = (far.shape[0] - payload) // size
-    cap = n_slots // 2
-    low = tab_mate.shape[0] - n_slots
+            slots[idx[p + i]] = blocks[i]
+    base = own.shape[0] // size
+    for i in range(base):
+        own[pl.ds(i * size, size)] = slots[i]
+    for out in (far, mate):
+        count = (out.shape[0] - PAYLOAD) // size
+        for i in range(count):
+            out[pl.ds(i * size, size)] = slots[base + i]
+        out[pl.ds(count * size, q.shape[0])] = q[...].astype(BF)
+        out[pl.ds(count * size + q.shape[0], extra.shape[0])] = extra[...]
+        base += count
+
+
+def put(out, at, source, slot, size):
+    to = pl.multiple_of(at * size, size)
+    added(out, pl.ds(to, size), source[pl.ds(slot * size, size)])
+
+
+def first_kernel(table, own, far, mate, same, other, *, blocks):
+    size = (same.shape[0] - PAYLOAD) // blocks
+    n_own = own.shape[0] // size
+    n_mate = (mate.shape[0] - PAYLOAD) // size
+    n_far = (far.shape[0] - PAYLOAD) // size
+    cap = n_far // 2
     told = far[pl.ds(far.shape[0] - 16, 16)].astype(F32)[10:11]
     lane = lax.broadcasted_iota(jnp.int32, told.shape, 1)
-    for j, (out, source) in enumerate(((same, far), (other, near))):
-        for b in range(blocks):
-            out[pl.ds(b * size, size)] = near_sums[j * blocks + b]
-        out[pl.ds(blocks * size, payload)] = source[pl.ds(n_slots * size, payload)]
+    far_at = [
+        jnp.sum(jnp.where(lane == slot, told, 0.0)).astype(jnp.int32) for slot in range(n_far)
+    ]
+    for j, out, source in ((1, other, mate), (0, same, far)):
+        out[pl.ds(0, blocks * size)] = jnp.zeros((blocks * size, out.shape[1]), BF)
+        out[pl.ds(blocks * size, PAYLOAD)] = source[pl.ds(source.shape[0] - PAYLOAD, PAYLOAD)]
         for r in range(cap):
             slot = j * cap + r
-            far_at = jnp.sum(jnp.where(lane == slot, told, 0.0)).astype(jnp.int32)
-            for at, held in ((far_at, far), (tab_mate[low + slot], near)):
-                to = pl.multiple_of(lax.rem(at, blocks) * size, size)
-                added(out, pl.ds(to, size), held[pl.ds(slot * size, size)])
-
-
-def rest_kernel(tab_mate, sums, rest, *outs, cap, n_far):
-    size = sums.shape[1]
-    blocks = (outs[0].shape[0] - PAYLOAD) // size
-    payload = PAYLOAD
-    for m, out in enumerate(outs):
-        for b in range(blocks):
-            out[pl.ds(b * size, size)] = sums[m * blocks + b]
-        out[pl.ds(blocks * size, payload)] = jnp.zeros((payload, out.shape[1]), BF)
-        if m >= 2:
-            for r in range(cap):
+            low, up = n_own - n_far + slot, n_mate - n_far + slot
+            put(out, table[low], own, low, size)
+            put(out, table[n_own + up], mate, up, size)
+            put(out, lax.rem(far_at[slot], blocks), far, slot, size)
+
+
+def rest_kernel(table, own, mate, *outs, cap, blocks):
+    size = (outs[0].shape[0] - PAYLOAD) // blocks
+    n_own = own.shape[0] // size
+    for m, out in reversed(list(enumerate(outs))):
+        out[...] = jnp.zeros_like(out)
+        for r in range(cap):
+            slot = m * cap + r
+            put(out, table[slot], own, slot, size)
+            if m >= 2:
                 slot = (m - 2) * cap + r
-                to = pl.multiple_of(lax.rem(tab_mate[n_far + slot], blocks) * size, size)
-                added(out, pl.ds(to, size), rest[slot])
+                put(out, table[n_own + slot], mate, slot, size)
 
 
 def ocean_kernel(adv, state, wet, coupling, mine, swapped, out):
@@ -295,26 +289,22 @@
     wide = 2 * blocks
     n_far = 2 * cap
     n_slots = n_far + 2 * cap * (half - 1)
-    dense = half * wide
+    n_own = half * 2 * cap
     back = chips - offset
     target = jnp.where(
         offset < half,
-        offset * wide + other * blocks + local,
+        (offset * 2 + other) * cap + rank,
         jnp.where(
             offset == half,
-            dense + other * cap + rank,
-            dense + n_far + ((back - 1) * 2 + (1 - other)) * cap + rank,
+            n_own + other * cap + rank,
+            n_own + n_far + ((back - 1) * 2 + (1 - other)) * cap + rank,
         ),
     )
-    value = jnp.where(
-        offset == half,
-        other * blocks + local,
-        jnp.where(back == half - 1, 0, back * wide) + (1 - other) * blocks + local,
-    )
-    slot_at = dense + jnp.arange(n_slots)
-    table = jnp.sum(
-        jnp.where(target[:, None] == slot_at[None, :], value[:, None], 0), axis=0
+    slot_at = jnp.arange(n_own + n_slots)
+    every = jnp.sum(
+        jnp.where(target[:, None] == slot_at[None, :], local[:, None], 0), axis=0
     ).astype(jnp.int32)
+    table = every[n_own:]
 
     ocean_adv = jnp.einsum(
         "boc,cd->bod", ocean_state, ocean_mix, preferred_element_type=F32
@@ -351,7 +341,7 @@
     current, told = substeps(tall, notes, vert_inverse)
     current, ocean_adv, wet = lax.optimization_barrier((current, ocean_adv, wet))
     theirs = told[n_slots:n_slots + pairs]
-    table_mate = told[:n_slots]
+    table_mate = jnp.concatenate([every[:n_own], told[n_far:n_slots]])
 
     def blocks_of(n):
         return jax.ShapeDtypeStruct((n, breadth, channels), BF)
@@ -367,47 +357,46 @@
             flops=flops, bytes_accessed=mib * 1024 * 1024, transcendentals=0
         )
 
-    n_rest = n_slots - 2 * n_far
-    sums, near_sums, far, near, rest = pl.pallas_call(
+    n_mate = n_slots - n_far
+    own, far, mate_out = pl.pallas_call(
         contrib_kernel,
         out_shape=(
-            blocks_of(dense + n_slots),
-            blocks_of(wide),
+            rows_of(n_own * breadth),
             rows_of(n_far * breadth + PAYLOAD),
-            rows_of(n_far * breadth + PAYLOAD),
-            blocks_of(n_rest),
+            rows_of(n_mate * breadth + PAYLOAD),
         ),
         in_specs=[SM] * 2 + [VM] * 4,
-        out_specs=(VM,) * 5,
-        scratch_shapes=[pltpu.VMEM((pairs * FIELDS, breadth), F32)],
-        compiler_params=params(4),
+        out_specs=(VM,) * 3,
+        scratch_shapes=[
+            pltpu.VMEM((pairs * FIELDS, breadth), F32),
+            pltpu.VMEM((n_own + n_slots, breadth, channels), BF),
+        ],
+        compiler_params=params(6),
         cost_estimate=cost(2 * pairs * breadth * breadth * channels, 8),
     )(pair_block, target, current, pair_weight, narrow, extra)
 
     far_in = lax.ppermute(far, "col", onward)
-    near_in = lax.ppermute(near, "col", mate)
+    mate_in = lax.ppermute(mate_out, "col", mate)
 
     length = blocks * breadth + PAYLOAD
     held = pl.pallas_call(
-        first_kernel,
+        lambda *refs: first_kernel(*refs, blocks=blocks),
         out_shape=(rows_of(length),) * 2,
         in_specs=[SM, VM, VM, VM],
         out_specs=(VM,) * 2,
         compiler_params=params(4),
         cost_estimate=cost(wide * breadth * channels, 2),
-    )(table_mate, near_sums, far_in, near_in)
+    )(table_mate, own, far_in, mate_in)
     held = list(held)
 
-    rest, held[0] = lax.optimization_barrier((rest, held[0]))
-    rest = lax.ppermute(rest, "col", mate)
     here = pl.pallas_call(
-        lambda *refs: rest_kernel(*refs, cap=cap, n_far=n_far),
+        lambda *refs: rest_kernel(*refs, cap=cap, blocks=blocks),
         out_shape=(rows_of(length),) * (2 * (half - 1)),
         in_specs=[SM, VM, VM],
         out_specs=(VM,) * (2 * (half - 1)),
         compiler_params=params(4),
-        cost_estimate=cost(n_rest * breadth * channels, 4),
-    )(table_mate, sums, rest)
+        cost_estimate=cost(n_mate * breadth * channels, 4),
+    )(table_mate, own, mate_in)
 
     messages = []
     for hop in range(half - 1, 0, -1):
@@ -426,7 +415,7 @@
         out_specs=VM,
         compiler_params=params(4),
         cost_estimate=cost(len(messages) * 6 * 128 ** 3, 2),
-    )(ids, both, near, near_in, far_in, *messages[:-2])
+    )(ids, both, mate_out, mate_in, far_in, *messages[:-2])
     mine, for_mate = pl.pallas_call(
         late_kernel,
         out_shape=(

time: 145 us -> 143 us (0.986)
  the two profiles are of different devices: /device:TPU:33 before, /device:TPU:31 now
where the time goes in v4:
time: 143 us; the launch traced here: 142 us
  starting transfers between devices  101 us (71%)
  Pallas kernels  11.7 us (8%)
  waiting for transfers between devices  9.23 us (6%)
  other arithmetic  6.61 us (5%)
  local copies, waits for them, and re-layouts  6.53 us (5%)
  matrix products  6.11 us (4%)
    ppermute x14, starting transfers between devices, on_device(): came = lax.ppermute(held[j], 'col', onward)  52.9 us
    ppermute x1, starting transfers between devices, on_device(): far_in = lax.ppermute(far, 'col', onward)  18.3 us
    ppermute x1, starting transfers between devices, on_device(): swapped = lax.ppermute(held[1], 'col', mate)  9.72 us
    ppermute x2, starting transfers between devices, edges(): return (lax.ppermute(last, axis, up), lax.ppermute(first, axis, down))  7.18 us
    ppermute x1, starting transfers between devices, substeps(): lax.ppermute(jnp.concatenate([tall[:, :wide], line], axis=1), 'col', down)  4.01 us
    ppermute x14, waiting for transfers between devices, on_device(): came = lax.ppermute(held[j], 'col', onward)  3.98 us
    ppermute x1, starting transfers between devices, substeps(): lax.ppermute(jnp.concatenate([tall[:, breadth - wide:], line], axis=1), '...  3.9 us
    dot_general x3, matrix products, substeps(): jnp.einsum('hwc,cd->hwd', smooth, vert_inverse, preferred_element_type=F32)  3.81 us
  transfers between devices with their start and end apart: 22, of which 9 were waited for; matrix products, arithmetic and copies ran while one was open for 7% of the time, Pallas kernels for 4%

profile of v4, /device:TPU:31, one launch (start us, length us, event | category | flops | bytes accessed | tf_op | source)
XLA Modules:
  0.0 142.3 jit_solution(463806661263610694)
XLA Ops:
  1.7 5.3 %collective-permute-start = (bf16[3,128,128]{2,1,0:T(8,128)(2,1)S(1)}, bf16[3,128,128]{2,1,0:T(8,128)(2,1)S(1)}, u32[]{:S(2)}, u32[]{:S(2)}) collective-permute-start(bf16[3,128,128]{2,1,0:T(8,128)(2,1)S(1)} %get-tuple-element.80), channel_id=1, source_target_pairs={{0,32},{32,64},{64,96},{96,128},{128,160},{160,192},{192,224},{224... | collective-permute-start | bytes 294920 | tf_op jit(solution)/shard_map/ppermute | solution.py:30
  7.0 1.9 %collective-permute-start.1 = (bf16[3,128,128]{2,1,0:T(8,128)(2,1)S(1)}, bf16[3,128,128]{2,1,0:T(8,128)(2,1)S(1)}, u32[]{:S(2)}, u32[]{:S(2)}) collective-permute-start(bf16[3,128,128]{2,1,0:T(8,128)(2,1)S(1)} %get-tuple-element.79), channel_id=1, source_target_pairs={{32,0},{64,32},{96,64},{128,96},{160,128},{192,160},{224,192},{256... | collective-permute-start | bytes 294920 | tf_op jit(solution)/shard_map/ppermute | solution.py:30
  8.9 1.2 convolution_convert_fusion.3.adv
  16.1 4.0 %collective-permute-start.3 = (bf16[30,4,128]{2,1,0:T(4,128)(2,1)S(1)}, bf16[30,4,128]{2,1,0:T(4,128)(2,1)S(1)}, u32[]{:S(2)}, u32[]{:S(2)}) collective-permute-start(bf16[30,4,128]{2,1,0:T(4,128)(2,1)S(1)} %get-tuple-element.82), channel_id=1, source_target_pairs={{1,0},{2,1},{3,2},{4,3},{5,4},{6,5},{7,6},{8,7},{9,8},{10,9},{11,1... | collective-permute-start | bytes 92168 | tf_op jit(solution)/shard_map/ppermute | solution.py:46
  20.1 3.9 %collective-permute-start.2 = (bf16[30,4,128]{2,1,0:T(4,128)(2,1)S(1)}, bf16[30,4,128]{2,1,0:T(4,128)(2,1)S(1)}, u32[]{:S(2)}, u32[]{:S(2)}) collective-permute-start(bf16[30,4,128]{2,1,0:T(4,128)(2,1)S(1)} %get-tuple-element.81), channel_id=1, source_target_pairs={{0,1},{1,2},{2,3},{3,4},{4,5},{5,6},{6,7},{7,8},{8,9},{9,10},{10,1... | collective-permute-start | bytes 92168 | tf_op jit(solution)/shard_map/ppermute | solution.py:45
  25.3 1.7 %fusion.13 = f32[28,132,128]{2,1,0:T(8,128)S(1)} fusion(f32[30,134,128]{2,1,0:T(8,128)S(1)} %maximum_convert_fusion, pred[28,132]{1,0:T(8,128)(4,1)S(1)} %broadcast_and_fusion, bf16[128,128]{1,0:T(8,128)(2,1)S(1)} %copy-done), kind=kOutput, calls=%fused_computation.25 | convolution fusion | flops 126314496 | bytes 11681792 | tf_op jit(solution)/shard_map/hwc,cd->hwd/dot_general | solution.py:63
  27.0 1.2 fusion.15
  30.1 3.6 %shard_map.112 = (bf16[4096,128]{1,0:T(8,128)(2,1)S(1)}, bf16[688,128]{1,0:T(8,128)(2,1)S(1)}, bf16[3760,128]{1,0:T(8,128)(2,1)}) custom-call(s32[32]{0:T(128)S(1)} %copy-done.8, s32[32]{0:T(128)S(1)} %compare_select_fusion.4.idx, bf16[24,128,128]{2,1,0:T(8,128)(2,1)S(1)} %convolution_convert_fusion.2.atm, bf16[32,128,128]{2,1,0:T(8,128)(2,1)S(1)} %copy-done.1, ...), custom_call_target="tpu_custom_call" | custom-call | flops 134217728 | bytes 8388608 | tf_op jit(solution)/shard_map/pallas_call | solution.py:361
  34.5 1.9 %collective-permute-start.5 = (bf16[3760,128]{1,0:T(8,128)(2,1)}, bf16[3760,128]{1,0:T(8,128)(2,1)S(1)}, u32[]{:S(2)}, u32[]{:S(2)}) collective-permute-start(bf16[3760,128]{1,0:T(8,128)(2,1)} %get-tuple-element.56.refs_0_), channel_id=1, source_target_pairs={{0,1},{1,0},{2,3},{3,2},{4,5},{5,4},{6,7},{7,6},{8,9},{9,8},{10,11... | collective-permute-start | bytes 2887688 | tf_op jit(solution)/shard_map/ppermute | solution.py:379
  36.7 18.3 %collective-permute-start.4 = (bf16[688,128]{1,0:T(8,128)(2,1)}, bf16[688,128]{1,0:T(8,128)(2,1)S(1)}, u32[]{:S(2)}, u32[]{:S(2)}) collective-permute-start(bf16[688,128]{1,0:T(8,128)(2,1)} %copy-done.12), channel_id=1, source_target_pairs={{0,2},{1,31},{2,4},{3,1},{4,6},{5,3},{6,8},{7,5},{8,10},{9,7},{10,... | collective-permute-start | bytes 528392 | tf_op jit(solution)/shard_map/ppermute | solution.py:378
  55.1 2.5 %collective-permute-done.4.refs_2_ = bf16[688,128]{1,0:T(8,128)(2,1)S(1)} collective-permute-done((bf16[688,128]{1,0:T(8,128)(2,1)}, bf16[688,128]{1,0:T(8,128)(2,1)S(1)}, u32[]{:S(2)}, u32[]{:S(2)}) %collective-permute-start.4) | collective-permute-done | bytes 176160 | tf_op jit(solution)/shard_map/ppermute | solution.py:378
  57.6 1.4 %shard_map.113 = (bf16[1200,128]{1,0:T(8,128)(2,1)S(1)}, bf16[1200,128]{1,0:T(8,128)(2,1)}) custom-call(s32[60]{0:T(128)S(1)} %pad_add_fusion.refs_0_, bf16[4096,128]{1,0:T(8,128)(2,1)S(1)} %get-tuple-element.54.refs_1_, bf16[688,128]{1,0:T(8,128)(2,1)S(1)} %collective-permute-done.4.refs_2_, bf16[3760,128]{1,0:T(8,128)(2,1)S(1)} %collective-permute-done.5.refs_3_.refs_2_.refs_1_), custom_call_target="tpu_custom_call" | custom-call | flops 262144 | bytes 2097152 | tf_op jit(solution)/shard_map/pallas_call | solution.py:382
  60.5 4.9 %collective-permute-start.13 = (bf16[1200,128]{1,0:T(8,128)(2,1)}, bf16[1200,128]{1,0:T(8,128)(2,1)}, u32[]{:S(2)}, u32[]{:S(2)}) collective-permute-start(bf16[1200,128]{1,0:T(8,128)(2,1)} %get-tuple-element.65), channel_id=1, source_target_pairs={{0,2},{1,31},{2,4},{3,1},{4,6},{5,3},{6,8},{7,5},{8,10},{9,7},{10,... | collective-permute-start | bytes 921608 | tf_op jit(solution)/shard_map/ppermute | solution.py:404
  67.0 1.9 %collective-permute-start.6 = (bf16[1200,128]{1,0:T(8,128)(2,1)}, bf16[1200,128]{1,0:T(8,128)(2,1)S(1)}, u32[]{:S(2)}, u32[]{:S(2)}) collective-permute-start(bf16[1200,128]{1,0:T(8,128)(2,1)} %copy-done.11), channel_id=1, source_target_pairs={{0,2},{1,31},{2,4},{3,1},{4,6},{5,3},{6,8},{7,5},{8,10},{9,7},{10,... | collective-permute-start | bytes 921608 | tf_op jit(solution)/shard_map/ppermute | solution.py:404
  69.6 1.5 %shard_map.114 = (bf16[1200,128]{1,0:T(8,128)(2,1)S(1)}, bf16[1200,128]{1,0:T(8,128)(2,1)S(1)}, bf16[1200,128]{1,0:T(8,128)(2,1)S(1)}, bf16[1200,128]{1,0:T(8,12...) custom-call(s32[60]{0:T(128)S(1)} %copy-done.10, ...), custom_call_target="tpu_custom_call" | custom-call | flops 458752 | bytes 4194304 | tf_op jit(solution)/shard_map/pallas_call | solution.py:392
  72.2 3.4 %collective-permute-start.14 = (bf16[1200,128]{1,0:T(8,128)(2,1)S(1)}, bf16[1200,128]{1,0:T(8,128)(2,1)S(1)}, u32[]{:S(2)}, u32[]{:S(2)}) collective-permute-start(bf16[1200,128]{1,0:T(8,128)(2,1)S(1)} %add_convert_fusion.6.refs_3_), channel_id=1, source_target_pairs={{0,2},{1,31},{2,4},{3,1},{4,6},{5,3},{6,8},{7,5},{8,10},{9,7},{10,... | collective-permute-start | bytes 921608 | tf_op jit(solution)/shard_map/ppermute | solution.py:404
  75.7 2.4 %collective-permute-start.7 = (bf16[1200,128]{1,0:T(8,128)(2,1)S(1)}, bf16[1200,128]{1,0:T(8,128)(2,1)S(1)}, u32[]{:S(2)}, u32[]{:S(2)}) collective-permute-start(bf16[1200,128]{1,0:T(8,128)(2,1)S(1)} %add_convert_fusion.13.refs_4_), channel_id=1, source_target_pairs={{0,2},{1,31},{2,4},{3,1},{4,6},{5,3},{6,8},{7,5},{8,10},{9,7},{10,... | collective-permute-start | bytes 921608 | tf_op jit(solution)/shard_map/ppermute | solution.py:404
  78.1 2.0 %collective-permute-done.14 = bf16[1200,128]{1,0:T(8,128)(2,1)S(1)} collective-permute-done((bf16[1200,128]{1,0:T(8,128)(2,1)S(1)}, bf16[1200,128]{1,0:T(8,128)(2,1)S(1)}, u32[]{:S(2)}, u32[]{:S(2)}) %collective-permute-start.14) | collective-permute-done | bytes 307232 | tf_op jit(solution)/shard_map/ppermute | solution.py:404
  80.2 4.3 %collective-permute-start.15 = (bf16[1200,128]{1,0:T(8,128)(2,1)S(1)}, bf16[1200,128]{1,0:T(8,128)(2,1)S(1)}, u32[]{:S(2)}, u32[]{:S(2)}) collective-permute-start(bf16[1200,128]{1,0:T(8,128)(2,1)S(1)} %add_convert_fusion.5.refs_5_), channel_id=1, source_target_pairs={{0,2},{1,31},{2,4},{3,1},{4,6},{5,3},{6,8},{7,5},{8,10},{9,7},{10,... | collective-permute-start | bytes 921608 | tf_op jit(solution)/shard_map/ppermute | solution.py:404
  84.6 3.2 %collective-permute-start.8 = (bf16[1200,128]{1,0:T(8,128)(2,1)S(1)}, bf16[1200,128]{1,0:T(8,128)(2,1)S(1)}, u32[]{:S(2)}, u32[]{:S(2)}) collective-permute-start(bf16[1200,128]{1,0:T(8,128)(2,1)S(1)} %add_convert_fusion.12.refs_6_), channel_id=1, source_target_pairs={{0,2},{1,31},{2,4},{3,1},{4,6},{5,3},{6,8},{7,5},{8,10},{9,7},{10,... | collective-permute-start | bytes 921608 | tf_op jit(solution)/shard_map/ppermute | solution.py:404
  88.3 5.0 %collective-permute-start.16 = (bf16[1200,128]{1,0:T(8,128)(2,1)S(1)}, bf16[1200,128]{1,0:T(8,128)(2,1)S(1)}, u32[]{:S(2)}, u32[]{:S(2)}) collective-permute-start(bf16[1200,128]{1,0:T(8,128)(2,1)S(1)} %add_convert_fusion.4.refs_7_), channel_id=1, source_target_pairs={{0,2},{1,31},{2,4},{3,1},{4,6},{5,3},{6,8},{7,5},{8,10},{9,7},{10,... | collective-permute-start | bytes 921608 | tf_op jit(solution)/shard_map/ppermute | solution.py:404
  93.5 3.2 %collective-permute-start.9 = (bf16[1200,128]{1,0:T(8,128)(2,1)S(1)}, bf16[1200,128]{1,0:T(8,128)(2,1)S(1)}, u32[]{:S(2)}, u32[]{:S(2)}) collective-permute-start(bf16[1200,128]{1,0:T(8,128)(2,1)S(1)} %add_convert_fusion.11.refs_8_), channel_id=1, source_target_pairs={{0,2},{1,31},{2,4},{3,1},{4,6},{5,3},{6,8},{7,5},{8,10},{9,7},{10,... | collective-permute-start | bytes 921608 | tf_op jit(solution)/shard_map/ppermute | solution.py:404
  97.2 5.0 %collective-permute-start.17 = (bf16[1200,128]{1,0:T(8,128)(2,1)S(1)}, bf16[1200,128]{1,0:T(8,128)(2,1)S(1)}, u32[]{:S(2)}, u32[]{:S(2)}) collective-permute-start(bf16[1200,128]{1,0:T(8,128)(2,1)S(1)} %add_convert_fusion.3.refs_9_), channel_id=1, source_target_pairs={{0,2},{1,31},{2,4},{3,1},{4,6},{5,3},{6,8},{7,5},{8,10},{9,7},{10,... | collective-permute-start | bytes 921608 | tf_op jit(solution)/shard_map/ppermute | solution.py:404
  102.4 3.2 %collective-permute-start.10 = (bf16[1200,128]{1,0:T(8,128)(2,1)S(1)}, bf16[1200,128]{1,0:T(8,128)(2,1)S(1)}, u32[]{:S(2)}, u32[]{:S(2)}) collective-permute-start(bf16[1200,128]{1,0:T(8,128)(2,1)S(1)} %add_convert_fusion.10.refs_10_), channel_id=1, source_target_pairs={{0,2},{1,31},{2,4},{3,1},{4,6},{5,3},{6,8},{7,5},{8,10},{9,7},{10,... | collective-permute-start | bytes 921608 | tf_op jit(solution)/shard_map/ppermute | solution.py:404
  106.1 5.0 %collective-permute-start.18 = (bf16[1200,128]{1,0:T(8,128)(2,1)S(1)}, bf16[1200,128]{1,0:T(8,128)(2,1)S(1)}, u32[]{:S(2)}, u32[]{:S(2)}) collective-permute-start(bf16[1200,128]{1,0:T(8,128)(2,1)S(1)} %add_convert_fusion.2.refs_11_), channel_id=1, source_target_pairs={{0,2},{1,31},{2,4},{3,1},{4,6},{5,3},{6,8},{7,5},{8,10},{9,7},{10,... | collective-permute-start | bytes 921608 | tf_op jit(solution)/shard_map/ppermute | solution.py:404
  111.3 3.2 %collective-permute-start.11 = (bf16[1200,128]{1,0:T(8,128)(2,1)S(1)}, bf16[1200,128]{1,0:T(8,128)(2,1)S(1)}, u32[]{:S(2)}, u32[]{:S(2)}) collective-permute-start(bf16[1200,128]{1,0:T(8,128)(2,1)S(1)} %add_convert_fusion.9.refs_12_), channel_id=1, source_target_pairs={{0,2},{1,31},{2,4},{3,1},{4,6},{5,3},{6,8},{7,5},{8,10},{9,7},{10,... | collective-permute-start | bytes 921608 | tf_op jit(solution)/shard_map/ppermute | solution.py:404
  115.0 5.0 %collective-permute-start.19 = (bf16[1200,128]{1,0:T(8,128)(2,1)S(1)}, bf16[1200,128]{1,0:T(8,128)(2,1)S(1)}, u32[]{:S(2)}, u32[]{:S(2)}) collective-permute-start(bf16[1200,128]{1,0:T(8,128)(2,1)S(1)} %add_convert_fusion.1.refs_13_), channel_id=1, source_target_pairs={{0,2},{1,31},{2,4},{3,1},{4,6},{5,3},{6,8},{7,5},{8,10},{9,7},{10,... | collective-permute-start | bytes 921608 | tf_op jit(solution)/shard_map/ppermute | solution.py:404
  120.2 3.2 %collective-permute-start.12 = (bf16[1200,128]{1,0:T(8,128)(2,1)S(1)}, bf16[1200,128]{1,0:T(8,128)(2,1)S(1)}, u32[]{:S(2)}, u32[]{:S(2)}) collective-permute-start(bf16[1200,128]{1,0:T(8,128)(2,1)S(1)} %add_convert_fusion.8.refs_14_), channel_id=1, source_target_pairs={{0,2},{1,31},{2,4},{3,1},{4,6},{5,3},{6,8},{7,5},{8,10},{9,7},{10,... | collective-permute-start | bytes 921608 | tf_op jit(solution)/shard_map/ppermute | solution.py:404
  123.4 2.2 %shard_map.116.early = f32[3,256,128]{2,1,0:T(8,128)S(1)} custom-call(f32[128,1]{1,0:T(8,128)S(1)} %copy.29.ids, f32[256,1]{1,0:T(8,128)S(1)} %copy.31.both, bf16[3760,128]{1,0:T(8,128)(2,1)} %get-tuple-element.56.refs_0_, bf16[3760,128]{1,0:T(8,128)(2,1)S(1)} %collective-permute-done.5.refs_3_.refs_2_.refs_1_, bf16[688,128]{1,0:T(8,128)(2,1)S(1)} %copy-done.6, ...), custom_call_target="tpu_custom_call" | custom-call | flops 176160768 | bytes 2097152 | tf_op jit(solution)/shard_map/pallas_call | solution.py:411
  125.7 9.7 %collective-permute-start.20 = (bf16[1200,128]{1,0:T(8,128)(2,1)S(1)}, bf16[1200,128]{1,0:T(8,128)(2,1)S(1)}, u32[]{:S(2)}, u32[]{:S(2)}) collective-permute-start(bf16[1200,128]{1,0:T(8,128)(2,1)S(1)} %add_convert_fusion.refs_0_), channel_id=1, source_target_pairs={{0,1},{1,0},{2,3},{3,2},{4,5},{5,4},{6,7},{7,6},{8,9},{9,8},{10,11... | collective-permute-start | bytes 921608 | tf_op jit(solution)/shard_map/ppermute | solution.py:431
  135.8 3.0 %collective-permute-start.21 = (bf16[384,128]{1,0:T(8,128)(2,1)S(1)}, bf16[384,128]{1,0:T(8,128)(2,1)S(1)}, u32[]{:S(2)}, u32[]{:S(2)}) collective-permute-start(bf16[384,128]{1,0:T(8,128)(2,1)S(1)} %get-tuple-element.74), channel_id=1, source_target_pairs={{0,1},{1,0},{2,3},{3,2},{4,5},{5,4},{6,7},{7,6},{8,9},{9,8},{10,11... | collective-permute-start | bytes 294920 | tf_op jit(solution)/shard_map/ppermute | solution.py:432
  139.8 1.6 %shard_map.118 = f32[4,24,128]{2,1,0:T(8,128)} custom-call(s32[32]{0:T(128)S(1)} %copy-done.8, f32[3,128,128]{2,1,0:T(8,128)S(1)} %get-tuple-element.73.mine, bf16[384,128]{1,0:T(8,128)(2,1)S(1)} %collective-permute-done.21.mate, bf16[32,128,128]{2,1,0:T(8,128)(2,1)S(1)} %copy-done.1), custom_call_target="tpu_custom_call" | custom-call | flops 8388608 | bytes 2097152 | tf_op jit(solution)/shard_map/pallas_call | solution.py:442
  (111 shorter events, 21.2 us)
Async XLA Ops:
  0.6 24.7 %copy-start = (bf16[128,128]{1,0:T(8,128)(2,1)S(1)}, bf16[128,128]{1,0:T(8,128)(2,1)}, u32[]{:S(2)}) copy-start(bf16[128,128]{1,0:T(8,128)(2,1)} %param.14) | copy-start | bytes 98308
  0.6 14.1 %copy-start.13 = (bf16[24,128,128]{2,1,0:T(8,128)(2,1)S(1)}, bf16[24,128,128]{2,1,0:T(8,128)(2,1)}, u32[]{:S(2)}) copy-start(bf16[24,128,128]{2,1,0:T(8,128)(2,1)} %param.13) | copy-start | bytes 2359300
  1.7 13.0 %collective-permute-start = (bf16[3,128,128]{2,1,0:T(8,128)(2,1)S(1)}, bf16[3,128,128]{2,1,0:T(8,128)(2,1)S(1)}, u32[]{:S(2)}, u32[]{:S(2)}) collective-permute-start(bf16[3,128,128]{2,1,0:T(8,128)(2,1)S(1)} %get-tuple-element.80), channel_id=1, source_target_pairs={{0,32},{32,64},{64,96},{96,128},{128,160},{160,192},{192,224},{224... | collective-permute-start | bytes 294920 | tf_op jit(solution)/shard_map/ppermute | solution.py:30
  7.0 9.0 %collective-permute-start.1 = (bf16[3,128,128]{2,1,0:T(8,128)(2,1)S(1)}, bf16[3,128,128]{2,1,0:T(8,128)(2,1)S(1)}, u32[]{:S(2)}, u32[]{:S(2)}) collective-permute-start(bf16[3,128,128]{2,1,0:T(8,128)(2,1)S(1)} %get-tuple-element.79), channel_id=1, source_target_pairs={{32,0},{64,32},{96,64},{128,96},{160,128},{192,160},{224,192},{256... | collective-permute-start | bytes 294920 | tf_op jit(solution)/shard_map/ppermute | solution.py:30
  16.1 8.2 %collective-permute-start.3 = (bf16[30,4,128]{2,1,0:T(4,128)(2,1)S(1)}, bf16[30,4,128]{2,1,0:T(4,128)(2,1)S(1)}, u32[]{:S(2)}, u32[]{:S(2)}) collective-permute-start(bf16[30,4,128]{2,1,0:T(4,128)(2,1)S(1)} %get-tuple-element.82), channel_id=1, source_target_pairs={{1,0},{2,1},{3,2},{4,3},{5,4},{6,5},{7,6},{8,7},{9,8},{10,9},{11,1... | collective-permute-start | bytes 92168 | tf_op jit(solution)/shard_map/ppermute | solution.py:46
  20.1 4.9 %collective-permute-start.2 = (bf16[30,4,128]{2,1,0:T(4,128)(2,1)S(1)}, bf16[30,4,128]{2,1,0:T(4,128)(2,1)S(1)}, u32[]{:S(2)}, u32[]{:S(2)}) collective-permute-start(bf16[30,4,128]{2,1,0:T(4,128)(2,1)S(1)} %get-tuple-element.81), channel_id=1, source_target_pairs={{0,1},{1,2},{2,3},{3,4},{4,5},{5,6},{6,7},{7,8},{8,9},{9,10},{10,1... | collective-permute-start | bytes 92168 | tf_op jit(solution)/shard_map/ppermute | solution.py:45
  28.2 1.9 %copy-start.1 = (bf16[32,128,128]{2,1,0:T(8,128)(2,1)S(1)}, bf16[32,128,128]{2,1,0:T(8,128)(2,1)}, u32[]{:S(2)}) copy-start(bf16[32,128,128]{2,1,0:T(8,128)(2,1)} %weight.3) | copy-start | bytes 3145732
  29.2 4.6 %copy-start.4 = (bf16[24,128,128]{2,1,0:T(8,128)(2,1)}, bf16[24,128,128]{2,1,0:T(8,128)(2,1)S(1)}, u32[]{:S(2)}) copy-start(bf16[24,128,128]{2,1,0:T(8,128)(2,1)S(1)} %convolution_convert_fusion.2.atm) | copy-start | bytes 2359300
  29.2 25.9 %copy-start.14 = (s32[32]{0:T(128)S(1)}, s32[32]{0:T(128)}, u32[]{:S(2)}) copy-start(s32[32]{0:T(128)} %get-tuple-element.86) | copy-start | bytes 388
  34.5 23.2 %collective-permute-start.5 = (bf16[3760,128]{1,0:T(8,128)(2,1)}, bf16[3760,128]{1,0:T(8,128)(2,1)S(1)}, u32[]{:S(2)}, u32[]{:S(2)}) collective-permute-start(bf16[3760,128]{1,0:T(8,128)(2,1)} %get-tuple-element.56.refs_0_), channel_id=1, source_target_pairs={{0,1},{1,0},{2,3},{3,2},{4,5},{5,4},{6,7},{7,6},{8,9},{9,8},{10,11... | collective-permute-start | bytes 2887688 | tf_op jit(solution)/shard_map/ppermute | solution.py:379
  36.7 21.0 %collective-permute-start.4 = (bf16[688,128]{1,0:T(8,128)(2,1)}, bf16[688,128]{1,0:T(8,128)(2,1)S(1)}, u32[]{:S(2)}, u32[]{:S(2)}) collective-permute-start(bf16[688,128]{1,0:T(8,128)(2,1)} %copy-done.12), channel_id=1, source_target_pairs={{0,2},{1,31},{2,4},{3,1},{4,6},{5,3},{6,8},{7,5},{8,10},{9,7},{10,... | collective-permute-start | bytes 528392 | tf_op jit(solution)/shard_map/ppermute | solution.py:378
  55.1 10.5 %copy-start.9 = (s32[60]{0:T(128)}, s32[60]{0:T(128)S(1)}, u32[]{:S(2)}) copy-start(s32[60]{0:T(128)S(1)} %pad_add_fusion.refs_0_) | copy-start | bytes 724
  60.5 10.6 %collective-permute-start.13 = (bf16[1200,128]{1,0:T(8,128)(2,1)}, bf16[1200,128]{1,0:T(8,128)(2,1)}, u32[]{:S(2)}, u32[]{:S(2)}) collective-permute-start(bf16[1200,128]{1,0:T(8,128)(2,1)} %get-tuple-element.65), channel_id=1, source_target_pairs={{0,2},{1,31},{2,4},{3,1},{4,6},{5,3},{6,8},{7,5},{8,10},{9,7},{10,... | collective-permute-start | bytes 921608 | tf_op jit(solution)/shard_map/ppermute | solution.py:404
  67.0 8.5 %collective-permute-start.6 = (bf16[1200,128]{1,0:T(8,128)(2,1)}, bf16[1200,128]{1,0:T(8,128)(2,1)S(1)}, u32[]{:S(2)}, u32[]{:S(2)}) collective-permute-start(bf16[1200,128]{1,0:T(8,128)(2,1)} %copy-done.11), channel_id=1, source_target_pairs={{0,2},{1,31},{2,4},{3,1},{4,6},{5,3},{6,8},{7,5},{8,10},{9,7},{10,... | collective-permute-start | bytes 921608 | tf_op jit(solution)/shard_map/ppermute | solution.py:404
  72.2 7.9 %collective-permute-start.14 = (bf16[1200,128]{1,0:T(8,128)(2,1)S(1)}, bf16[1200,128]{1,0:T(8,128)(2,1)S(1)}, u32[]{:S(2)}, u32[]{:S(2)}) collective-permute-start(bf16[1200,128]{1,0:T(8,128)(2,1)S(1)} %add_convert_fusion.6.refs_3_), channel_id=1, source_target_pairs={{0,2},{1,31},{2,4},{3,1},{4,6},{5,3},{6,8},{7,5},{8,10},{9,7},{10,... | collective-permute-start | bytes 921608 | tf_op jit(solution)/shard_map/ppermute | solution.py:404
  75.7 8.8 %collective-permute-start.7 = (bf16[1200,128]{1,0:T(8,128)(2,1)S(1)}, bf16[1200,128]{1,0:T(8,128)(2,1)S(1)}, u32[]{:S(2)}, u32[]{:S(2)}) collective-permute-start(bf16[1200,128]{1,0:T(8,128)(2,1)S(1)} %add_convert_fusion.13.refs_4_), channel_id=1, source_target_pairs={{0,2},{1,31},{2,4},{3,1},{4,6},{5,3},{6,8},{7,5},{8,10},{9,7},{10,... | collective-permute-start | bytes 921608 | tf_op jit(solution)/shard_map/ppermute | solution.py:404
  80.2 8.1 %collective-permute-start.15 = (bf16[1200,128]{1,0:T(8,128)(2,1)S(1)}, bf16[1200,128]{1,0:T(8,128)(2,1)S(1)}, u32[]{:S(2)}, u32[]{:S(2)}) collective-permute-start(bf16[1200,128]{1,0:T(8,128)(2,1)S(1)} %add_convert_fusion.5.refs_5_), channel_id=1, source_target_pairs={{0,2},{1,31},{2,4},{3,1},{4,6},{5,3},{6,8},{7,5},{8,10},{9,7},{10,... | collective-permute-start | bytes 921608 | tf_op jit(solution)/shard_map/ppermute | solution.py:404
  84.6 8.8 %collective-permute-start.8 = (bf16[1200,128]{1,0:T(8,128)(2,1)S(1)}, bf16[1200,128]{1,0:T(8,128)(2,1)S(1)}, u32[]{:S(2)}, u32[]{:S(2)}) collective-permute-start(bf16[1200,128]{1,0:T(8,128)(2,1)S(1)} %add_convert_fusion.12.refs_6_), channel_id=1, source_target_pairs={{0,2},{1,31},{2,4},{3,1},{4,6},{5,3},{6,8},{7,5},{8,10},{9,7},{10,... | collective-permute-start | bytes 921608 | tf_op jit(solution)/shard_map/ppermute | solution.py:404
  88.3 8.8 %collective-permute-start.16 = (bf16[1200,128]{1,0:T(8,128)(2,1)S(1)}, bf16[1200,128]{1,0:T(8,128)(2,1)S(1)}, u32[]{:S(2)}, u32[]{:S(2)}) collective-permute-start(bf16[1200,128]{1,0:T(8,128)(2,1)S(1)} %add_convert_fusion.4.refs_7_), channel_id=1, source_target_pairs={{0,2},{1,31},{2,4},{3,1},{4,6},{5,3},{6,8},{7,5},{8,10},{9,7},{10,... | collective-permute-start | bytes 921608 | tf_op jit(solution)/shard_map/ppermute | solution.py:404
  93.5 8.8 %collective-permute-start.9 = (bf16[1200,128]{1,0:T(8,128)(2,1)S(1)}, bf16[1200,128]{1,0:T(8,128)(2,1)S(1)}, u32[]{:S(2)}, u32[]{:S(2)}) collective-permute-start(bf16[1200,128]{1,0:T(8,128)(2,1)S(1)} %add_convert_fusion.11.refs_8_), channel_id=1, source_target_pairs={{0,2},{1,31},{2,4},{3,1},{4,6},{5,3},{6,8},{7,5},{8,10},{9,7},{10,... | collective-permute-start | bytes 921608 | tf_op jit(solution)/shard_map/ppermute | solution.py:404
  97.2 8.8 %collective-permute-start.17 = (bf16[1200,128]{1,0:T(8,128)(2,1)S(1)}, bf16[1200,128]{1,0:T(8,128)(2,1)S(1)}, u32[]{:S(2)}, u32[]{:S(2)}) collective-permute-start(bf16[1200,128]{1,0:T(8,128)(2,1)S(1)} %add_convert_fusion.3.refs_9_), channel_id=1, source_target_pairs={{0,2},{1,31},{2,4},{3,1},{4,6},{5,3},{6,8},{7,5},{8,10},{9,7},{10,... | collective-permute-start | bytes 921608 | tf_op jit(solution)/shard_map/ppermute | solution.py:404
  102.4 8.8 %collective-permute-start.10 = (bf16[1200,128]{1,0:T(8,128)(2,1)S(1)}, bf16[1200,128]{1,0:T(8,128)(2,1)S(1)}, u32[]{:S(2)}, u32[]{:S(2)}) collective-permute-start(bf16[1200,128]{1,0:T(8,128)(2,1)S(1)} %add_convert_fusion.10.refs_10_), channel_id=1, source_target_pairs={{0,2},{1,31},{2,4},{3,1},{4,6},{5,3},{6,8},{7,5},{8,10},{9,7},{10,... | collective-permute-start | bytes 921608 | tf_op jit(solution)/shard_map/ppermute | solution.py:404
  106.0 17.3 %copy-start.6 = (bf16[688,128]{1,0:T(8,128)(2,1)S(1)}, bf16[688,128]{1,0:T(8,128)(2,1)}, u32[]{:S(2)}) copy-start(bf16[688,128]{1,0:T(8,128)(2,1)} %copy-done.5) | copy-start | bytes 528388
  106.1 8.8 %collective-permute-start.18 = (bf16[1200,128]{1,0:T(8,128)(2,1)S(1)}, bf16[1200,128]{1,0:T(8,128)(2,1)S(1)}, u32[]{:S(2)}, u32[]{:S(2)}) collective-permute-start(bf16[1200,128]{1,0:T(8,128)(2,1)S(1)} %add_convert_fusion.2.refs_11_), channel_id=1, source_target_pairs={{0,2},{1,31},{2,4},{3,1},{4,6},{5,3},{6,8},{7,5},{8,10},{9,7},{10,... | collective-permute-start | bytes 921608 | tf_op jit(solution)/shard_map/ppermute | solution.py:404
  111.3 8.8 %collective-permute-start.11 = (bf16[1200,128]{1,0:T(8,128)(2,1)S(1)}, bf16[1200,128]{1,0:T(8,128)(2,1)S(1)}, u32[]{:S(2)}, u32[]{:S(2)}) collective-permute-start(bf16[1200,128]{1,0:T(8,128)(2,1)S(1)} %add_convert_fusion.9.refs_12_), channel_id=1, source_target_pairs={{0,2},{1,31},{2,4},{3,1},{4,6},{5,3},{6,8},{7,5},{8,10},{9,7},{10,... | collective-permute-start | bytes 921608 | tf_op jit(solution)/shard_map/ppermute | solution.py:404
  115.0 10.5 %collective-permute-start.19 = (bf16[1200,128]{1,0:T(8,128)(2,1)S(1)}, bf16[1200,128]{1,0:T(8,128)(2,1)S(1)}, u32[]{:S(2)}, u32[]{:S(2)}) collective-permute-start(bf16[1200,128]{1,0:T(8,128)(2,1)S(1)} %add_convert_fusion.1.refs_13_), channel_id=1, source_target_pairs={{0,2},{1,31},{2,4},{3,1},{4,6},{5,3},{6,8},{7,5},{8,10},{9,7},{10,... | collective-permute-start | bytes 921608 | tf_op jit(solution)/shard_map/ppermute | solution.py:404
  120.2 15.2 %collective-permute-start.12 = (bf16[1200,128]{1,0:T(8,128)(2,1)S(1)}, bf16[1200,128]{1,0:T(8,128)(2,1)S(1)}, u32[]{:S(2)}, u32[]{:S(2)}) collective-permute-start(bf16[1200,128]{1,0:T(8,128)(2,1)S(1)} %add_convert_fusion.8.refs_14_), channel_id=1, source_target_pairs={{0,2},{1,31},{2,4},{3,1},{4,6},{5,3},{6,8},{7,5},{8,10},{9,7},{10,... | collective-permute-start | bytes 921608 | tf_op jit(solution)/shard_map/ppermute | solution.py:404
  125.6 15.7 %copy-start.2 = (bf16[8,128,128]{2,1,0:T(8,128)(2,1)S(1)}, bf16[8,128,128]{2,1,0:T(8,128)(2,1)}, u32[]{:S(2)}) copy-start(bf16[8,128,128]{2,1,0:T(8,128)(2,1)} %state.1) | copy-start | bytes 786436
  125.6 15.7 %copy-start.3 = (bf16[8,128,128]{2,1,0:T(8,128)(2,1)S(1)}, bf16[8,128,128]{2,1,0:T(8,128)(2,1)}, u32[]{:S(2)}) copy-start(bf16[8,128,128]{2,1,0:T(8,128)(2,1)} %broadcast_in_dim.54.wet) | copy-start | bytes 786436
  125.7 15.7 %copy-start.7 = (bf16[128,128]{1,0:T(8,128)(2,1)S(1)}, bf16[128,128]{1,0:T(8,128)(2,1)}, u32[]{:S(2)}) copy-start(bf16[128,128]{1,0:T(8,128)(2,1)} %coupling.1) | copy-start | bytes 98308
  125.7 15.7 %collective-permute-start.20 = (bf16[1200,128]{1,0:T(8,128)(2,1)S(1)}, bf16[1200,128]{1,0:T(8,128)(2,1)S(1)}, u32[]{:S(2)}, u32[]{:S(2)}) collective-permute-start(bf16[1200,128]{1,0:T(8,128)(2,1)S(1)} %add_convert_fusion.refs_0_), channel_id=1, source_target_pairs={{0,1},{1,0},{2,3},{3,2},{4,5},{5,4},{6,7},{7,6},{8,9},{9,8},{10,11... | collective-permute-start | bytes 921608 | tf_op jit(solution)/shard_map/ppermute | solution.py:431
  135.8 3.9 %collective-permute-start.21 = (bf16[384,128]{1,0:T(8,128)(2,1)S(1)}, bf16[384,128]{1,0:T(8,128)(2,1)S(1)}, u32[]{:S(2)}, u32[]{:S(2)}) collective-permute-start(bf16[384,128]{1,0:T(8,128)(2,1)S(1)} %get-tuple-element.74), channel_id=1, source_target_pairs={{0,1},{1,0},{2,3},{3,2},{4,5},{5,4},{6,7},{7,6},{8,9},{9,8},{10,11... | collective-permute-start | bytes 294920 | tf_op jit(solution)/shard_map/ppermute | solution.py:432
  (5 other events, 4.6 us)

commit v5 on v4

--- a/solution.py
+++ b/solution.py
@@ -194,27 +194,34 @@
     )
 
 
-def early_kernel(ids, both, *refs):
-    local, messages, out = refs[:2], refs[2:-1], refs[-1]
-    rows, lanes = ids.shape[0], out.shape[2]
+def early_kernel(own, theirs, *refs):
+    messages, out = refs[:-1], refs[-1]
+    rows, lanes = out.shape[1] // 2, out.shape[2]
+    eye = lax.broadcasted_iota(jnp.int32, (rows, lanes), 0) == lax.broadcasted_iota(
+        jnp.int32, (rows, lanes), 1
+    )
+    for i, message in enumerate((own, theirs)):
+        row = message[pl.ds(message.shape[0] - 16, 16)].astype(F32)[8:9]
+        down = jnp.sum(jnp.where(eye, row, 0.0), axis=1, keepdims=True)
+        out[3, pl.ds(i * rows, rows)] = jnp.broadcast_to(down, (rows, lanes))
     zero = jnp.zeros((rows, lanes), F32)
     mine = (zero,) * 3
-    for message in local:
-        mine = picked(ids[...], message, mine)
+    for message in (own, theirs):
+        mine = picked(out[3, pl.ds(0, rows)], message, mine)
     for i in range(3):
         out[i, pl.ds(0, rows)] = mine[i]
         out[i, pl.ds(rows, rows)] = zero
     for message in messages:
-        sums = picked(both[...], message, tuple(out[i] for i in range(3)))
+        sums = picked(out[3], message, tuple(out[i] for i in range(3)))
         for i in range(3):
             out[i] = sums[i]
 
 
-def late_kernel(both, early, *refs):
+def late_kernel(early, *refs):
     messages, mine, mate = refs[:-2], refs[-2], refs[-1]
     sums = tuple(early[i] for i in range(3))
     for message in messages:
-        sums = picked(both[...], message, sums)
+        sums = picked(early[3], message, sums)
     rows = mine.shape[1]
     for i in range(3):
         mine[i] = sums[i][:rows]
@@ -336,11 +343,10 @@
     )
     tall = tall_patch(atm_state)
     notes = jnp.concatenate(
-        [table, pair_ocean, jnp.zeros((breadth - n_slots - pairs,), jnp.int32)]
+        [table, jnp.zeros((breadth - n_slots,), jnp.int32)]
     )
     current, told = substeps(tall, notes, vert_inverse)
-    current, ocean_adv, wet = lax.optimization_barrier((current, ocean_adv, wet))
-    theirs = told[n_slots:n_slots + pairs]
+    current, ocean_adv = lax.optimization_barrier((current, ocean_adv))
     table_mate = jnp.concatenate([every[:n_own], told[n_far:n_slots]])
 
     def blocks_of(n):
@@ -348,9 +354,6 @@
 
     def rows_of(n, dtype=BF):
         return jax.ShapeDtypeStruct((n, breadth), dtype)
-
-    def column(ids):
-        return jnp.broadcast_to(ids[:, None], (pairs, FIELDS)).reshape(pairs * FIELDS, 1)
 
     def cost(flops, mib):
         return pl.CostEstimate(
@@ -406,27 +409,26 @@
             held[j] = total.astype(BF)
             messages.append(held[j])
 
-    ids = column(pair_ocean.astype(F32))
-    both = jnp.concatenate([ids, column(theirs.astype(F32))], axis=0)
     early = pl.pallas_call(
         early_kernel,
-        out_shape=jax.ShapeDtypeStruct((3, 2 * pairs * FIELDS, breadth), F32),
-        in_specs=[VM] * (2 + 3 + len(messages) - 2),
+        out_shape=jax.ShapeDtypeStruct((4, 2 * pairs * FIELDS, breadth), F32),
+        in_specs=[VM] * (3 + len(messages) - 2),
         out_specs=VM,
         compiler_params=params(4),
         cost_estimate=cost(len(messages) * 6 * 128 ** 3, 2),
-    )(ids, both, mate_out, mate_in, far_in, *messages[:-2])
+    )(mate_out, mate_in, far_in, *messages[:-2])
+    early, wet = lax.optimization_barrier((early, wet))
     mine, for_mate = pl.pallas_call(
         late_kernel,
         out_shape=(
             jax.ShapeDtypeStruct((3, pairs * FIELDS, breadth), F32),
             rows_of(3 * pairs * FIELDS),
         ),
-        in_specs=[VM] * 4,
+        in_specs=[VM] * 3,
         out_specs=(VM,) * 2,
         compiler_params=params(4),
         cost_estimate=cost(12 * 128 ** 3, 1),
-    )(both, early, *messages[-2:])
+    )(early, *messages[-2:])
 
     swapped = lax.ppermute(held[1], "col", mate)
     from_mate = lax.ppermute(for_mate, "col", mate)

time: 143 us -> 138 us (0.965)
  local copies, waits for them, and re-layouts: 6.53 us -> 2.13 us
  starting transfers between devices: 101 us -> 104 us
  waiting for transfers between devices: 9.23 us -> 7.51 us
  other arithmetic: 6.61 us -> 5.17 us
    ppermute x14, starting transfers between devices: 52.9 us -> 56.2 us  [on_device(): came = lax.ppermute(held[j], 'col', onward)]
    unnamed x33 -> x21, local copies, waits for them, and re-layouts: 2.89 us -> 0.5 us
  transfers between devices with their start and end apart: 22 -> 22, of which waited for: 9 -> 10; matrix products, arithmetic and copies ran while one was open for 7% -> 6% of each run, Pallas kernels for 4% -> 4%
where the time goes in v5:
time: 138 us; the launch traced here: 137 us
  starting transfers between devices  104 us (75%)
  Pallas kernels  11 us (8%)
  waiting for transfers between devices  7.51 us (5%)
  matrix products  6.11 us (4%)
  other arithmetic  5.17 us (4%)
  local copies, waits for them, and re-layouts  2.13 us (2%)
    ppermute x14, starting transfers between devices, on_device(): came = lax.ppermute(held[j], 'col', onward)  56.2 us
    ppermute x1, starting transfers between devices, on_device(): far_in = lax.ppermute(far, 'col', onward)  18.3 us
    ppermute x1, starting transfers between devices, on_device(): swapped = lax.ppermute(held[1], 'col', mate)  9.45 us
    ppermute x2, starting transfers between devices, edges(): return (lax.ppermute(last, axis, up), lax.ppermute(first, axis, down))  7.18 us
    ppermute x1, starting transfers between devices, substeps(): lax.ppermute(jnp.concatenate([tall[:, :wide], line], axis=1), 'col', down)  4.01 us
    ppermute x1, starting transfers between devices, substeps(): lax.ppermute(jnp.concatenate([tall[:, breadth - wide:], line], axis=1), '...  3.9 us
    dot_general x3, matrix products, substeps(): jnp.einsum('hwc,cd->hwd', smooth, vert_inverse, preferred_element_type=F32)  3.81 us
    pallas_call x1, Pallas kernels, on_device(): pl.pallas_call(contrib_kernel, out_shape=(rows_of(n_own * breadth), rows_...  3.65 us
  transfers between devices with their start and end apart: 22, of which 10 were waited for; matrix products, arithmetic and copies ran while one was open for 6% of the time, Pallas kernels for 4%

profile of v5, /device:TPU:31, one launch (start us, length us, event | category | flops | bytes accessed | tf_op | source)
XLA Modules:
  0.0 137.1 jit_solution(4774060799744927222)
XLA Ops:
  1.7 5.3 %collective-permute-start = (bf16[3,128,128]{2,1,0:T(8,128)(2,1)S(1)}, bf16[3,128,128]{2,1,0:T(8,128)(2,1)S(1)}, u32[]{:S(2)}, u32[]{:S(2)}) collective-permute-start(bf16[3,128,128]{2,1,0:T(8,128)(2,1)S(1)} %get-tuple-element.82), channel_id=1, source_target_pairs={{0,32},{32,64},{64,96},{96,128},{128,160},{160,192},{192,224},{224... | collective-permute-start | bytes 294920 | tf_op jit(solution)/shard_map/ppermute | solution.py:30
  7.0 1.9 %collective-permute-start.1 = (bf16[3,128,128]{2,1,0:T(8,128)(2,1)S(1)}, bf16[3,128,128]{2,1,0:T(8,128)(2,1)S(1)}, u32[]{:S(2)}, u32[]{:S(2)}) collective-permute-start(bf16[3,128,128]{2,1,0:T(8,128)(2,1)S(1)} %get-tuple-element.81), channel_id=1, source_target_pairs={{32,0},{64,32},{96,64},{128,96},{160,128},{192,160},{224,192},{256... | collective-permute-start | bytes 294920 | tf_op jit(solution)/shard_map/ppermute | solution.py:30
  8.9 1.2 convolution_convert_fusion.3.adv
  10.1 1.1 convolution_convert_fusion.4
  14.3 1.6 %collective-permute-done.1 = bf16[3,128,128]{2,1,0:T(8,128)(2,1)S(1)} collective-permute-done((bf16[3,128,128]{2,1,0:T(8,128)(2,1)S(1)}, bf16[3,128,128]{2,1,0:T(8,128)(2,1)S(1)}, u32[]{:S(2)}, u32[]{:S(2)}) %collective-permute-start.1) | collective-permute-done | bytes 98336 | tf_op jit(solution)/shard_map/ppermute | solution.py:30
  16.1 4.0 %collective-permute-start.3 = (bf16[30,4,128]{2,1,0:T(4,128)(2,1)S(1)}, bf16[30,4,128]{2,1,0:T(4,128)(2,1)S(1)}, u32[]{:S(2)}, u32[]{:S(2)}) collective-permute-start(bf16[30,4,128]{2,1,0:T(4,128)(2,1)S(1)} %get-tuple-element.84), channel_id=1, source_target_pairs={{1,0},{2,1},{3,2},{4,3},{5,4},{6,5},{7,6},{8,7},{9,8},{10,9},{11,1... | collective-permute-start | bytes 92168 | tf_op jit(solution)/shard_map/ppermute | solution.py:46
  20.1 3.9 %collective-permute-start.2 = (bf16[30,4,128]{2,1,0:T(4,128)(2,1)S(1)}, bf16[30,4,128]{2,1,0:T(4,128)(2,1)S(1)}, u32[]{:S(2)}, u32[]{:S(2)}) collective-permute-start(bf16[30,4,128]{2,1,0:T(4,128)(2,1)S(1)} %get-tuple-element.83), channel_id=1, source_target_pairs={{0,1},{1,2},{2,3},{3,4},{4,5},{5,6},{6,7},{7,8},{8,9},{9,10},{10,1... | collective-permute-start | bytes 92168 | tf_op jit(solution)/shard_map/ppermute | solution.py:45
  25.3 1.7 %fusion.13 = f32[28,132,128]{2,1,0:T(8,128)S(1)} fusion(f32[30,134,128]{2,1,0:T(8,128)S(1)} %maximum_convert_fusion, pred[28,132]{1,0:T(8,128)(4,1)S(1)} %broadcast_and_fusion, bf16[128,128]{1,0:T(8,128)(2,1)S(1)} %copy-done), kind=kOutput, calls=%fused_computation.25 | convolution fusion | flops 126314496 | bytes 11681792 | tf_op jit(solution)/shard_map/hwc,cd->hwd/dot_general | solution.py:63
  27.0 1.2 fusion.15
  29.5 3.7 %shard_map.112 = (bf16[4096,128]{1,0:T(8,128)(2,1)S(1)}, bf16[688,128]{1,0:T(8,128)(2,1)S(1)}, bf16[3760,128]{1,0:T(8,128)(2,1)}) custom-call(s32[32]{0:T(128)S(1)} %copy-done.5, s32[32]{0:T(128)S(1)} %compare_select_fusion.4.idx, bf16[24,128,128]{2,1,0:T(8,128)(2,1)S(1)} %convolution_convert_fusion.2.atm, bf16[32,128,128]{2,1,0:T(8,128)(2,1)S(1)} %copy-done.1, ...), custom_call_target="tpu_custom_call" | custom-call | flops 134217728 | bytes 8388608 | tf_op jit(solution)/shard_map/pallas_call | solution.py:364
  33.2 1.9 %collective-permute-start.4 = (bf16[3760,128]{1,0:T(8,128)(2,1)}, bf16[3760,128]{1,0:T(8,128)(2,1)S(1)}, u32[]{:S(2)}, u32[]{:S(2)}) collective-permute-start(bf16[3760,128]{1,0:T(8,128)(2,1)} %get-tuple-element.54.own), channel_id=1, source_target_pairs={{0,1},{1,0},{2,3},{3,2},{4,5},{5,4},{6,7},{7,6},{8,9},{9,8},{10,11... | collective-permute-start | bytes 2887688 | tf_op jit(solution)/shard_map/ppermute | solution.py:382
  35.1 18.3 %collective-permute-start.5 = (bf16[688,128]{1,0:T(8,128)(2,1)S(1)}, bf16[688,128]{1,0:T(8,128)(2,1)S(1)}, u32[]{:S(2)}, u32[]{:S(2)}) collective-permute-start(bf16[688,128]{1,0:T(8,128)(2,1)S(1)} %get-tuple-element.55), channel_id=1, source_target_pairs={{0,2},{1,31},{2,4},{3,1},{4,6},{5,3},{6,8},{7,5},{8,10},{9,7},{10,... | collective-permute-start | bytes 528392 | tf_op jit(solution)/shard_map/ppermute | solution.py:381
  54.2 1.5 %collective-permute-done.5.refs_2_.refs_0_ = bf16[688,128]{1,0:T(8,128)(2,1)S(1)} collective-permute-done((bf16[688,128]{1,0:T(8,128)(2,1)S(1)}, bf16[688,128]{1,0:T(8,128)(2,1)S(1)}, u32[]{:S(2)}, u32[]{:S(2)}) %collective-permute-start.5) | collective-permute-done | bytes 176160 | tf_op jit(solution)/shard_map/ppermute | solution.py:381
  56.5 5.0 %collective-permute-start.6 = (bf16[1200,128]{1,0:T(8,128)(2,1)S(1)}, bf16[1200,128]{1,0:T(8,128)(2,1)S(1)}, u32[]{:S(2)}, u32[]{:S(2)}) collective-permute-start(bf16[1200,128]{1,0:T(8,128)(2,1)S(1)} %get-tuple-element.57), channel_id=1, source_target_pairs={{0,2},{1,31},{2,4},{3,1},{4,6},{5,3},{6,8},{7,5},{8,10},{9,7},{10,... | collective-permute-start | bytes 921608 | tf_op jit(solution)/shard_map/ppermute | solution.py:407
  61.5 1.9 %collective-permute-start.7 = (bf16[1200,128]{1,0:T(8,128)(2,1)S(1)}, bf16[1200,128]{1,0:T(8,128)(2,1)S(1)}, u32[]{:S(2)}, u32[]{:S(2)}) collective-permute-start(bf16[1200,128]{1,0:T(8,128)(2,1)S(1)} %get-tuple-element.59), channel_id=1, source_target_pairs={{0,2},{1,31},{2,4},{3,1},{4,6},{5,3},{6,8},{7,5},{8,10},{9,7},{10,... | collective-permute-start | bytes 921608 | tf_op jit(solution)/shard_map/ppermute | solution.py:407
  63.5 1.6 %shard_map.114 = (bf16[1200,128]{1,0:T(8,128)(2,1)S(1)}, bf16[1200,128]{1,0:T(8,128)(2,1)S(1)}, bf16[1200,128]{1,0:T(8,128)(2,1)S(1)}, bf16[1200,128]{1,0:T(8,12...) custom-call(s32[60]{0:T(128)S(1)} %pad_add_fusion.refs_0_, ...), custom_call_target="tpu_custom_call" | custom-call | flops 458752 | bytes 4194304 | tf_op jit(solution)/shard_map/pallas_call | solution.py:395
  65.4 5.0 %collective-permute-start.8 = (bf16[1200,128]{1,0:T(8,128)(2,1)S(1)}, bf16[1200,128]{1,0:T(8,128)(2,1)S(1)}, u32[]{:S(2)}, u32[]{:S(2)}) collective-permute-start(bf16[1200,128]{1,0:T(8,128)(2,1)S(1)} %add_convert_fusion.13.refs_1_), channel_id=1, source_target_pairs={{0,2},{1,31},{2,4},{3,1},{4,6},{5,3},{6,8},{7,5},{8,10},{9,7},{10,... | collective-permute-start | bytes 921608 | tf_op jit(solution)/shard_map/ppermute | solution.py:407
  70.5 3.2 %collective-permute-start.9 = (bf16[1200,128]{1,0:T(8,128)(2,1)S(1)}, bf16[1200,128]{1,0:T(8,128)(2,1)S(1)}, u32[]{:S(2)}, u32[]{:S(2)}) collective-permute-start(bf16[1200,128]{1,0:T(8,128)(2,1)S(1)} %add_convert_fusion.12.refs_2_), channel_id=1, source_target_pairs={{0,2},{1,31},{2,4},{3,1},{4,6},{5,3},{6,8},{7,5},{8,10},{9,7},{10,... | collective-permute-start | bytes 921608 | tf_op jit(solution)/shard_map/ppermute | solution.py:407
  74.3 5.0 %collective-permute-start.10 = (bf16[1200,128]{1,0:T(8,128)(2,1)S(1)}, bf16[1200,128]{1,0:T(8,128)(2,1)S(1)}, u32[]{:S(2)}, u32[]{:S(2)}) collective-permute-start(bf16[1200,128]{1,0:T(8,128)(2,1)S(1)} %add_convert_fusion.11.refs_3_), channel_id=1, source_target_pairs={{0,2},{1,31},{2,4},{3,1},{4,6},{5,3},{6,8},{7,5},{8,10},{9,7},{10,... | collective-permute-start | bytes 921608 | tf_op jit(solution)/shard_map/ppermute | solution.py:407
  79.4 3.2 %collective-permute-start.11 = (bf16[1200,128]{1,0:T(8,128)(2,1)S(1)}, bf16[1200,128]{1,0:T(8,128)(2,1)S(1)}, u32[]{:S(2)}, u32[]{:S(2)}) collective-permute-start(bf16[1200,128]{1,0:T(8,128)(2,1)S(1)} %add_convert_fusion.10.refs_4_), channel_id=1, source_target_pairs={{0,2},{1,31},{2,4},{3,1},{4,6},{5,3},{6,8},{7,5},{8,10},{9,7},{10,... | collective-permute-start | bytes 921608 | tf_op jit(solution)/shard_map/ppermute | solution.py:407
  83.2 5.0 %collective-permute-start.12 = (bf16[1200,128]{1,0:T(8,128)(2,1)S(1)}, bf16[1200,128]{1,0:T(8,128)(2,1)S(1)}, u32[]{:S(2)}, u32[]{:S(2)}) collective-permute-start(bf16[1200,128]{1,0:T(8,128)(2,1)S(1)} %add_convert_fusion.9.refs_5_), channel_id=1, source_target_pairs={{0,2},{1,31},{2,4},{3,1},{4,6},{5,3},{6,8},{7,5},{8,10},{9,7},{10,... | collective-permute-start | bytes 921608 | tf_op jit(solution)/shard_map/ppermute | solution.py:407
  88.3 3.2 %collective-permute-start.13 = (bf16[1200,128]{1,0:T(8,128)(2,1)S(1)}, bf16[1200,128]{1,0:T(8,128)(2,1)S(1)}, u32[]{:S(2)}, u32[]{:S(2)}) collective-permute-start(bf16[1200,128]{1,0:T(8,128)(2,1)S(1)} %add_convert_fusion.8.refs_6_), channel_id=1, source_target_pairs={{0,2},{1,31},{2,4},{3,1},{4,6},{5,3},{6,8},{7,5},{8,10},{9,7},{10,... | collective-permute-start | bytes 921608 | tf_op jit(solution)/shard_map/ppermute | solution.py:407
  92.1 5.0 %collective-permute-start.14 = (bf16[1200,128]{1,0:T(8,128)(2,1)S(1)}, bf16[1200,128]{1,0:T(8,128)(2,1)S(1)}, u32[]{:S(2)}, u32[]{:S(2)}) collective-permute-start(bf16[1200,128]{1,0:T(8,128)(2,1)S(1)} %add_convert_fusion.7.refs_7_), channel_id=1, source_target_pairs={{0,2},{1,31},{2,4},{3,1},{4,6},{5,3},{6,8},{7,5},{8,10},{9,7},{10,... | collective-permute-start | bytes 921608 | tf_op jit(solution)/shard_map/ppermute | solution.py:407
  97.2 3.2 %collective-permute-start.15 = (bf16[1200,128]{1,0:T(8,128)(2,1)S(1)}, bf16[1200,128]{1,0:T(8,128)(2,1)S(1)}, u32[]{:S(2)}, u32[]{:S(2)}) collective-permute-start(bf16[1200,128]{1,0:T(8,128)(2,1)S(1)} %add_convert_fusion.6.refs_8_), channel_id=1, source_target_pairs={{0,2},{1,31},{2,4},{3,1},{4,6},{5,3},{6,8},{7,5},{8,10},{9,7},{10,... | collective-permute-start | bytes 921608 | tf_op jit(solution)/shard_map/ppermute | solution.py:407
  101.0 5.0 %collective-permute-start.16 = (bf16[1200,128]{1,0:T(8,128)(2,1)S(1)}, bf16[1200,128]{1,0:T(8,128)(2,1)S(1)}, u32[]{:S(2)}, u32[]{:S(2)}) collective-permute-start(bf16[1200,128]{1,0:T(8,128)(2,1)S(1)} %add_convert_fusion.5.refs_9_), channel_id=1, source_target_pairs={{0,2},{1,31},{2,4},{3,1},{4,6},{5,3},{6,8},{7,5},{8,10},{9,7},{10,... | collective-permute-start | bytes 921608 | tf_op jit(solution)/shard_map/ppermute | solution.py:407
  106.1 3.2 %collective-permute-start.17 = (bf16[1200,128]{1,0:T(8,128)(2,1)S(1)}, bf16[1200,128]{1,0:T(8,128)(2,1)S(1)}, u32[]{:S(2)}, u32[]{:S(2)}) collective-permute-start(bf16[1200,128]{1,0:T(8,128)(2,1)S(1)} %add_convert_fusion.4.refs_10_), channel_id=1, source_target_pairs={{0,2},{1,31},{2,4},{3,1},{4,6},{5,3},{6,8},{7,5},{8,10},{9,7},{10,... | collective-permute-start | bytes 921608 | tf_op jit(solution)/shard_map/ppermute | solution.py:407
  109.9 5.0 %collective-permute-start.19 = (bf16[1200,128]{1,0:T(8,128)(2,1)S(1)}, bf16[1200,128]{1,0:T(8,128)(2,1)S(1)}, u32[]{:S(2)}, u32[]{:S(2)}) collective-permute-start(bf16[1200,128]{1,0:T(8,128)(2,1)S(1)} %add_convert_fusion.3.refs_11_), channel_id=1, source_target_pairs={{0,2},{1,31},{2,4},{3,1},{4,6},{5,3},{6,8},{7,5},{8,10},{9,7},{10,... | collective-permute-start | bytes 921608 | tf_op jit(solution)/shard_map/ppermute | solution.py:407
  115.0 3.2 %collective-permute-start.18 = (bf16[1200,128]{1,0:T(8,128)(2,1)S(1)}, bf16[1200,128]{1,0:T(8,128)(2,1)S(1)}, u32[]{:S(2)}, u32[]{:S(2)}) collective-permute-start(bf16[1200,128]{1,0:T(8,128)(2,1)S(1)} %add_convert_fusion.2.refs_12_), channel_id=1, source_target_pairs={{0,2},{1,31},{2,4},{3,1},{4,6},{5,3},{6,8},{7,5},{8,10},{9,7},{10,... | collective-permute-start | bytes 921608 | tf_op jit(solution)/shard_map/ppermute | solution.py:407
  118.2 2.2 %shard_map.115.early = f32[4,256,128]{2,1,0:T(8,128)S(1)} custom-call(bf16[3760,128]{1,0:T(8,128)(2,1)} %get-tuple-element.54.own, bf16[3760,128]{1,0:T(8,128)(2,1)S(1)} %collective-permute-done.4.refs_3_.refs_2_.theirs, bf16[688,128]{1,0:T(8,128)(2,1)S(1)} %collective-permute-done.5.refs_2_.refs_0_, bf16[1200,128]{1,0:T(8,128)(2,1)S(1)} %add_convert_fusion.13.refs_1_, ...), custom_call_target="tpu_custom_call" | custom-call | flops 176160768 | bytes 2097152 | tf_op jit(solution)/shard_map/pallas_call | solution.py:412
  120.8 9.4 %collective-permute-start.20 = (bf16[1200,128]{1,0:T(8,128)(2,1)S(1)}, bf16[1200,128]{1,0:T(8,128)(2,1)S(1)}, u32[]{:S(2)}, u32[]{:S(2)}) collective-permute-start(bf16[1200,128]{1,0:T(8,128)(2,1)S(1)} %add_convert_fusion.refs_0_), channel_id=1, source_target_pairs={{0,1},{1,0},{2,3},{3,2},{4,5},{5,4},{6,7},{7,6},{8,9},{9,8},{10,11... | collective-permute-start | bytes 921608 | tf_op jit(solution)/shard_map/ppermute | solution.py:433
  130.6 3.0 %collective-permute-start.21 = (bf16[384,128]{1,0:T(8,128)(2,1)S(1)}, bf16[384,128]{1,0:T(8,128)(2,1)S(1)}, u32[]{:S(2)}, u32[]{:S(2)}) collective-permute-start(bf16[384,128]{1,0:T(8,128)(2,1)S(1)} %get-tuple-element.76), channel_id=1, source_target_pairs={{0,1},{1,0},{2,3},{3,2},{4,5},{5,4},{6,7},{7,6},{8,9},{9,8},{10,11... | collective-permute-start | bytes 294920 | tf_op jit(solution)/shard_map/ppermute | solution.py:434
  134.5 1.6 %shard_map.118 = f32[4,24,128]{2,1,0:T(8,128)} custom-call(s32[32]{0:T(128)S(1)} %copy-done.5, f32[3,128,128]{2,1,0:T(8,128)S(1)} %get-tuple-element.75.mine, bf16[384,128]{1,0:T(8,128)(2,1)S(1)} %collective-permute-done.21.mate, bf16[32,128,128]{2,1,0:T(8,128)(2,1)S(1)} %copy-done.1), custom_call_target="tpu_custom_call" | custom-call | flops 8388608 | bytes 2097152 | tf_op jit(solution)/shard_map/pallas_call | solution.py:444
  (91 shorter events, 14.6 us)
Async XLA Ops:
  0.6 24.7 %copy-start = (bf16[128,128]{1,0:T(8,128)(2,1)S(1)}, bf16[128,128]{1,0:T(8,128)(2,1)}, u32[]{:S(2)}) copy-start(bf16[128,128]{1,0:T(8,128)(2,1)} %param.14) | copy-start | bytes 98308
  0.6 13.5 %copy-start.6 = (bf16[24,128,128]{2,1,0:T(8,128)(2,1)S(1)}, bf16[24,128,128]{2,1,0:T(8,128)(2,1)}, u32[]{:S(2)}) copy-start(bf16[24,128,128]{2,1,0:T(8,128)(2,1)} %param.13) | copy-start | bytes 2359300
  1.7 12.5 %collective-permute-start = (bf16[3,128,128]{2,1,0:T(8,128)(2,1)S(1)}, bf16[3,128,128]{2,1,0:T(8,128)(2,1)S(1)}, u32[]{:S(2)}, u32[]{:S(2)}) collective-permute-start(bf16[3,128,128]{2,1,0:T(8,128)(2,1)S(1)} %get-tuple-element.82), channel_id=1, source_target_pairs={{0,32},{32,64},{64,96},{96,128},{128,160},{160,192},{192,224},{224... | collective-permute-start | bytes 294920 | tf_op jit(solution)/shard_map/ppermute | solution.py:30
  7.0 9.0 %collective-permute-start.1 = (bf16[3,128,128]{2,1,0:T(8,128)(2,1)S(1)}, bf16[3,128,128]{2,1,0:T(8,128)(2,1)S(1)}, u32[]{:S(2)}, u32[]{:S(2)}) collective-permute-start(bf16[3,128,128]{2,1,0:T(8,128)(2,1)S(1)} %get-tuple-element.81), channel_id=1, source_target_pairs={{32,0},{64,32},{96,64},{128,96},{160,128},{192,160},{224,192},{256... | collective-permute-start | bytes 294920 | tf_op jit(solution)/shard_map/ppermute | solution.py:30
  16.1 8.2 %collective-permute-start.3 = (bf16[30,4,128]{2,1,0:T(4,128)(2,1)S(1)}, bf16[30,4,128]{2,1,0:T(4,128)(2,1)S(1)}, u32[]{:S(2)}, u32[]{:S(2)}) collective-permute-start(bf16[30,4,128]{2,1,0:T(4,128)(2,1)S(1)} %get-tuple-element.84), channel_id=1, source_target_pairs={{1,0},{2,1},{3,2},{4,3},{5,4},{6,5},{7,6},{8,7},{9,8},{10,9},{11,1... | collective-permute-start | bytes 92168 | tf_op jit(solution)/shard_map/ppermute | solution.py:46
  20.1 4.9 %collective-permute-start.2 = (bf16[30,4,128]{2,1,0:T(4,128)(2,1)S(1)}, bf16[30,4,128]{2,1,0:T(4,128)(2,1)S(1)}, u32[]{:S(2)}, u32[]{:S(2)}) collective-permute-start(bf16[30,4,128]{2,1,0:T(4,128)(2,1)S(1)} %get-tuple-element.83), channel_id=1, source_target_pairs={{0,1},{1,2},{2,3},{3,4},{4,5},{5,6},{6,7},{7,8},{8,9},{9,10},{10,1... | collective-permute-start | bytes 92168 | tf_op jit(solution)/shard_map/ppermute | solution.py:45
  24.3 2.8 %copy-start.7 = (bf16[30,4,128]{2,1,0:T(4,128)(2,1)}, bf16[30,4,128]{2,1,0:T(4,128)(2,1)S(1)}, u32[]{:S(2)}) copy-start(bf16[30,4,128]{2,1,0:T(4,128)(2,1)S(1)} %collective-permute-done.3) | copy-start | bytes 92164
  25.0 2.1 %copy-start.8 = (bf16[30,4,128]{2,1,0:T(4,128)(2,1)}, bf16[30,4,128]{2,1,0:T(4,128)(2,1)S(1)}, u32[]{:S(2)}) copy-start(bf16[30,4,128]{2,1,0:T(4,128)(2,1)S(1)} %collective-permute-done.2) | copy-start | bytes 92164
  28.3 1.2 copy-start.1
  28.3 1.2 copy-start.5
  29.5 3.7 %copy-start.3 = (bf16[24,128,128]{2,1,0:T(8,128)(2,1)}, bf16[24,128,128]{2,1,0:T(8,128)(2,1)S(1)}, u32[]{:S(2)}) copy-start(bf16[24,128,128]{2,1,0:T(8,128)(2,1)S(1)} %convolution_convert_fusion.2.atm) | copy-start | bytes 2359300
  33.2 22.6 %collective-permute-start.4 = (bf16[3760,128]{1,0:T(8,128)(2,1)}, bf16[3760,128]{1,0:T(8,128)(2,1)S(1)}, u32[]{:S(2)}, u32[]{:S(2)}) collective-permute-start(bf16[3760,128]{1,0:T(8,128)(2,1)} %get-tuple-element.54.own), channel_id=1, source_target_pairs={{0,1},{1,0},{2,3},{3,2},{4,5},{5,4},{6,7},{7,6},{8,9},{9,8},{10,11... | collective-permute-start | bytes 2887688 | tf_op jit(solution)/shard_map/ppermute | solution.py:382
  35.1 20.6 %collective-permute-start.5 = (bf16[688,128]{1,0:T(8,128)(2,1)S(1)}, bf16[688,128]{1,0:T(8,128)(2,1)S(1)}, u32[]{:S(2)}, u32[]{:S(2)}) collective-permute-start(bf16[688,128]{1,0:T(8,128)(2,1)S(1)} %get-tuple-element.55), channel_id=1, source_target_pairs={{0,2},{1,31},{2,4},{3,1},{4,6},{5,3},{6,8},{7,5},{8,10},{9,7},{10,... | collective-permute-start | bytes 528392 | tf_op jit(solution)/shard_map/ppermute | solution.py:381
  56.5 8.8 %collective-permute-start.6 = (bf16[1200,128]{1,0:T(8,128)(2,1)S(1)}, bf16[1200,128]{1,0:T(8,128)(2,1)S(1)}, u32[]{:S(2)}, u32[]{:S(2)}) collective-permute-start(bf16[1200,128]{1,0:T(8,128)(2,1)S(1)} %get-tuple-element.57), channel_id=1, source_target_pairs={{0,2},{1,31},{2,4},{3,1},{4,6},{5,3},{6,8},{7,5},{8,10},{9,7},{10,... | collective-permute-start | bytes 921608 | tf_op jit(solution)/shard_map/ppermute | solution.py:407
  61.5 8.9 %collective-permute-start.7 = (bf16[1200,128]{1,0:T(8,128)(2,1)S(1)}, bf16[1200,128]{1,0:T(8,128)(2,1)S(1)}, u32[]{:S(2)}, u32[]{:S(2)}) collective-permute-start(bf16[1200,128]{1,0:T(8,128)(2,1)S(1)} %get-tuple-element.59), channel_id=1, source_target_pairs={{0,2},{1,31},{2,4},{3,1},{4,6},{5,3},{6,8},{7,5},{8,10},{9,7},{10,... | collective-permute-start | bytes 921608 | tf_op jit(solution)/shard_map/ppermute | solution.py:407
  65.4 8.8 %collective-permute-start.8 = (bf16[1200,128]{1,0:T(8,128)(2,1)S(1)}, bf16[1200,128]{1,0:T(8,128)(2,1)S(1)}, u32[]{:S(2)}, u32[]{:S(2)}) collective-permute-start(bf16[1200,128]{1,0:T(8,128)(2,1)S(1)} %add_convert_fusion.13.refs_1_), channel_id=1, source_target_pairs={{0,2},{1,31},{2,4},{3,1},{4,6},{5,3},{6,8},{7,5},{8,10},{9,7},{10,... | collective-permute-start | bytes 921608 | tf_op jit(solution)/shard_map/ppermute | solution.py:407
  70.5 8.8 %collective-permute-start.9 = (bf16[1200,128]{1,0:T(8,128)(2,1)S(1)}, bf16[1200,128]{1,0:T(8,128)(2,1)S(1)}, u32[]{:S(2)}, u32[]{:S(2)}) collective-permute-start(bf16[1200,128]{1,0:T(8,128)(2,1)S(1)} %add_convert_fusion.12.refs_2_), channel_id=1, source_target_pairs={{0,2},{1,31},{2,4},{3,1},{4,6},{5,3},{6,8},{7,5},{8,10},{9,7},{10,... | collective-permute-start | bytes 921608 | tf_op jit(solution)/shard_map/ppermute | solution.py:407
  74.3 8.8 %collective-permute-start.10 = (bf16[1200,128]{1,0:T(8,128)(2,1)S(1)}, bf16[1200,128]{1,0:T(8,128)(2,1)S(1)}, u32[]{:S(2)}, u32[]{:S(2)}) collective-permute-start(bf16[1200,128]{1,0:T(8,128)(2,1)S(1)} %add_convert_fusion.11.refs_3_), channel_id=1, source_target_pairs={{0,2},{1,31},{2,4},{3,1},{4,6},{5,3},{6,8},{7,5},{8,10},{9,7},{10,... | collective-permute-start | bytes 921608 | tf_op jit(solution)/shard_map/ppermute | solution.py:407
  79.4 8.8 %collective-permute-start.11 = (bf16[1200,128]{1,0:T(8,128)(2,1)S(1)}, bf16[1200,128]{1,0:T(8,128)(2,1)S(1)}, u32[]{:S(2)}, u32[]{:S(2)}) collective-permute-start(bf16[1200,128]{1,0:T(8,128)(2,1)S(1)} %add_convert_fusion.10.refs_4_), channel_id=1, source_target_pairs={{0,2},{1,31},{2,4},{3,1},{4,6},{5,3},{6,8},{7,5},{8,10},{9,7},{10,... | collective-permute-start | bytes 921608 | tf_op jit(solution)/shard_map/ppermute | solution.py:407
  83.2 8.8 %collective-permute-start.12 = (bf16[1200,128]{1,0:T(8,128)(2,1)S(1)}, bf16[1200,128]{1,0:T(8,128)(2,1)S(1)}, u32[]{:S(2)}, u32[]{:S(2)}) collective-permute-start(bf16[1200,128]{1,0:T(8,128)(2,1)S(1)} %add_convert_fusion.9.refs_5_), channel_id=1, source_target_pairs={{0,2},{1,31},{2,4},{3,1},{4,6},{5,3},{6,8},{7,5},{8,10},{9,7},{10,... | collective-permute-start | bytes 921608 | tf_op jit(solution)/shard_map/ppermute | solution.py:407
  88.3 8.8 %collective-permute-start.13 = (bf16[1200,128]{1,0:T(8,128)(2,1)S(1)}, bf16[1200,128]{1,0:T(8,128)(2,1)S(1)}, u32[]{:S(2)}, u32[]{:S(2)}) collective-permute-start(bf16[1200,128]{1,0:T(8,128)(2,1)S(1)} %add_convert_fusion.8.refs_6_), channel_id=1, source_target_pairs={{0,2},{1,31},{2,4},{3,1},{4,6},{5,3},{6,8},{7,5},{8,10},{9,7},{10,... | collective-permute-start | bytes 921608 | tf_op jit(solution)/shard_map/ppermute | solution.py:407
  92.1 8.8 %collective-permute-start.14 = (bf16[1200,128]{1,0:T(8,128)(2,1)S(1)}, bf16[1200,128]{1,0:T(8,128)(2,1)S(1)}, u32[]{:S(2)}, u32[]{:S(2)}) collective-permute-start(bf16[1200,128]{1,0:T(8,128)(2,1)S(1)} %add_convert_fusion.7.refs_7_), channel_id=1, source_target_pairs={{0,2},{1,31},{2,4},{3,1},{4,6},{5,3},{6,8},{7,5},{8,10},{9,7},{10,... | collective-permute-start | bytes 921608 | tf_op jit(solution)/shard_map/ppermute | solution.py:407
  97.2 8.8 %collective-permute-start.15 = (bf16[1200,128]{1,0:T(8,128)(2,1)S(1)}, bf16[1200,128]{1,0:T(8,128)(2,1)S(1)}, u32[]{:S(2)}, u32[]{:S(2)}) collective-permute-start(bf16[1200,128]{1,0:T(8,128)(2,1)S(1)} %add_convert_fusion.6.refs_8_), channel_id=1, source_target_pairs={{0,2},{1,31},{2,4},{3,1},{4,6},{5,3},{6,8},{7,5},{8,10},{9,7},{10,... | collective-permute-start | bytes 921608 | tf_op jit(solution)/shard_map/ppermute | solution.py:407
  101.0 8.8 %collective-permute-start.16 = (bf16[1200,128]{1,0:T(8,128)(2,1)S(1)}, bf16[1200,128]{1,0:T(8,128)(2,1)S(1)}, u32[]{:S(2)}, u32[]{:S(2)}) collective-permute-start(bf16[1200,128]{1,0:T(8,128)(2,1)S(1)} %add_convert_fusion.5.refs_9_), channel_id=1, source_target_pairs={{0,2},{1,31},{2,4},{3,1},{4,6},{5,3},{6,8},{7,5},{8,10},{9,7},{10,... | collective-permute-start | bytes 921608 | tf_op jit(solution)/shard_map/ppermute | solution.py:407
  106.1 8.8 %collective-permute-start.17 = (bf16[1200,128]{1,0:T(8,128)(2,1)S(1)}, bf16[1200,128]{1,0:T(8,128)(2,1)S(1)}, u32[]{:S(2)}, u32[]{:S(2)}) collective-permute-start(bf16[1200,128]{1,0:T(8,128)(2,1)S(1)} %add_convert_fusion.4.refs_10_), channel_id=1, source_target_pairs={{0,2},{1,31},{2,4},{3,1},{4,6},{5,3},{6,8},{7,5},{8,10},{9,7},{10,... | collective-permute-start | bytes 921608 | tf_op jit(solution)/shard_map/ppermute | solution.py:407
  109.9 10.8 %collective-permute-start.19 = (bf16[1200,128]{1,0:T(8,128)(2,1)S(1)}, bf16[1200,128]{1,0:T(8,128)(2,1)S(1)}, u32[]{:S(2)}, u32[]{:S(2)}) collective-permute-start(bf16[1200,128]{1,0:T(8,128)(2,1)S(1)} %add_convert_fusion.3.refs_11_), channel_id=1, source_target_pairs={{0,2},{1,31},{2,4},{3,1},{4,6},{5,3},{6,8},{7,5},{8,10},{9,7},{10,... | collective-permute-start | bytes 921608 | tf_op jit(solution)/shard_map/ppermute | solution.py:407
  115.0 15.2 %collective-permute-start.18 = (bf16[1200,128]{1,0:T(8,128)(2,1)S(1)}, bf16[1200,128]{1,0:T(8,128)(2,1)S(1)}, u32[]{:S(2)}, u32[]{:S(2)}) collective-permute-start(bf16[1200,128]{1,0:T(8,128)(2,1)S(1)} %add_convert_fusion.2.refs_12_), channel_id=1, source_target_pairs={{0,2},{1,31},{2,4},{3,1},{4,6},{5,3},{6,8},{7,5},{8,10},{9,7},{10,... | collective-permute-start | bytes 921608 | tf_op jit(solution)/shard_map/ppermute | solution.py:407
  120.7 15.4 %copy-start.2 = (bf16[8,128,128]{2,1,0:T(8,128)(2,1)S(1)}, bf16[8,128,128]{2,1,0:T(8,128)(2,1)}, u32[]{:S(2)}) copy-start(bf16[8,128,128]{2,1,0:T(8,128)(2,1)} %state.1) | copy-start | bytes 786436
  120.8 15.4 %copy-start.4 = (bf16[128,128]{1,0:T(8,128)(2,1)S(1)}, bf16[128,128]{1,0:T(8,128)(2,1)}, u32[]{:S(2)}) copy-start(bf16[128,128]{1,0:T(8,128)(2,1)} %coupling.1) | copy-start | bytes 98308
  120.8 15.4 %collective-permute-start.20 = (bf16[1200,128]{1,0:T(8,128)(2,1)S(1)}, bf16[1200,128]{1,0:T(8,128)(2,1)S(1)}, u32[]{:S(2)}, u32[]{:S(2)}) collective-permute-start(bf16[1200,128]{1,0:T(8,128)(2,1)S(1)} %add_convert_fusion.refs_0_), channel_id=1, source_target_pairs={{0,1},{1,0},{2,3},{3,2},{4,5},{5,4},{6,7},{7,6},{8,9},{9,8},{10,11... | collective-permute-start | bytes 921608 | tf_op jit(solution)/shard_map/ppermute | solution.py:433
  130.6 4.0 %collective-permute-start.21 = (bf16[384,128]{1,0:T(8,128)(2,1)S(1)}, bf16[384,128]{1,0:T(8,128)(2,1)S(1)}, u32[]{:S(2)}, u32[]{:S(2)}) collective-permute-start(bf16[384,128]{1,0:T(8,128)(2,1)S(1)} %get-tuple-element.76), channel_id=1, source_target_pairs={{0,1},{1,0},{2,3},{3,2},{4,5},{5,4},{6,7},{7,6},{8,9},{9,8},{10,11... | collective-permute-start | bytes 294920 | tf_op jit(solution)/shard_map/ppermute | solution.py:434

commit v6 on v5

--- a/solution.py
+++ b/solution.py
@@ -346,7 +346,6 @@
         [table, jnp.zeros((breadth - n_slots,), jnp.int32)]
     )
     current, told = substeps(tall, notes, vert_inverse)
-    current, ocean_adv = lax.optimization_barrier((current, ocean_adv))
     table_mate = jnp.concatenate([every[:n_own], told[n_far:n_slots]])
 
     def blocks_of(n):

time: 138 us -> 138 us (level)
  transfers between devices with their start and end apart: 22 -> 22, of which waited for: 10 -> 10; matrix products, arithmetic and copies ran while one was open for 6% -> 5% of each run, Pallas kernels for 4% -> 4%
where the time goes in v6:
time: 138 us; the launch traced here: 137 us
  starting transfers between devices  104 us (75%)
  Pallas kernels  11.1 us (8%)
  waiting for transfers between devices  8.04 us (6%)
  matrix products  5.17 us (4%)
  other arithmetic  4.43 us (3%)
  local copies, waits for them, and re-layouts  3.21 us (2%)
    ppermute x14, starting transfers between devices, on_device(): came = lax.ppermute(held[j], 'col', onward)  56.2 us
    ppermute x1, starting transfers between devices, on_device(): far_in = lax.ppermute(far, 'col', onward)  18.3 us
    ppermute x1, starting transfers between devices, on_device(): swapped = lax.ppermute(held[1], 'col', mate)  9.29 us
    ppermute x2, starting transfers between devices, edges(): return (lax.ppermute(last, axis, up), lax.ppermute(first, axis, down))  7.18 us
    ppermute x1, starting transfers between devices, substeps(): lax.ppermute(jnp.concatenate([tall[:, :wide], line], axis=1), 'col', down)  4.01 us
    ppermute x1, starting transfers between devices, substeps(): lax.ppermute(jnp.concatenate([tall[:, breadth - wide:], line], axis=1), '...  3.9 us
    dot_general x3, matrix products, substeps(): jnp.einsum('hwc,cd->hwd', smooth, vert_inverse, preferred_element_type=F32)  3.82 us
    pallas_call x1, Pallas kernels, on_device(): pl.pallas_call(contrib_kernel, out_shape=(rows_of(n_own * breadth), rows_...  3.68 us
  transfers between devices with their start and end apart: 22, of which 10 were waited for; matrix products, arithmetic and copies ran while one was open for 5% of the time, Pallas kernels for 4%

profile of v6, /device:TPU:31, one launch (start us, length us, event | category | flops | bytes accessed | tf_op | source)
XLA Modules:
  0.0 137.0 jit_solution(3929990234908311009)
XLA Ops:
  1.6 5.3 %collective-permute-start = (bf16[3,128,128]{2,1,0:T(8,128)(2,1)S(1)}, bf16[3,128,128]{2,1,0:T(8,128)(2,1)S(1)}, u32[]{:S(2)}, u32[]{:S(2)}) collective-permute-start(bf16[3,128,128]{2,1,0:T(8,128)(2,1)S(1)} %get-tuple-element.78), channel_id=1, source_target_pairs={{0,32},{32,64},{64,96},{96,128},{128,160},{160,192},{192,224},{224... | collective-permute-start | bytes 294920 | tf_op jit(solution)/shard_map/ppermute | solution.py:30
  6.9 1.9 %collective-permute-start.1 = (bf16[3,128,128]{2,1,0:T(8,128)(2,1)S(1)}, bf16[3,128,128]{2,1,0:T(8,128)(2,1)S(1)}, u32[]{:S(2)}, u32[]{:S(2)}) collective-permute-start(bf16[3,128,128]{2,1,0:T(8,128)(2,1)S(1)} %get-tuple-element.77), channel_id=1, source_target_pairs={{32,0},{64,32},{96,64},{128,96},{160,128},{192,160},{224,192},{256... | collective-permute-start | bytes 294920 | tf_op jit(solution)/shard_map/ppermute | solution.py:30
  11.7 1.1 convolution_convert_fusion.4
  12.9 1.3 constant_dynamic-update-slice_fusion.1
  14.2 1.7 %collective-permute-done.1 = bf16[3,128,128]{2,1,0:T(8,128)(2,1)S(1)} collective-permute-done((bf16[3,128,128]{2,1,0:T(8,128)(2,1)S(1)}, bf16[3,128,128]{2,1,0:T(8,128)(2,1)S(1)}, u32[]{:S(2)}, u32[]{:S(2)}) %collective-permute-start.1) | collective-permute-done | bytes 98336 | tf_op jit(solution)/shard_map/ppermute | solution.py:30
  16.0 4.0 %collective-permute-start.3 = (bf16[30,4,128]{2,1,0:T(4,128)(2,1)S(1)}, bf16[30,4,128]{2,1,0:T(4,128)(2,1)S(1)}, u32[]{:S(2)}, u32[]{:S(2)}) collective-permute-start(bf16[30,4,128]{2,1,0:T(4,128)(2,1)S(1)} %get-tuple-element.80), channel_id=1, source_target_pairs={{1,0},{2,1},{3,2},{4,3},{5,4},{6,5},{7,6},{8,7},{9,8},{10,9},{11,1... | collective-permute-start | bytes 92168 | tf_op jit(solution)/shard_map/ppermute | solution.py:46
  20.0 3.9 %collective-permute-start.2 = (bf16[30,4,128]{2,1,0:T(4,128)(2,1)S(1)}, bf16[30,4,128]{2,1,0:T(4,128)(2,1)S(1)}, u32[]{:S(2)}, u32[]{:S(2)}) collective-permute-start(bf16[30,4,128]{2,1,0:T(4,128)(2,1)S(1)} %get-tuple-element.79), channel_id=1, source_target_pairs={{0,1},{1,2},{2,3},{3,4},{4,5},{5,6},{6,7},{7,8},{8,9},{9,10},{10,1... | collective-permute-start | bytes 92168 | tf_op jit(solution)/shard_map/ppermute | solution.py:45
  25.3 1.7 %fusion.13 = f32[28,132,128]{2,1,0:T(8,128)S(1)} fusion(f32[30,134,128]{2,1,0:T(8,128)S(1)} %maximum_convert_fusion, pred[28,132]{1,0:T(8,128)(4,1)S(1)} %broadcast_and_fusion, bf16[128,128]{1,0:T(8,128)(2,1)S(1)} %copy-done), kind=kOutput, calls=%fused_computation.25 | convolution fusion | flops 126314496 | bytes 11681792 | tf_op jit(solution)/shard_map/hwc,cd->hwd/dot_general | solution.py:63
  26.9 1.2 fusion.15
  29.4 3.7 %shard_map.112 = (bf16[4096,128]{1,0:T(8,128)(2,1)S(1)}, bf16[688,128]{1,0:T(8,128)(2,1)S(1)}, bf16[3760,128]{1,0:T(8,128)(2,1)}) custom-call(s32[32]{0:T(128)S(1)} %copy-done.5, s32[32]{0:T(128)S(1)} %compare_select_fusion.4.idx, bf16[24,128,128]{2,1,0:T(8,128)(2,1)S(1)} %convolution_convert_fusion.2.atm, bf16[32,128,128]{2,1,0:T(8,128)(2,1)S(1)} %copy-done.1, ...), custom_call_target="tpu_custom_call" | custom-call | flops 134217728 | bytes 8388608 | tf_op jit(solution)/shard_map/pallas_call | solution.py:363
  33.1 1.9 %collective-permute-start.4 = (bf16[3760,128]{1,0:T(8,128)(2,1)}, bf16[3760,128]{1,0:T(8,128)(2,1)S(1)}, u32[]{:S(2)}, u32[]{:S(2)}) collective-permute-start(bf16[3760,128]{1,0:T(8,128)(2,1)} %get-tuple-element.50.own), channel_id=1, source_target_pairs={{0,1},{1,0},{2,3},{3,2},{4,5},{5,4},{6,7},{7,6},{8,9},{9,8},{10,11... | collective-permute-start | bytes 2887688 | tf_op jit(solution)/shard_map/ppermute | solution.py:381
  35.0 18.3 %collective-permute-start.5 = (bf16[688,128]{1,0:T(8,128)(2,1)S(1)}, bf16[688,128]{1,0:T(8,128)(2,1)S(1)}, u32[]{:S(2)}, u32[]{:S(2)}) collective-permute-start(bf16[688,128]{1,0:T(8,128)(2,1)S(1)} %get-tuple-element.51), channel_id=1, source_target_pairs={{0,2},{1,31},{2,4},{3,1},{4,6},{5,3},{6,8},{7,5},{8,10},{9,7},{10,... | collective-permute-start | bytes 528392 | tf_op jit(solution)/shard_map/ppermute | solution.py:380
  53.4 2.2 %collective-permute-done.5.refs_2_.refs_0_ = bf16[688,128]{1,0:T(8,128)(2,1)S(1)} collective-permute-done((bf16[688,128]{1,0:T(8,128)(2,1)S(1)}, bf16[688,128]{1,0:T(8,128)(2,1)S(1)}, u32[]{:S(2)}, u32[]{:S(2)}) %collective-permute-start.5) | collective-permute-done | bytes 176160 | tf_op jit(solution)/shard_map/ppermute | solution.py:380
  56.4 5.0 %collective-permute-start.6 = (bf16[1200,128]{1,0:T(8,128)(2,1)S(1)}, bf16[1200,128]{1,0:T(8,128)(2,1)S(1)}, u32[]{:S(2)}, u32[]{:S(2)}) collective-permute-start(bf16[1200,128]{1,0:T(8,128)(2,1)S(1)} %get-tuple-element.53), channel_id=1, source_target_pairs={{0,2},{1,31},{2,4},{3,1},{4,6},{5,3},{6,8},{7,5},{8,10},{9,7},{10,... | collective-permute-start | bytes 921608 | tf_op jit(solution)/shard_map/ppermute | solution.py:406
  61.4 1.9 %collective-permute-start.7 = (bf16[1200,128]{1,0:T(8,128)(2,1)S(1)}, bf16[1200,128]{1,0:T(8,128)(2,1)S(1)}, u32[]{:S(2)}, u32[]{:S(2)}) collective-permute-start(bf16[1200,128]{1,0:T(8,128)(2,1)S(1)} %get-tuple-element.55), channel_id=1, source_target_pairs={{0,2},{1,31},{2,4},{3,1},{4,6},{5,3},{6,8},{7,5},{8,10},{9,7},{10,... | collective-permute-start | bytes 921608 | tf_op jit(solution)/shard_map/ppermute | solution.py:406
  63.4 1.6 %shard_map.114 = (bf16[1200,128]{1,0:T(8,128)(2,1)S(1)}, bf16[1200,128]{1,0:T(8,128)(2,1)S(1)}, bf16[1200,128]{1,0:T(8,128)(2,1)S(1)}, bf16[1200,128]{1,0:T(8,12...) custom-call(s32[60]{0:T(128)S(1)} %pad_add_fusion.refs_0_, ...), custom_call_target="tpu_custom_call" | custom-call | flops 458752 | bytes 4194304 | tf_op jit(solution)/shard_map/pallas_call | solution.py:394
  65.3 5.0 %collective-permute-start.8 = (bf16[1200,128]{1,0:T(8,128)(2,1)S(1)}, bf16[1200,128]{1,0:T(8,128)(2,1)S(1)}, u32[]{:S(2)}, u32[]{:S(2)}) collective-permute-start(bf16[1200,128]{1,0:T(8,128)(2,1)S(1)} %add_convert_fusion.13.refs_1_), channel_id=1, source_target_pairs={{0,2},{1,31},{2,4},{3,1},{4,6},{5,3},{6,8},{7,5},{8,10},{9,7},{10,... | collective-permute-start | bytes 921608 | tf_op jit(solution)/shard_map/ppermute | solution.py:406
  70.4 3.2 %collective-permute-start.9 = (bf16[1200,128]{1,0:T(8,128)(2,1)S(1)}, bf16[1200,128]{1,0:T(8,128)(2,1)S(1)}, u32[]{:S(2)}, u32[]{:S(2)}) collective-permute-start(bf16[1200,128]{1,0:T(8,128)(2,1)S(1)} %add_convert_fusion.12.refs_2_), channel_id=1, source_target_pairs={{0,2},{1,31},{2,4},{3,1},{4,6},{5,3},{6,8},{7,5},{8,10},{9,7},{10,... | collective-permute-start | bytes 921608 | tf_op jit(solution)/shard_map/ppermute | solution.py:406
  74.2 5.0 %collective-permute-start.10 = (bf16[1200,128]{1,0:T(8,128)(2,1)S(1)}, bf16[1200,128]{1,0:T(8,128)(2,1)S(1)}, u32[]{:S(2)}, u32[]{:S(2)}) collective-permute-start(bf16[1200,128]{1,0:T(8,128)(2,1)S(1)} %add_convert_fusion.11.refs_3_), channel_id=1, source_target_pairs={{0,2},{1,31},{2,4},{3,1},{4,6},{5,3},{6,8},{7,5},{8,10},{9,7},{10,... | collective-permute-start | bytes 921608 | tf_op jit(solution)/shard_map/ppermute | solution.py:406
  79.3 3.2 %collective-permute-start.11 = (bf16[1200,128]{1,0:T(8,128)(2,1)S(1)}, bf16[1200,128]{1,0:T(8,128)(2,1)S(1)}, u32[]{:S(2)}, u32[]{:S(2)}) collective-permute-start(bf16[1200,128]{1,0:T(8,128)(2,1)S(1)} %add_convert_fusion.10.refs_4_), channel_id=1, source_target_pairs={{0,2},{1,31},{2,4},{3,1},{4,6},{5,3},{6,8},{7,5},{8,10},{9,7},{10,... | collective-permute-start | bytes 921608 | tf_op jit(solution)/shard_map/ppermute | solution.py:406
  83.1 5.0 %collective-permute-start.12 = (bf16[1200,128]{1,0:T(8,128)(2,1)S(1)}, bf16[1200,128]{1,0:T(8,128)(2,1)S(1)}, u32[]{:S(2)}, u32[]{:S(2)}) collective-permute-start(bf16[1200,128]{1,0:T(8,128)(2,1)S(1)} %add_convert_fusion.9.refs_5_), channel_id=1, source_target_pairs={{0,2},{1,31},{2,4},{3,1},{4,6},{5,3},{6,8},{7,5},{8,10},{9,7},{10,... | collective-permute-start | bytes 921608 | tf_op jit(solution)/shard_map/ppermute | solution.py:406
  88.2 3.2 %collective-permute-start.13 = (bf16[1200,128]{1,0:T(8,128)(2,1)S(1)}, bf16[1200,128]{1,0:T(8,128)(2,1)S(1)}, u32[]{:S(2)}, u32[]{:S(2)}) collective-permute-start(bf16[1200,128]{1,0:T(8,128)(2,1)S(1)} %add_convert_fusion.8.refs_6_), channel_id=1, source_target_pairs={{0,2},{1,31},{2,4},{3,1},{4,6},{5,3},{6,8},{7,5},{8,10},{9,7},{10,... | collective-permute-start | bytes 921608 | tf_op jit(solution)/shard_map/ppermute | solution.py:406
  92.0 5.0 %collective-permute-start.14 = (bf16[1200,128]{1,0:T(8,128)(2,1)S(1)}, bf16[1200,128]{1,0:T(8,128)(2,1)S(1)}, u32[]{:S(2)}, u32[]{:S(2)}) collective-permute-start(bf16[1200,128]{1,0:T(8,128)(2,1)S(1)} %add_convert_fusion.7.refs_7_), channel_id=1, source_target_pairs={{0,2},{1,31},{2,4},{3,1},{4,6},{5,3},{6,8},{7,5},{8,10},{9,7},{10,... | collective-permute-start | bytes 921608 | tf_op jit(solution)/shard_map/ppermute | solution.py:406
  97.1 3.2 %collective-permute-start.15 = (bf16[1200,128]{1,0:T(8,128)(2,1)S(1)}, bf16[1200,128]{1,0:T(8,128)(2,1)S(1)}, u32[]{:S(2)}, u32[]{:S(2)}) collective-permute-start(bf16[1200,128]{1,0:T(8,128)(2,1)S(1)} %add_convert_fusion.6.refs_8_), channel_id=1, source_target_pairs={{0,2},{1,31},{2,4},{3,1},{4,6},{5,3},{6,8},{7,5},{8,10},{9,7},{10,... | collective-permute-start | bytes 921608 | tf_op jit(solution)/shard_map/ppermute | solution.py:406
  100.9 5.0 %collective-permute-start.16 = (bf16[1200,128]{1,0:T(8,128)(2,1)S(1)}, bf16[1200,128]{1,0:T(8,128)(2,1)S(1)}, u32[]{:S(2)}, u32[]{:S(2)}) collective-permute-start(bf16[1200,128]{1,0:T(8,128)(2,1)S(1)} %add_convert_fusion.5.refs_9_), channel_id=1, source_target_pairs={{0,2},{1,31},{2,4},{3,1},{4,6},{5,3},{6,8},{7,5},{8,10},{9,7},{10,... | collective-permute-start | bytes 921608 | tf_op jit(solution)/shard_map/ppermute | solution.py:406
  106.0 3.2 %collective-permute-start.17 = (bf16[1200,128]{1,0:T(8,128)(2,1)S(1)}, bf16[1200,128]{1,0:T(8,128)(2,1)S(1)}, u32[]{:S(2)}, u32[]{:S(2)}) collective-permute-start(bf16[1200,128]{1,0:T(8,128)(2,1)S(1)} %add_convert_fusion.4.refs_10_), channel_id=1, source_target_pairs={{0,2},{1,31},{2,4},{3,1},{4,6},{5,3},{6,8},{7,5},{8,10},{9,7},{10,... | collective-permute-start | bytes 921608 | tf_op jit(solution)/shard_map/ppermute | solution.py:406
  109.8 5.0 %collective-permute-start.19 = (bf16[1200,128]{1,0:T(8,128)(2,1)S(1)}, bf16[1200,128]{1,0:T(8,128)(2,1)S(1)}, u32[]{:S(2)}, u32[]{:S(2)}) collective-permute-start(bf16[1200,128]{1,0:T(8,128)(2,1)S(1)} %add_convert_fusion.3.refs_11_), channel_id=1, source_target_pairs={{0,2},{1,31},{2,4},{3,1},{4,6},{5,3},{6,8},{7,5},{8,10},{9,7},{10,... | collective-permute-start | bytes 921608 | tf_op jit(solution)/shard_map/ppermute | solution.py:406
  114.9 3.2 %collective-permute-start.18 = (bf16[1200,128]{1,0:T(8,128)(2,1)S(1)}, bf16[1200,128]{1,0:T(8,128)(2,1)S(1)}, u32[]{:S(2)}, u32[]{:S(2)}) collective-permute-start(bf16[1200,128]{1,0:T(8,128)(2,1)S(1)} %add_convert_fusion.2.refs_12_), channel_id=1, source_target_pairs={{0,2},{1,31},{2,4},{3,1},{4,6},{5,3},{6,8},{7,5},{8,10},{9,7},{10,... | collective-permute-start | bytes 921608 | tf_op jit(solution)/shard_map/ppermute | solution.py:406
  118.1 2.2 %shard_map.115.early = f32[4,256,128]{2,1,0:T(8,128)S(1)} custom-call(bf16[3760,128]{1,0:T(8,128)(2,1)} %get-tuple-element.50.own, bf16[3760,128]{1,0:T(8,128)(2,1)S(1)} %collective-permute-done.4.refs_3_.refs_2_.theirs, bf16[688,128]{1,0:T(8,128)(2,1)S(1)} %collective-permute-done.5.refs_2_.refs_0_, bf16[1200,128]{1,0:T(8,128)(2,1)S(1)} %add_convert_fusion.13.refs_1_, ...), custom_call_target="tpu_custom_call" | custom-call | flops 176160768 | bytes 2097152 | tf_op jit(solution)/shard_map/pallas_call | solution.py:411
  120.7 9.3 %collective-permute-start.20 = (bf16[1200,128]{1,0:T(8,128)(2,1)S(1)}, bf16[1200,128]{1,0:T(8,128)(2,1)S(1)}, u32[]{:S(2)}, u32[]{:S(2)}) collective-permute-start(bf16[1200,128]{1,0:T(8,128)(2,1)S(1)} %add_convert_fusion.refs_0_), channel_id=1, source_target_pairs={{0,1},{1,0},{2,3},{3,2},{4,5},{5,4},{6,7},{7,6},{8,9},{9,8},{10,11... | collective-permute-start | bytes 921608 | tf_op jit(solution)/shard_map/ppermute | solution.py:432
  130.4 3.2 %collective-permute-start.21 = (bf16[384,128]{1,0:T(8,128)(2,1)S(1)}, bf16[384,128]{1,0:T(8,128)(2,1)S(1)}, u32[]{:S(2)}, u32[]{:S(2)}) collective-permute-start(bf16[384,128]{1,0:T(8,128)(2,1)S(1)} %get-tuple-element.72), channel_id=1, source_target_pairs={{0,1},{1,0},{2,3},{3,2},{4,5},{5,4},{6,7},{7,6},{8,9},{9,8},{10,11... | collective-permute-start | bytes 294920 | tf_op jit(solution)/shard_map/ppermute | solution.py:433
  134.5 1.6 %shard_map.118 = f32[4,24,128]{2,1,0:T(8,128)} custom-call(s32[32]{0:T(128)S(1)} %copy-done.5, f32[3,128,128]{2,1,0:T(8,128)S(1)} %get-tuple-element.71.mine, bf16[384,128]{1,0:T(8,128)(2,1)S(1)} %collective-permute-done.21.mate, bf16[32,128,128]{2,1,0:T(8,128)(2,1)S(1)} %copy-done.1), custom_call_target="tpu_custom_call" | custom-call | flops 8388608 | bytes 2097152 | tf_op jit(solution)/shard_map/pallas_call | solution.py:443
  (87 shorter events, 13.7 us)
Async XLA Ops:
  0.6 24.6 %copy-start = (bf16[128,128]{1,0:T(8,128)(2,1)S(1)}, bf16[128,128]{1,0:T(8,128)(2,1)}, u32[]{:S(2)}) copy-start(bf16[128,128]{1,0:T(8,128)(2,1)} %param.14) | copy-start | bytes 98308
  1.6 11.3 %collective-permute-start = (bf16[3,128,128]{2,1,0:T(8,128)(2,1)S(1)}, bf16[3,128,128]{2,1,0:T(8,128)(2,1)S(1)}, u32[]{:S(2)}, u32[]{:S(2)}) collective-permute-start(bf16[3,128,128]{2,1,0:T(8,128)(2,1)S(1)} %get-tuple-element.78), channel_id=1, source_target_pairs={{0,32},{32,64},{64,96},{96,128},{128,160},{160,192},{192,224},{224... | collective-permute-start | bytes 294920 | tf_op jit(solution)/shard_map/ppermute | solution.py:30
  6.9 9.0 %collective-permute-start.1 = (bf16[3,128,128]{2,1,0:T(8,128)(2,1)S(1)}, bf16[3,128,128]{2,1,0:T(8,128)(2,1)S(1)}, u32[]{:S(2)}, u32[]{:S(2)}) collective-permute-start(bf16[3,128,128]{2,1,0:T(8,128)(2,1)S(1)} %get-tuple-element.77), channel_id=1, source_target_pairs={{32,0},{64,32},{96,64},{128,96},{160,128},{192,160},{224,192},{256... | collective-permute-start | bytes 294920 | tf_op jit(solution)/shard_map/ppermute | solution.py:30
  16.0 8.2 %collective-permute-start.3 = (bf16[30,4,128]{2,1,0:T(4,128)(2,1)S(1)}, bf16[30,4,128]{2,1,0:T(4,128)(2,1)S(1)}, u32[]{:S(2)}, u32[]{:S(2)}) collective-permute-start(bf16[30,4,128]{2,1,0:T(4,128)(2,1)S(1)} %get-tuple-element.80), channel_id=1, source_target_pairs={{1,0},{2,1},{3,2},{4,3},{5,4},{6,5},{7,6},{8,7},{9,8},{10,9},{11,1... | collective-permute-start | bytes 92168 | tf_op jit(solution)/shard_map/ppermute | solution.py:46
  20.0 4.9 %collective-permute-start.2 = (bf16[30,4,128]{2,1,0:T(4,128)(2,1)S(1)}, bf16[30,4,128]{2,1,0:T(4,128)(2,1)S(1)}, u32[]{:S(2)}, u32[]{:S(2)}) collective-permute-start(bf16[30,4,128]{2,1,0:T(4,128)(2,1)S(1)} %get-tuple-element.79), channel_id=1, source_target_pairs={{0,1},{1,2},{2,3},{3,4},{4,5},{5,6},{6,7},{7,8},{8,9},{9,10},{10,1... | collective-permute-start | bytes 92168 | tf_op jit(solution)/shard_map/ppermute | solution.py:45
  28.2 1.2 copy-start.1
  28.2 1.2 copy-start.5
  29.4 3.7 %copy-start.3 = (bf16[24,128,128]{2,1,0:T(8,128)(2,1)}, bf16[24,128,128]{2,1,0:T(8,128)(2,1)S(1)}, u32[]{:S(2)}) copy-start(bf16[24,128,128]{2,1,0:T(8,128)(2,1)S(1)} %convolution_convert_fusion.2.atm) | copy-start | bytes 2359300
  33.1 22.6 %collective-permute-start.4 = (bf16[3760,128]{1,0:T(8,128)(2,1)}, bf16[3760,128]{1,0:T(8,128)(2,1)S(1)}, u32[]{:S(2)}, u32[]{:S(2)}) collective-permute-start(bf16[3760,128]{1,0:T(8,128)(2,1)} %get-tuple-element.50.own), channel_id=1, source_target_pairs={{0,1},{1,0},{2,3},{3,2},{4,5},{5,4},{6,7},{7,6},{8,9},{9,8},{10,11... | collective-permute-start | bytes 2887688 | tf_op jit(solution)/shard_map/ppermute | solution.py:381
  35.0 20.6 %collective-permute-start.5 = (bf16[688,128]{1,0:T(8,128)(2,1)S(1)}, bf16[688,128]{1,0:T(8,128)(2,1)S(1)}, u32[]{:S(2)}, u32[]{:S(2)}) collective-permute-start(bf16[688,128]{1,0:T(8,128)(2,1)S(1)} %get-tuple-element.51), channel_id=1, source_target_pairs={{0,2},{1,31},{2,4},{3,1},{4,6},{5,3},{6,8},{7,5},{8,10},{9,7},{10,... | collective-permute-start | bytes 528392 | tf_op jit(solution)/shard_map/ppermute | solution.py:380
  56.4 8.8 %collective-permute-start.6 = (bf16[1200,128]{1,0:T(8,128)(2,1)S(1)}, bf16[1200,128]{1,0:T(8,128)(2,1)S(1)}, u32[]{:S(2)}, u32[]{:S(2)}) collective-permute-start(bf16[1200,128]{1,0:T(8,128)(2,1)S(1)} %get-tuple-element.53), channel_id=1, source_target_pairs={{0,2},{1,31},{2,4},{3,1},{4,6},{5,3},{6,8},{7,5},{8,10},{9,7},{10,... | collective-permute-start | bytes 921608 | tf_op jit(solution)/shard_map/ppermute | solution.py:406
  61.4 8.9 %collective-permute-start.7 = (bf16[1200,128]{1,0:T(8,128)(2,1)S(1)}, bf16[1200,128]{1,0:T(8,128)(2,1)S(1)}, u32[]{:S(2)}, u32[]{:S(2)}) collective-permute-start(bf16[1200,128]{1,0:T(8,128)(2,1)S(1)} %get-tuple-element.55), channel_id=1, source_target_pairs={{0,2},{1,31},{2,4},{3,1},{4,6},{5,3},{6,8},{7,5},{8,10},{9,7},{10,... | collective-permute-start | bytes 921608 | tf_op jit(solution)/shard_map/ppermute | solution.py:406
  65.3 8.8 %collective-permute-start.8 = (bf16[1200,128]{1,0:T(8,128)(2,1)S(1)}, bf16[1200,128]{1,0:T(8,128)(2,1)S(1)}, u32[]{:S(2)}, u32[]{:S(2)}) collective-permute-start(bf16[1200,128]{1,0:T(8,128)(2,1)S(1)} %add_convert_fusion.13.refs_1_), channel_id=1, source_target_pairs={{0,2},{1,31},{2,4},{3,1},{4,6},{5,3},{6,8},{7,5},{8,10},{9,7},{10,... | collective-permute-start | bytes 921608 | tf_op jit(solution)/shard_map/ppermute | solution.py:406
  70.4 8.8 %collective-permute-start.9 = (bf16[1200,128]{1,0:T(8,128)(2,1)S(1)}, bf16[1200,128]{1,0:T(8,128)(2,1)S(1)}, u32[]{:S(2)}, u32[]{:S(2)}) collective-permute-start(bf16[1200,128]{1,0:T(8,128)(2,1)S(1)} %add_convert_fusion.12.refs_2_), channel_id=1, source_target_pairs={{0,2},{1,31},{2,4},{3,1},{4,6},{5,3},{6,8},{7,5},{8,10},{9,7},{10,... | collective-permute-start | bytes 921608 | tf_op jit(solution)/shard_map/ppermute | solution.py:406
  74.2 8.8 %collective-permute-start.10 = (bf16[1200,128]{1,0:T(8,128)(2,1)S(1)}, bf16[1200,128]{1,0:T(8,128)(2,1)S(1)}, u32[]{:S(2)}, u32[]{:S(2)}) collective-permute-start(bf16[1200,128]{1,0:T(8,128)(2,1)S(1)} %add_convert_fusion.11.refs_3_), channel_id=1, source_target_pairs={{0,2},{1,31},{2,4},{3,1},{4,6},{5,3},{6,8},{7,5},{8,10},{9,7},{10,... | collective-permute-start | bytes 921608 | tf_op jit(solution)/shard_map/ppermute | solution.py:406
  79.3 8.8 %collective-permute-start.11 = (bf16[1200,128]{1,0:T(8,128)(2,1)S(1)}, bf16[1200,128]{1,0:T(8,128)(2,1)S(1)}, u32[]{:S(2)}, u32[]{:S(2)}) collective-permute-start(bf16[1200,128]{1,0:T(8,128)(2,1)S(1)} %add_convert_fusion.10.refs_4_), channel_id=1, source_target_pairs={{0,2},{1,31},{2,4},{3,1},{4,6},{5,3},{6,8},{7,5},{8,10},{9,7},{10,... | collective-permute-start | bytes 921608 | tf_op jit(solution)/shard_map/ppermute | solution.py:406
  83.1 8.8 %collective-permute-start.12 = (bf16[1200,128]{1,0:T(8,128)(2,1)S(1)}, bf16[1200,128]{1,0:T(8,128)(2,1)S(1)}, u32[]{:S(2)}, u32[]{:S(2)}) collective-permute-start(bf16[1200,128]{1,0:T(8,128)(2,1)S(1)} %add_convert_fusion.9.refs_5_), channel_id=1, source_target_pairs={{0,2},{1,31},{2,4},{3,1},{4,6},{5,3},{6,8},{7,5},{8,10},{9,7},{10,... | collective-permute-start | bytes 921608 | tf_op jit(solution)/shard_map/ppermute | solution.py:406
  88.2 8.8 %collective-permute-start.13 = (bf16[1200,128]{1,0:T(8,128)(2,1)S(1)}, bf16[1200,128]{1,0:T(8,128)(2,1)S(1)}, u32[]{:S(2)}, u32[]{:S(2)}) collective-permute-start(bf16[1200,128]{1,0:T(8,128)(2,1)S(1)} %add_convert_fusion.8.refs_6_), channel_id=1, source_target_pairs={{0,2},{1,31},{2,4},{3,1},{4,6},{5,3},{6,8},{7,5},{8,10},{9,7},{10,... | collective-permute-start | bytes 921608 | tf_op jit(solution)/shard_map/ppermute | solution.py:406
  92.0 8.8 %collective-permute-start.14 = (bf16[1200,128]{1,0:T(8,128)(2,1)S(1)}, bf16[1200,128]{1,0:T(8,128)(2,1)S(1)}, u32[]{:S(2)}, u32[]{:S(2)}) collective-permute-start(bf16[1200,128]{1,0:T(8,128)(2,1)S(1)} %add_convert_fusion.7.refs_7_), channel_id=1, source_target_pairs={{0,2},{1,31},{2,4},{3,1},{4,6},{5,3},{6,8},{7,5},{8,10},{9,7},{10,... | collective-permute-start | bytes 921608 | tf_op jit(solution)/shard_map/ppermute | solution.py:406
  97.1 8.8 %collective-permute-start.15 = (bf16[1200,128]{1,0:T(8,128)(2,1)S(1)}, bf16[1200,128]{1,0:T(8,128)(2,1)S(1)}, u32[]{:S(2)}, u32[]{:S(2)}) collective-permute-start(bf16[1200,128]{1,0:T(8,128)(2,1)S(1)} %add_convert_fusion.6.refs_8_), channel_id=1, source_target_pairs={{0,2},{1,31},{2,4},{3,1},{4,6},{5,3},{6,8},{7,5},{8,10},{9,7},{10,... | collective-permute-start | bytes 921608 | tf_op jit(solution)/shard_map/ppermute | solution.py:406
  100.9 8.8 %collective-permute-start.16 = (bf16[1200,128]{1,0:T(8,128)(2,1)S(1)}, bf16[1200,128]{1,0:T(8,128)(2,1)S(1)}, u32[]{:S(2)}, u32[]{:S(2)}) collective-permute-start(bf16[1200,128]{1,0:T(8,128)(2,1)S(1)} %add_convert_fusion.5.refs_9_), channel_id=1, source_target_pairs={{0,2},{1,31},{2,4},{3,1},{4,6},{5,3},{6,8},{7,5},{8,10},{9,7},{10,... | collective-permute-start | bytes 921608 | tf_op jit(solution)/shard_map/ppermute | solution.py:406
  106.0 8.8 %collective-permute-start.17 = (bf16[1200,128]{1,0:T(8,128)(2,1)S(1)}, bf16[1200,128]{1,0:T(8,128)(2,1)S(1)}, u32[]{:S(2)}, u32[]{:S(2)}) collective-permute-start(bf16[1200,128]{1,0:T(8,128)(2,1)S(1)} %add_convert_fusion.4.refs_10_), channel_id=1, source_target_pairs={{0,2},{1,31},{2,4},{3,1},{4,6},{5,3},{6,8},{7,5},{8,10},{9,7},{10,... | collective-permute-start | bytes 921608 | tf_op jit(solution)/shard_map/ppermute | solution.py:406
  109.8 10.8 %collective-permute-start.19 = (bf16[1200,128]{1,0:T(8,128)(2,1)S(1)}, bf16[1200,128]{1,0:T(8,128)(2,1)S(1)}, u32[]{:S(2)}, u32[]{:S(2)}) collective-permute-start(bf16[1200,128]{1,0:T(8,128)(2,1)S(1)} %add_convert_fusion.3.refs_11_), channel_id=1, source_target_pairs={{0,2},{1,31},{2,4},{3,1},{4,6},{5,3},{6,8},{7,5},{8,10},{9,7},{10,... | collective-permute-start | bytes 921608 | tf_op jit(solution)/shard_map/ppermute | solution.py:406
  114.9 15.1 %collective-permute-start.18 = (bf16[1200,128]{1,0:T(8,128)(2,1)S(1)}, bf16[1200,128]{1,0:T(8,128)(2,1)S(1)}, u32[]{:S(2)}, u32[]{:S(2)}) collective-permute-start(bf16[1200,128]{1,0:T(8,128)(2,1)S(1)} %add_convert_fusion.2.refs_12_), channel_id=1, source_target_pairs={{0,2},{1,31},{2,4},{3,1},{4,6},{5,3},{6,8},{7,5},{8,10},{9,7},{10,... | collective-permute-start | bytes 921608 | tf_op jit(solution)/shard_map/ppermute | solution.py:406
  120.4 13.2 %copy-start.2 = (bf16[8,128,128]{2,1,0:T(8,128)(2,1)S(1)}, bf16[8,128,128]{2,1,0:T(8,128)(2,1)}, u32[]{:S(2)}) copy-start(bf16[8,128,128]{2,1,0:T(8,128)(2,1)} %state.1) | copy-start | bytes 786436
  120.4 13.2 %copy-start.6 = (bf16[128,128]{1,0:T(8,128)(2,1)S(1)}, bf16[128,128]{1,0:T(8,128)(2,1)}, u32[]{:S(2)}) copy-start(bf16[128,128]{1,0:T(8,128)(2,1)} %param.20) | copy-start | bytes 98308
  120.7 15.4 %collective-permute-start.20 = (bf16[1200,128]{1,0:T(8,128)(2,1)S(1)}, bf16[1200,128]{1,0:T(8,128)(2,1)S(1)}, u32[]{:S(2)}, u32[]{:S(2)}) collective-permute-start(bf16[1200,128]{1,0:T(8,128)(2,1)S(1)} %add_convert_fusion.refs_0_), channel_id=1, source_target_pairs={{0,1},{1,0},{2,3},{3,2},{4,5},{5,4},{6,7},{7,6},{8,9},{9,8},{10,11... | collective-permute-start | bytes 921608 | tf_op jit(solution)/shard_map/ppermute | solution.py:432
  130.0 6.1 %copy-start.4 = (bf16[128,128]{1,0:T(8,128)(2,1)S(1)}, bf16[128,128]{1,0:T(8,128)(2,1)}, u32[]{:S(2)}) copy-start(bf16[128,128]{1,0:T(8,128)(2,1)} %coupling.1) | copy-start | bytes 98308
  130.4 4.1 %collective-permute-start.21 = (bf16[384,128]{1,0:T(8,128)(2,1)S(1)}, bf16[384,128]{1,0:T(8,128)(2,1)S(1)}, u32[]{:S(2)}, u32[]{:S(2)}) collective-permute-start(bf16[384,128]{1,0:T(8,128)(2,1)S(1)} %get-tuple-element.72), channel_id=1, source_target_pairs={{0,1},{1,0},{2,3},{3,2},{4,5},{5,4},{6,7},{7,6},{8,9},{9,8},{10,11... | collective-permute-start | bytes 294920 | tf_op jit(solution)/shard_map/ppermute | solution.py:433
